TPU v7x, 768 devices: a whole 4x8x12 slice. The times are simulated.
768 devices in a mesh: slab: 16 (over y, core), dom: 48 (over x, z).
Axes of the slice: x: 4, y: 8, z: 12, core: 2. Of those that a mesh axis runs over, the one named last changes fastest.
Arguments:
- resident_now: bfloat16 [6144, 4096], P(('slab', 'dom')), may hold values from -6 to 6
- resident_old: bfloat16 [6144, 4096], P(('slab', 'dom')), may hold values from -6 to 6
- source_now: bfloat16 [73728, 4096], P(('slab', 'dom')), may hold values from -6 to 6
- source_old: bfloat16 [73728, 4096], P(('slab', 'dom')), may hold values from -6 to 6
- destination: int32 [73728], P(('slab', 'dom')), may hold values from -1 to 2303, as said below
- anchor: int32 [36864], P(('slab', 'dom')), may hold values from 0 to 47, as said below
- floor_height: int32 [43008, 256], P(('slab', 'dom')), may hold values from 0 to 7
- admit_class: int32 [43008], P(('slab', 'dom')), may hold values from 0 to 7
- admittance: float32 [8], replicated, may hold values from 0.05 to 1
- neighbours: int32 [6, 43008], P(None, ('slab', 'dom')), may hold values from -1 to 43007, as said below
Outputs:
- pressure: float32 [43008, 4096], P(('slab', 'dom'))
Inputs may be any that keep to these rules, and one draw needn't show every extreme that they name: `destination`: each entry is -1 or o * 48 + j: the slot's brick becomes arriving brick j of dom index o in the same slab. Every arriving brick of every device comes from exactly one slot. The slots of one device send either none or exactly 2 bricks to each dom index. anchor agrees with destination: the named device of the same slab holds the slot whose destination is that arriving brick. Entry [f, b] is the global index of the brick across face f of brick b (faces -x, +x, -y, +y, -z, +z), or -1. If a meets c across face f, c meets a across the opposite face. -x and +x neighbours lie in the slab below and above (-1 at the first and last slab); -y and +y neighbours on another device of the same slab; -z and +z neighbours on the same device, and one of the two z faces of every brick is -1. For each face and each pair of devices at most 2 bricks of the first meet bricks of the second, and some pair reaches it.
All inputs are finite; a program needn't handle non-finite values.
Results may differ from a plain program's by a relative error of at most 0.0003.
Values may be sent and summed in bfloat16 or wider, within the bound.
No kernel may reach another device: no remote copies, remote signals or barrier semaphores. Data moves between devices by JAX's collectives and lax.ppermute only.
A program may use at most 64 MiB of HBM per device.

v0:
```python
import functools

import jax
import jax.numpy as jnp
from jax import lax
from jax.experimental import pallas as pl
from jax.experimental.pallas import tpu as pltpu
from jax.sharding import PartitionSpec as P

EDGE = 16
CAP = 2
ITERS = 4
FACE = EDGE * EDGE
CELLS = EDGE * FACE
LANES = 128
SUB = 8
DIRS = 4
ROWS = DIRS * CAP

courant_sq = 0.3
courant = 0.3**0.5

OCTAVE = 1024.0
LOWEST = 23.5

VMEM = pltpu.CompilerParams(vmem_limit_bytes=44 * 1024 * 1024)


def rank_within(groups, orderings, usable):
    earlier = (
        (groups[:, None] == groups[None, :])
        & (orderings[None, :] < orderings[:, None])
        & usable[None, :]
    )
    return jnp.sum(earlier.astype(jnp.int32), axis=1)


def encode(values):
    size = jnp.abs(values)
    level = jnp.floor((jnp.log2(jnp.maximum(size, 1e-30)) + LOWEST) * OCTAVE + 0.5)
    level = jnp.clip(level, 0.0, 32767.0)
    return jnp.where(values < 0.0, -level, level).astype(jnp.int32).astype(jnp.int16)


def decode(codes):
    level = codes.astype(jnp.int32).astype(jnp.float32)
    size = jnp.exp2(jnp.abs(level) * (1.0 / OCTAVE) - LOWEST)
    return jnp.where(level > 0.0, size, jnp.where(level < 0.0, -size, 0.0))


def halves(values):
    high = values.astype(jnp.bfloat16)
    low = (values - high.astype(jnp.float32)).astype(jnp.bfloat16)
    return high, low


def picked(matrix, values):
    high, low = halves(values)
    return jnp.dot(matrix, high, preferred_element_type=jnp.float32) + jnp.dot(
        matrix, low, preferred_element_type=jnp.float32
    )


def turn(block, shift, axis=1):
    size = block.shape[axis]
    shift = shift % size
    return pltpu.roll(block, shift, axis) if shift else block


class Grid:
    def __init__(self, joined):
        lane = lax.broadcasted_iota(jnp.int32, (SUB, LANES), 1)
        row = lax.broadcasted_iota(jnp.int32, (SUB, LANES), 0)
        self.first_y = lane < EDGE
        self.last_y = lane >= LANES - EDGE
        self.bottom = lane % EDGE == 0
        self.top = lane % EDGE == EDGE - 1
        self.odd = row % 2 == 1
        self.strip = lane // EDGE
        upper = jnp.where(self.odd, 1.0, 0.0)
        self.joined_down = joined * upper
        self.joined_up = joined * (1.0 - upper)

    def along_z(self, block):
        partner = jnp.where(self.odd, turn(block, 1, 0), turn(block, -1, 0))
        below = jnp.where(
            self.bottom, turn(partner, 1 - EDGE) * self.joined_down, turn(block, 1)
        )
        above = jnp.where(self.top, turn(partner, EDGE - 1) * self.joined_up, turn(block, -1))
        return below + above

    def total(self, plane, x, ghost_x, ghost_y):
        first, second = plane(x)
        before = plane(x - 1) if x else ghost_x(0)
        after = plane(x + 1) if x < EDGE - 1 else ghost_x(1)
        up_first, up_second = turn(first, EDGE), turn(second, EDGE)
        down_first, down_second = turn(first, -EDGE), turn(second, -EDGE)
        low, high = ghost_y(x)
        total_first = (
            (before[0] + after[0])
            + (jnp.where(self.first_y, low, up_first) + jnp.where(self.last_y, down_second, down_first))
            + self.along_z(first)
        )
        total_second = (
            (before[1] + after[1])
            + (jnp.where(self.first_y, up_first, up_second) + jnp.where(self.last_y, high, down_second))
            + self.along_z(second)
        )
        return total_first, total_second


def pieces(ref, rows, x):
    at = x * FACE
    return ref[rows, at : at + LANES], ref[rows, at + LANES : at + FACE]


class Faces:
    def __init__(self, ref, owned, grid):
        self.ref, self.owned, self.grid = ref, owned, grid
        self.low = [None, None]
        self.high = [None, None]

    def add(self, x, first, second, group):
        if x in (0, EDGE - 1):
            at = pl.ds(pl.multiple_of((self.owned if x else 0) + group * SUB, SUB), SUB)
            self.ref[at, :LANES] = first
            self.ref[at, LANES:] = second
        half, place = x // SUB, x % SUB
        here = self.grid.strip == place
        low = turn(first, EDGE * place)
        high = turn(second, EDGE * (place + 1))
        self.low[half] = low if place == 0 else jnp.where(here, low, self.low[half])
        self.high[half] = high if place == 0 else jnp.where(here, high, self.high[half])

    def finish(self, group):
        for order, parts in ((2, self.low), (3, self.high)):
            at = pl.ds(pl.multiple_of(order * self.owned + group * SUB, SUB), SUB)
            self.ref[at, :LANES] = parts[0]
            self.ref[at, LANES:] = parts[1]


def as_message(rows):
    number = rows.shape[0] // ROWS
    return jnp.concatenate(
        [rows[:, :LANES].reshape(number, ROWS, LANES), rows[:, LANES:].reshape(number, ROWS, LANES)],
        axis=1,
    )


def from_message(message):
    number = message.shape[0]
    return jnp.concatenate(
        [
            message[:, :ROWS].reshape(number * ROWS, LANES),
            message[:, ROWS:].reshape(number * ROWS, LANES),
        ],
        axis=1,
    )


def pack_kernel(incoming, members, dest_ref, now_ref, old_ref, out_ref):
    slots = dest_ref.shape[1]
    dest = dest_ref[...]
    src = lax.broadcasted_iota(jnp.int32, (slots, slots), 1)
    other = lax.broadcasted_iota(jnp.int32, (slots, slots), 0)
    across = jnp.broadcast_to(dest, (slots, slots))
    down = jnp.sum(jnp.where(src == other, across, 0), axis=1, keepdims=True)
    receiver = jnp.zeros((1, slots), jnp.int32)
    base = jnp.zeros((1, slots), jnp.int32)
    for member in range(1, members):
        reached = dest >= member * incoming
        receiver = receiver + reached.astype(jnp.int32)
    base = receiver * incoming
    earlier = (down >= base) & (down < dest)
    place = jnp.sum(earlier.astype(jnp.int32), axis=0, keepdims=True)
    spot = jnp.where(dest >= 0, receiver * CAP + place, -1)
    chosen = jnp.where(other == spot, 1.0, 0.0).astype(jnp.bfloat16)
    cells = now_ref.shape[1]
    for index, ref in ((0, now_ref), (1, old_ref)):
        rows = jnp.dot(chosen, ref[...], preferred_element_type=jnp.float32)
        out_ref[:, :, index * cells : (index + 1) * cells] = rows.astype(jnp.bfloat16).reshape(
            members, CAP, cells
        )


def prepare_kernel(height_ref, present_ref, rate_ref, mask_ref, keep_ref, gain_ref, lag_ref):
    owned = height_ref.shape[0]
    row = lax.broadcasted_iota(jnp.int32, (FACE, FACE), 0)
    column = lax.broadcasted_iota(jnp.int32, (FACE, FACE), 1)
    level = (lax.broadcasted_iota(jnp.int32, (owned, FACE), 1) % EDGE).astype(jnp.float32)
    heights = height_ref[...].astype(jnp.bfloat16)
    for x in range(EDGE):
        spread = jnp.where(row == column // EDGE + x * EDGE, 1.0, 0.0).astype(jnp.bfloat16)
        floor = jnp.dot(heights, spread, preferred_element_type=jnp.float32)
        mask_ref[:, x * FACE : (x + 1) * FACE] = jnp.where(level >= floor, 1.0, 0.0)

    def group_step(group, carry):
        rows = pl.ds(pl.multiple_of(group * SUB, SUB), SUB)
        present = present_ref[rows, :]
        near = [jnp.broadcast_to(present[:, d : d + 1], (SUB, LANES)) for d in range(6)]
        rate = jnp.broadcast_to(rate_ref[rows, :1], (SUB, LANES))
        grid = Grid(near[4] + near[5])
        for x in range(EDGE):
            count = grid.total(
                lambda at: pieces(mask_ref, rows, at),
                x,
                lambda d: (near[d], near[d]),
                lambda at: (near[2], near[3]),
            )
            air = pieces(mask_ref, rows, x)
            for half in range(2):
                damping = courant * (6.0 - count[half]) * rate / 2.0
                share = air[half] / (1.0 + damping)
                at = slice(x * FACE + half * LANES, x * FACE + (half + 1) * LANES)
                keep_ref[rows, at] = (2.0 - count[half] * courant_sq) * share
                gain_ref[rows, at] = courant_sq * share
                lag_ref[rows, at] = (1.0 - damping) * share
        return carry

    lax.fori_loop(0, owned // SUB, group_step, 0)


def begin_kernel(
    got_ref, now_ref, old_ref, chosen_ref, kept_ref, mask_ref, send_ref, p_ref, q_ref, out_ref, face_ref
):
    members, _, width = got_ref.shape
    owned, cells = p_ref.shape
    chosen = chosen_ref[...]
    kept = kept_ref[...]
    for index, (own_ref, to_ref) in enumerate(((now_ref, p_ref), (old_ref, q_ref))):
        arrived = got_ref[:, :, index * cells : (index + 1) * cells].reshape(members * CAP, cells)
        rows = jnp.dot(chosen, arrived, preferred_element_type=jnp.float32)
        rows = rows + jnp.dot(kept, own_ref[...], preferred_element_type=jnp.float32)
        to_ref[...] = mask_ref[...] * rows

    def group_step(group, carry):
        rows = pl.ds(pl.multiple_of(group * SUB, SUB), SUB)
        faces = Faces(face_ref, owned, Grid(jnp.ones((SUB, LANES), jnp.float32)))
        for x in range(EDGE):
            faces.add(x, *pieces(p_ref, rows, x), group)
        faces.finish(group)
        return carry

    lax.fori_loop(0, owned // SUB, group_step, 0)
    sent = jnp.dot(
        send_ref[...], face_ref[...].astype(jnp.bfloat16), preferred_element_type=jnp.float32
    )
    out_ref[...] = as_message(sent).astype(jnp.bfloat16)


def step_kernel(
    coded,
    last,
    here_ref,
    low_ref,
    high_ref,
    take_ref,
    send_ref,
    joined_ref,
    p_ref,
    q_ref,
    keep_ref,
    gain_ref,
    lag_ref,
    new_ref,
    out_ref,
    ghost_ref,
    face_ref,
):
    owned = p_ref.shape[0]
    for ref, low_row, number in ((low_ref, 0, 1), (high_ref, 1, 1), (here_ref, 2, 2)):
        at = slice(low_row * owned, (low_row + number) * owned)
        matrix = take_ref[at, :]
        if coded:
            ghost_ref[at, :] = picked(matrix, from_message(decode(ref[...])))
        else:
            received = from_message(ref[...].astype(jnp.float32)).astype(jnp.bfloat16)
            ghost_ref[at, :] = jnp.dot(matrix, received, preferred_element_type=jnp.float32)
    target_ref = face_ref if last else new_ref

    def group_step(group, carry):
        rows = pl.ds(pl.multiple_of(group * SUB, SUB), SUB)
        grid = Grid(jnp.broadcast_to(joined_ref[rows, :1], (SUB, LANES)))
        ghosts = []
        for d in range(DIRS):
            at = pl.ds(pl.multiple_of(d * owned + group * SUB, SUB), SUB)
            ghosts.append((ghost_ref[at, :LANES], ghost_ref[at, LANES:]))

        def ghost_y(x):
            half, place = x // SUB, x % SUB
            low = turn(ghosts[2][half], -EDGE * place)
            high = turn(ghosts[3][half], -EDGE * (place + 1))
            return low, high

        faces = None if last else Faces(face_ref, owned, grid)
        for x in range(EDGE):
            total = grid.total(
                lambda at: pieces(p_ref, rows, at), x, lambda d: ghosts[d], ghost_y
            )
            state = pieces(p_ref, rows, x)
            lagging = pieces(q_ref, rows, x)
            keep = pieces(keep_ref, rows, x)
            gain = pieces(gain_ref, rows, x)
            lag = pieces(lag_ref, rows, x)
            updated = [
                keep[h] * state[h] + gain[h] * total[h] - lag[h] * lagging[h] for h in range(2)
            ]
            for h in range(2):
                target_ref[rows, x * FACE + h * LANES : x * FACE + (h + 1) * LANES] = updated[h]
            if faces is not None:
                faces.add(x, updated[0], updated[1], group)
        if faces is not None:
            faces.finish(group)
        return carry

    lax.fori_loop(0, owned // SUB, group_step, 0)
    if last:
        new_ref[...] = picked(send_ref[...], face_ref[...])
    else:
        out_ref[...] = encode(as_message(picked(send_ref[...], face_ref[...])))


def last_kernel(*refs):
    ins, (new_ref, ghost_ref, state_ref) = refs[:-3], refs[-3:]
    step_kernel(True, True, *ins, new_ref, None, ghost_ref, state_ref)


def on_device(
    resident_now,
    resident_old,
    source_now,
    source_old,
    destination,
    anchor,
    floor_height,
    admit_class,
    admittance,
    neighbours,
):
    members = lax.axis_size("dom")
    slabs = lax.axis_size("slab")
    owned = floor_height.shape[0]
    incoming = anchor.shape[0]
    cells = source_now.shape[1]
    kept = owned - incoming
    f32, bf16, i32 = jnp.float32, jnp.bfloat16, jnp.int32

    outgoing = pl.pallas_call(
        functools.partial(pack_kernel, incoming, members),
        out_shape=jax.ShapeDtypeStruct((members, CAP, 2 * cells), bf16),
        compiler_params=VMEM,
    )(destination[None, :], source_now, source_old)
    got = lax.all_to_all(outgoing, "dom", split_axis=0, concat_axis=0, tiled=True)

    present = neighbours >= 0
    peer_dev = neighbours // owned % members
    peer_slot = neighbours % owned
    slot_ids = jnp.arange(owned, dtype=i32)
    lower = present[5]
    upper = present[4]
    lower_rank = jnp.sum((lower[None, :] & (slot_ids[None, :] < slot_ids[:, None])).astype(i32), axis=1)
    partner_rank = jnp.sum(
        (lower[None, :] & (slot_ids[None, :] < peer_slot[4][:, None])).astype(i32), axis=1
    )
    alone = ~(lower | upper)
    alone_rank = jnp.sum((alone[None, :] & (slot_ids[None, :] < slot_ids[:, None])).astype(i32), axis=1)
    pairs = jnp.sum(lower.astype(i32))
    position = jnp.where(
        lower, 2 * lower_rank, jnp.where(upper, 2 * partner_rank + 1, 2 * pairs + alone_rank)
    )
    order_is = position[None, :] == slot_ids[:, None]
    order = jnp.sum(jnp.where(order_is, slot_ids[None, :], 0), axis=1)
    back = (position[:, None] == slot_ids[None, :]).astype(bf16)

    seat = rank_within(anchor, jnp.arange(incoming, dtype=i32), anchor >= 0)
    inbox = jnp.concatenate([jnp.full((kept,), -1, i32), anchor * CAP + seat])
    class_ids = jnp.arange(admittance.shape[0], dtype=i32)
    send_at = []
    take_at = []
    for d in range(DIRS):
        order_out = rank_within(peer_dev[d], peer_slot[d], present[d])
        order_in = rank_within(peer_dev[d], slot_ids, present[d])
        send_at.append(jnp.where(present[d], peer_dev[d] * ROWS + d * CAP + order_out, -1))
        take_at.append(jnp.where(present[d], peer_dev[d] * ROWS + (d ^ 1) * CAP + order_in, -1))
    table = jnp.stack(
        send_at + take_at + [inbox, admit_class] + [present[d].astype(i32) for d in range(6)]
    )
    table = jnp.sum(jnp.where(order_is[None], table[:, None, :], 0), axis=2)
    message_rows = jnp.arange(members * ROWS, dtype=i32)
    send = (table[:DIRS].reshape(1, -1) == message_rows[:, None]).astype(bf16)
    take = (table[DIRS : 2 * DIRS].reshape(-1, 1) == message_rows[None, :]).astype(bf16)
    chosen = (table[8][:, None] == jnp.arange(members * CAP, dtype=i32)[None, :]).astype(bf16)
    stay = (order[:, None] == jnp.arange(kept, dtype=i32)[None, :]).astype(bf16)
    rates = jnp.sum(
        jnp.where(table[9][:, None] == class_ids[None, :], admittance[None, :], 0.0), axis=1
    )[:, None]
    near = table[10:].T.astype(f32)
    joined = near[:, 4:5] + near[:, 5:6]
    heights = floor_height[order].astype(f32)

    grid_shape = jax.ShapeDtypeStruct((owned, cells), f32)
    mask, keep, gain, lag = pl.pallas_call(
        prepare_kernel,
        out_shape=[grid_shape] * 4,
        compiler_params=VMEM,
    )(heights, near, rates)

    message = (members, 2 * ROWS, LANES)
    state, lagging, outbox = pl.pallas_call(
        begin_kernel,
        out_shape=[grid_shape, grid_shape, jax.ShapeDtypeStruct(message, bf16)],
        scratch_shapes=[pltpu.VMEM((DIRS * owned, FACE), f32)],
        compiler_params=VMEM,
    )(got, resident_now, resident_old, chosen, stay, mask, send)

    ends = slabs - 1
    for sweep in range(ITERS):
        here = lax.all_to_all(outbox, "dom", split_axis=0, concat_axis=0, tiled=True)
        from_low = lax.ppermute(here, "slab", [(i, i + 1) for i in range(ends)])
        from_high = lax.ppermute(here, "slab", [(i + 1, i) for i in range(ends)])
        common = (here, from_low, from_high, take)
        fields = (joined, state, lagging, keep, gain, lag)
        ghost_scratch = pltpu.VMEM((DIRS * owned, FACE), f32)
        if sweep < ITERS - 1:
            updated, outbox = pl.pallas_call(
                functools.partial(step_kernel, sweep > 0, False),
                out_shape=[grid_shape, jax.ShapeDtypeStruct(message, jnp.int16)],
                scratch_shapes=[ghost_scratch, pltpu.VMEM((DIRS * owned, FACE), f32)],
                compiler_params=VMEM,
            )(*common, send, *fields)
        else:
            updated = pl.pallas_call(
                last_kernel,
                out_shape=grid_shape,
                scratch_shapes=[ghost_scratch, pltpu.VMEM((owned, cells), f32)],
                compiler_params=VMEM,
            )(*common, back, *fields)
        lagging, state = state, updated
    return state


def solution(mesh):
    split = P(("slab", "dom"), None)
    line = P(("slab", "dom"))
    return jax.shard_map(
        on_device,
        mesh=mesh,
        in_specs=(split, split, split, split, line, line, split, line, P(), P(None, ("slab", "dom"))),
        out_specs=split,
        check_vma=False,
    )
```

profile of v0, /device:TPU:1, one launch (start us, length us, event | category | flops | bytes accessed | tf_op | source)
XLA Modules:
  0.0 245.9 jit_solution(1894036596529554369)
XLA Ops:
  4.8 19.2 %all-to-all-start = ((bf16[48,2,8192]{2,1,0:T(2,128)(2,1)}), bf16[48,2,8192]{2,1,0:T(2,128)(2,1)}, u32[]{:S(2)}, u32[]{:S(2)}) async-start(bf16[48,2,8192]{2,1,0:T(2,128)(2,1)} %shard_map.100), calls=%async_computation | async-start | bytes 3145728 | tf_op jit(solution)/shard_map/all_to_all | solution.py:353
  28.4 2.6 %shard_map.101 = (f32[56,4096]{1,0:T(8,128)S(1)}, f32[56,4096]{1,0:T(8,128)S(1)}, f32[56,4096]{1,0:T(8,128)S(1)}, f32[56,4096]{1,0:T(8,128)S(1)}) custom-call(f32[56,256]{1,0:T(8,128)S(1)} %convert_element_type.107.height_ref, f32[56,6]{1,0:T(8,128)S(1)} %bitcast.94, f32[56,1]{1,0:T(8,128)S(1)} %copy.16.rate_ref), custom_call_target="tpu_custom_call" | custom-call | tf_op jit(solution)/shard_map/pallas_call | solution.py:402
  32.1 44.5 %all-to-all-done.got_ref = bf16[48,2,8192]{2,1,0:T(2,128)(2,1)} async-done(((bf16[48,2,8192]{2,1,0:T(2,128)(2,1)}), bf16[48,2,8192]{2,1,0:T(2,128)(2,1)}, u32[]{:S(2)}, u32[]{:S(2)}) %all-to-all-start) | async-done | bytes 1572896 | tf_op jit(solution)/shard_map/all_to_all | solution.py:353
  77.7 3.0 %shard_map.102 = (f32[56,4096]{1,0:T(8,128)S(1)}, f32[56,4096]{1,0:T(8,128)S(1)}, bf16[48,16,128]{2,1,0:T(8,128)(2,1)S(1)}) custom-call(bf16[48,2,8192]{2,1,0:T(2,128)(2,1)} %all-to-all-done.got_ref, bf16[8,4096]{1,0:T(8,128)(2,1)S(1)} %copy-done.14, bf16[8,4096]{1,0:T(8,128)(2,1)S(1)} %copy-done.15, bf16[56,96]{1,0:T(8,128)(2,1)S(1)} %fusion.9.chosen_ref, ...), custom_call_target="tpu_custom_call" | custom-call | tf_op jit(solution)/shard_map/pallas_call | solution.py:409
  83.3 12.1 %all-to-all-start.1 = ((bf16[48,16,128]{2,1,0:T(8,128)(2,1)}), bf16[48,16,128]{2,1,0:T(8,128)(2,1)S(1)}, u32[]{:S(2)}, u32[]{:S(2)}) async-start(bf16[48,16,128]{2,1,0:T(8,128)(2,1)} %copy-done.13), calls=%async_computation.1 | async-start | bytes 393216 | tf_op jit(solution)/shard_map/all_to_all | solution.py:418
  95.5 13.3 %all-to-all-done.1.here_ref = bf16[48,16,128]{2,1,0:T(8,128)(2,1)S(1)} async-done(((bf16[48,16,128]{2,1,0:T(8,128)(2,1)}), bf16[48,16,128]{2,1,0:T(8,128)(2,1)S(1)}, u32[]{:S(2)}, u32[]{:S(2)}) %all-to-all-start.1) | async-done | bytes 196640 | tf_op jit(solution)/shard_map/all_to_all | solution.py:418
  108.9 6.2 %collective-permute-start = (bf16[48,16,128]{2,1,0:T(8,128)(2,1)S(1)}, bf16[48,16,128]{2,1,0:T(8,128)(2,1)S(1)}, u32[]{:S(2)}, u32[]{:S(2)}) collective-permute-start(bf16[48,16,128]{2,1,0:T(8,128)(2,1)S(1)} %all-to-all-done.1.here_ref), channel_id=1, source_target_pairs={{0,48},{48,96},{96,144},{144,192},{192,240},{240,288},{288,336},{3... | collective-permute-start | bytes 589832 | tf_op jit(solution)/shard_map/ppermute | solution.py:419
  117.6 4.4 %collective-permute-done.1.high_ref = bf16[48,16,128]{2,1,0:T(8,128)(2,1)S(1)} collective-permute-done((bf16[48,16,128]{2,1,0:T(8,128)(2,1)S(1)}, bf16[48,16,128]{2,1,0:T(8,128)(2,1)S(1)}, u32[]{:S(2)}, u32[]{:S(2)}) %collective-permute-start.1) | collective-permute-done | bytes 196640 | tf_op jit(solution)/shard_map/ppermute | solution.py:420
  124.4 7.3 %shard_map.103 = (f32[56,4096]{1,0:T(8,128)S(1)}, s16[48,16,128]{2,1,0:T(8,128)(2,1)S(1)}) custom-call(bf16[48,16,128]{2,1,0:T(8,128)(2,1)S(1)} %all-to-all-done.1.here_ref, bf16[48,16,128]{2,1,0:T(8,128)(2,1)S(1)} %collective-permute-done.low_ref, bf16[48,16,128]{2,1,0:T(8,128)(2,1)S(1)} %collective-permute-done.1.high_ref, ...), custom_call_target="tpu_custom_call" | custom-call | tf_op jit(solution)/shard_map/pallas_call | solution.py:425
  131.7 18.1 %all_to_all.25.here_ref = s16[48,16,128]{2,1,0:T(8,128)(2,1)S(1)} all-to-all(s16[48,16,128]{2,1,0:T(8,128)(2,1)S(1)} %get-tuple-element.25), channel_id=1, replica_groups=mesh['slab'=16,'dom'=48] {'dom'}, dimensions={0} | all-to-all | bytes 393216 | tf_op jit(solution)/shard_map/all_to_all | solution.py:418
  149.7 4.2 %collective-permute-start.2 = (s16[48,16,128]{2,1,0:T(8,128)(2,1)S(1)}, s16[48,16,128]{2,1,0:T(8,128)(2,1)S(1)}, u32[]{:S(2)}, u32[]{:S(2)}) collective-permute-start(s16[48,16,128]{2,1,0:T(8,128)(2,1)S(1)} %all_to_all.25.here_ref), channel_id=1, source_target_pairs={{0,48},{48,96},{96,144},{144,192},{192,240},{240,288},{288,336},{3... | collective-permute-start | bytes 589832 | tf_op jit(solution)/shard_map/ppermute | solution.py:419
  154.0 1.9 collective-permute-start.3
  156.6 4.4 %collective-permute-done.3.high_ref = s16[48,16,128]{2,1,0:T(8,128)(2,1)S(1)} collective-permute-done((s16[48,16,128]{2,1,0:T(8,128)(2,1)S(1)}, s16[48,16,128]{2,1,0:T(8,128)(2,1)S(1)}, u32[]{:S(2)}, u32[]{:S(2)}) %collective-permute-start.3) | collective-permute-done | bytes 196640 | tf_op jit(solution)/shard_map/ppermute | solution.py:420
  161.0 7.8 %shard_map.104 = (f32[56,4096]{1,0:T(8,128)S(1)}, s16[48,16,128]{2,1,0:T(8,128)(2,1)S(1)}) custom-call(s16[48,16,128]{2,1,0:T(8,128)(2,1)S(1)} %all_to_all.25.here_ref, s16[48,16,128]{2,1,0:T(8,128)(2,1)S(1)} %collective-permute-done.2.low_ref, s16[48,16,128]{2,1,0:T(8,128)(2,1)S(1)} %collective-permute-done.3.high_ref, ...), custom_call_target="tpu_custom_call" | custom-call | tf_op jit(solution)/shard_map/pallas_call | solution.py:425
  168.8 18.9 %all_to_all.26.here_ref = s16[48,16,128]{2,1,0:T(8,128)(2,1)S(1)} all-to-all(s16[48,16,128]{2,1,0:T(8,128)(2,1)S(1)} %get-tuple-element.27), channel_id=1, replica_groups=mesh['slab'=16,'dom'=48] {'dom'}, dimensions={0} | all-to-all | bytes 393216 | tf_op jit(solution)/shard_map/all_to_all | solution.py:418
  187.7 4.2 %collective-permute-start.4 = (s16[48,16,128]{2,1,0:T(8,128)(2,1)S(1)}, s16[48,16,128]{2,1,0:T(8,128)(2,1)S(1)}, u32[]{:S(2)}, u32[]{:S(2)}) collective-permute-start(s16[48,16,128]{2,1,0:T(8,128)(2,1)S(1)} %all_to_all.26.here_ref), channel_id=1, source_target_pairs={{0,48},{48,96},{96,144},{144,192},{192,240},{240,288},{288,336},{3... | collective-permute-start | bytes 589832 | tf_op jit(solution)/shard_map/ppermute | solution.py:419
  192.0 1.9 collective-permute-start.5
  194.6 4.4 %collective-permute-done.5.high_ref = s16[48,16,128]{2,1,0:T(8,128)(2,1)S(1)} collective-permute-done((s16[48,16,128]{2,1,0:T(8,128)(2,1)S(1)}, s16[48,16,128]{2,1,0:T(8,128)(2,1)S(1)}, u32[]{:S(2)}, u32[]{:S(2)}) %collective-permute-start.5) | collective-permute-done | bytes 196640 | tf_op jit(solution)/shard_map/ppermute | solution.py:420
  199.0 8.5 %shard_map.105 = (f32[56,4096]{1,0:T(8,128)S(1)}, s16[48,16,128]{2,1,0:T(8,128)(2,1)}) custom-call(s16[48,16,128]{2,1,0:T(8,128)(2,1)S(1)} %all_to_all.26.here_ref, s16[48,16,128]{2,1,0:T(8,128)(2,1)S(1)} %collective-permute-done.4.low_ref, s16[48,16,128]{2,1,0:T(8,128)(2,1)S(1)} %collective-permute-done.5.high_ref, ...), custom_call_target="tpu_custom_call" | custom-call | tf_op jit(solution)/shard_map/pallas_call | solution.py:425
  208.4 5.6 %all-to-all-start.4 = ((s16[48,16,128]{2,1,0:T(8,128)(2,1)}), s16[48,16,128]{2,1,0:T(8,128)(2,1)S(1)}, u32[]{:S(2)}, u32[]{:S(2)}) async-start(s16[48,16,128]{2,1,0:T(8,128)(2,1)} %get-tuple-element.29), calls=%async_computation.4 | async-start | bytes 393216 | tf_op jit(solution)/shard_map/all_to_all | solution.py:418
  214.0 13.5 %all-to-all-done.4.refs_0_ = s16[48,16,128]{2,1,0:T(8,128)(2,1)S(1)} async-done(((s16[48,16,128]{2,1,0:T(8,128)(2,1)}), s16[48,16,128]{2,1,0:T(8,128)(2,1)S(1)}, u32[]{:S(2)}, u32[]{:S(2)}) %all-to-all-start.4) | async-done | bytes 196640 | tf_op jit(solution)/shard_map/all_to_all | solution.py:418
  227.5 4.7 %collective-permute-start.6 = (s16[48,16,128]{2,1,0:T(8,128)(2,1)S(1)}, s16[48,16,128]{2,1,0:T(8,128)(2,1)S(1)}, u32[]{:S(2)}, u32[]{:S(2)}) collective-permute-start(s16[48,16,128]{2,1,0:T(8,128)(2,1)S(1)} %all-to-all-done.4.refs_0_), channel_id=1, source_target_pairs={{0,48},{48,96},{96,144},{144,192},{192,240},{240,288},{288,336},{3... | collective-permute-start | bytes 589832 | tf_op jit(solution)/shard_map/ppermute | solution.py:419
  234.8 4.4 %collective-permute-done.7.refs_2_ = s16[48,16,128]{2,1,0:T(8,128)(2,1)S(1)} collective-permute-done((s16[48,16,128]{2,1,0:T(8,128)(2,1)S(1)}, s16[48,16,128]{2,1,0:T(8,128)(2,1)S(1)}, u32[]{:S(2)}, u32[]{:S(2)}) %collective-permute-start.7) | collective-permute-done | bytes 196640 | tf_op jit(solution)/shard_map/ppermute | solution.py:420
  241.6 4.4 %shard_map.106 = f32[56,4096]{1,0:T(8,128)} custom-call(s16[48,16,128]{2,1,0:T(8,128)(2,1)S(1)} %all-to-all-done.4.refs_0_, s16[48,16,128]{2,1,0:T(8,128)(2,1)S(1)} %collective-permute-done.6.refs_1_, s16[48,16,128]{2,1,0:T(8,128)(2,1)S(1)} %collective-permute-done.7.refs_2_, bf16[224,384]{1,0:T(8,128)(2,1)S(1)} %fusion.1.take_ref.refs_3_, ...), custom_call_target="tpu_custom_call" | custom-call | tf_op jit(solution)/shard_map/pallas_call | solution.py:432
  (89 shorter events, 25.5 us)
Async XLA Ops:
  0.0 27.6 %copy-start = (s32[56,256]{1,0:T(8,128)S(1)}, s32[56,256]{1,0:T(8,128)}, u32[]{:S(2)}) copy-start(s32[56,256]{1,0:T(8,128)} %param.16) | copy-start | bytes 172036
  4.8 19.2 %copy-start.17 = (s32[6,56]{1,0:T(8,128)S(1)}, s32[6,56]{1,0:T(8,128)}, u32[]{:S(2)}) copy-start(s32[6,56]{1,0:T(8,128)} %param.19) | copy-start | bytes 4036
  4.8 19.2 %copy-start.18 = (s32[48]{0:T(128)S(1)}, s32[48]{0:T(128)}, u32[]{:S(2)}) copy-start(s32[48]{0:T(128)} %param.15) | copy-start | bytes 580
  4.8 22.0 %copy-start.19 = (s32[56]{0:T(128)S(1)}, s32[56]{0:T(128)}, u32[]{:S(2)}) copy-start(s32[56]{0:T(128)} %param.17) | copy-start | bytes 676
  4.8 22.5 %copy-start.20 = (f32[8]{0:T(128)S(1)}, f32[8]{0:T(128)}, u32[]{:S(2)}) copy-start(f32[8]{0:T(128)} %param.18) | copy-start | bytes 100
  4.8 71.7 %copy-start.14 = (bf16[8,4096]{1,0:T(8,128)(2,1)S(1)}, bf16[8,4096]{1,0:T(8,128)(2,1)}, u32[]{:S(2)}) copy-start(bf16[8,4096]{1,0:T(8,128)(2,1)} %now_ref.3) | copy-start | bytes 196612
  4.8 71.7 %copy-start.15 = (bf16[8,4096]{1,0:T(8,128)(2,1)S(1)}, bf16[8,4096]{1,0:T(8,128)(2,1)}, u32[]{:S(2)}) copy-start(bf16[8,4096]{1,0:T(8,128)(2,1)} %old_ref.3) | copy-start | bytes 196612
  4.8 71.7 %all-to-all-start = ((bf16[48,2,8192]{2,1,0:T(2,128)(2,1)}), bf16[48,2,8192]{2,1,0:T(2,128)(2,1)}, u32[]{:S(2)}, u32[]{:S(2)}) async-start(bf16[48,2,8192]{2,1,0:T(2,128)(2,1)} %shard_map.100), calls=%async_computation | async-start | bytes 3145728 | tf_op jit(solution)/shard_map/all_to_all | solution.py:353
  76.6 1.2 copy-start.8
  83.3 25.6 %all-to-all-start.1 = ((bf16[48,16,128]{2,1,0:T(8,128)(2,1)}), bf16[48,16,128]{2,1,0:T(8,128)(2,1)S(1)}, u32[]{:S(2)}, u32[]{:S(2)}) async-start(bf16[48,16,128]{2,1,0:T(8,128)(2,1)} %copy-done.13), calls=%async_computation.1 | async-start | bytes 393216 | tf_op jit(solution)/shard_map/all_to_all | solution.py:418
  108.9 8.8 %collective-permute-start = (bf16[48,16,128]{2,1,0:T(8,128)(2,1)S(1)}, bf16[48,16,128]{2,1,0:T(8,128)(2,1)S(1)}, u32[]{:S(2)}, u32[]{:S(2)}) collective-permute-start(bf16[48,16,128]{2,1,0:T(8,128)(2,1)S(1)} %all-to-all-done.1.here_ref), channel_id=1, source_target_pairs={{0,48},{48,96},{96,144},{144,192},{192,240},{240,288},{288,336},{3... | collective-permute-start | bytes 589832 | tf_op jit(solution)/shard_map/ppermute | solution.py:419
  115.0 7.0 %collective-permute-start.1 = (bf16[48,16,128]{2,1,0:T(8,128)(2,1)S(1)}, bf16[48,16,128]{2,1,0:T(8,128)(2,1)S(1)}, u32[]{:S(2)}, u32[]{:S(2)}) collective-permute-start(bf16[48,16,128]{2,1,0:T(8,128)(2,1)S(1)} %all-to-all-done.1.here_ref), channel_id=1, source_target_pairs={{48,0},{96,48},{144,96},{192,144},{240,192},{288,240},{336,288},{3... | collective-permute-start | bytes 589832 | tf_op jit(solution)/shard_map/ppermute | solution.py:420
  122.0 1.2 copy-start.2
  123.2 1.2 copy-start.6
  149.7 6.8 %collective-permute-start.2 = (s16[48,16,128]{2,1,0:T(8,128)(2,1)S(1)}, s16[48,16,128]{2,1,0:T(8,128)(2,1)S(1)}, u32[]{:S(2)}, u32[]{:S(2)}) collective-permute-start(s16[48,16,128]{2,1,0:T(8,128)(2,1)S(1)} %all_to_all.25.here_ref), channel_id=1, source_target_pairs={{0,48},{48,96},{96,144},{144,192},{192,240},{240,288},{288,336},{3... | collective-permute-start | bytes 589832 | tf_op jit(solution)/shard_map/ppermute | solution.py:419
  154.0 7.0 %collective-permute-start.3 = (s16[48,16,128]{2,1,0:T(8,128)(2,1)S(1)}, s16[48,16,128]{2,1,0:T(8,128)(2,1)S(1)}, u32[]{:S(2)}, u32[]{:S(2)}) collective-permute-start(s16[48,16,128]{2,1,0:T(8,128)(2,1)S(1)} %all_to_all.25.here_ref), channel_id=1, source_target_pairs={{48,0},{96,48},{144,96},{192,144},{240,192},{288,240},{336,288},{3... | collective-permute-start | bytes 589832 | tf_op jit(solution)/shard_map/ppermute | solution.py:420
  168.8 38.7 %copy-start.3 = (f32[56,4096]{1,0:T(8,128)}, f32[56,4096]{1,0:T(8,128)S(1)}, u32[]{:S(2)}) copy-start(f32[56,4096]{1,0:T(8,128)S(1)} %get-tuple-element.28.p_ref.refs_7_) | copy-start | bytes 2752516
  187.7 6.8 %collective-permute-start.4 = (s16[48,16,128]{2,1,0:T(8,128)(2,1)S(1)}, s16[48,16,128]{2,1,0:T(8,128)(2,1)S(1)}, u32[]{:S(2)}, u32[]{:S(2)}) collective-permute-start(s16[48,16,128]{2,1,0:T(8,128)(2,1)S(1)} %all_to_all.26.here_ref), channel_id=1, source_target_pairs={{0,48},{48,96},{96,144},{144,192},{192,240},{240,288},{288,336},{3... | collective-permute-start | bytes 589832 | tf_op jit(solution)/shard_map/ppermute | solution.py:419
  192.0 7.0 %collective-permute-start.5 = (s16[48,16,128]{2,1,0:T(8,128)(2,1)S(1)}, s16[48,16,128]{2,1,0:T(8,128)(2,1)S(1)}, u32[]{:S(2)}, u32[]{:S(2)}) collective-permute-start(s16[48,16,128]{2,1,0:T(8,128)(2,1)S(1)} %all_to_all.26.here_ref), channel_id=1, source_target_pairs={{48,0},{96,48},{144,96},{192,144},{240,192},{288,240},{336,288},{3... | collective-permute-start | bytes 589832 | tf_op jit(solution)/shard_map/ppermute | solution.py:420
  208.4 19.1 %all-to-all-start.4 = ((s16[48,16,128]{2,1,0:T(8,128)(2,1)}), s16[48,16,128]{2,1,0:T(8,128)(2,1)S(1)}, u32[]{:S(2)}, u32[]{:S(2)}) async-start(s16[48,16,128]{2,1,0:T(8,128)(2,1)} %get-tuple-element.29), calls=%async_computation.4 | async-start | bytes 393216 | tf_op jit(solution)/shard_map/all_to_all | solution.py:418
  227.5 7.3 %collective-permute-start.6 = (s16[48,16,128]{2,1,0:T(8,128)(2,1)S(1)}, s16[48,16,128]{2,1,0:T(8,128)(2,1)S(1)}, u32[]{:S(2)}, u32[]{:S(2)}) collective-permute-start(s16[48,16,128]{2,1,0:T(8,128)(2,1)S(1)} %all-to-all-done.4.refs_0_), channel_id=1, source_target_pairs={{0,48},{48,96},{96,144},{144,192},{192,240},{240,288},{288,336},{3... | collective-permute-start | bytes 589832 | tf_op jit(solution)/shard_map/ppermute | solution.py:419
  232.2 7.0 %collective-permute-start.7 = (s16[48,16,128]{2,1,0:T(8,128)(2,1)S(1)}, s16[48,16,128]{2,1,0:T(8,128)(2,1)S(1)}, u32[]{:S(2)}, u32[]{:S(2)}) collective-permute-start(s16[48,16,128]{2,1,0:T(8,128)(2,1)S(1)} %all-to-all-done.4.refs_0_), channel_id=1, source_target_pairs={{48,0},{96,48},{144,96},{192,144},{240,192},{288,240},{336,288},{3... | collective-permute-start | bytes 589832 | tf_op jit(solution)/shard_map/ppermute | solution.py:420
  239.2 1.2 copy-start.4
  240.4 1.2 copy-start.10
  (8 other events, 7.3 us)
where the time goes:
time: 249 us; the launch traced here: 246 us
  waiting for transfers between devices  91.4 us (37%)
  starting transfers between devices  63.9 us (26%)
  blocking collectives  37 us (15%)
  Pallas kernels  35.3 us (14%)
  local copies, waits for them, and re-layouts  14.4 us (6%)
  other arithmetic  2.95 us (1%)
    all_to_all x1, waiting for transfers between devices, on_device(): lax.all_to_all(outgoing, 'dom', split_axis=0, concat_axis=0, tiled=True)  44.5 us
    all_to_all x2, blocking collectives, on_device(): lax.all_to_all(outbox, 'dom', split_axis=0, concat_axis=0, tiled=True)  37 us
    all_to_all x2, waiting for transfers between devices, on_device(): lax.all_to_all(outbox, 'dom', split_axis=0, concat_axis=0, tiled=True)  26.9 us
    pallas_call x3, Pallas kernels, on_device(): pl.pallas_call(functools.partial(step_kernel, sweep > 0, False), out_shap...  23.5 us
    ppermute x4, starting transfers between devices, on_device(): from_low = lax.ppermute(here, 'slab', [(i, i + 1) for i in range(ends)])  19.4 us
    all_to_all x1, starting transfers between devices, on_device(): lax.all_to_all(outgoing, 'dom', split_axis=0, concat_axis=0, tiled=True)  19.2 us
    all_to_all x2, starting transfers between devices, on_device(): lax.all_to_all(outbox, 'dom', split_axis=0, concat_axis=0, tiled=True)  17.6 us
    ppermute x4, waiting for transfers between devices, on_device(): from_high = lax.ppermute(here, 'slab', [(i + 1, i) for i in range(ends)])  17.6 us
  transfers between devices with their start and end apart: 11, of which 11 were waited for; matrix products, arithmetic and copies ran while one was open for 2% of the time, Pallas kernels for 1%

commit v1 on v0

v1 whole, which is shorter than its diff:
```python
import functools

import jax
import jax.numpy as jnp
from jax import lax
from jax.experimental import pallas as pl
from jax.experimental.pallas import tpu as pltpu
from jax.sharding import PartitionSpec as P

EDGE = 16
CAP = 2
ITERS = 4
FACE = EDGE * EDGE
CELLS = EDGE * FACE
LANES = 128
SUB = 8
DIRS = 4
ROWS = DIRS * CAP
CHUNKS = 4

INBOX, ORDER, RATE, JOINED, NEAR = 0, 1, 2, 3, 4

courant_sq = 0.3
courant = 0.3**0.5

OCTAVE = 1024.0
LOWEST = 23.5

VMEM = pltpu.CompilerParams(vmem_limit_bytes=16 * 1024 * 1024)


def rank_within(groups, orderings, usable):
    earlier = (
        (groups[:, None] == groups[None, :])
        & (orderings[None, :] < orderings[:, None])
        & usable[None, :]
    )
    return jnp.sum(earlier.astype(jnp.int32), axis=1)


def encode(values):
    size = jnp.abs(values)
    level = jnp.floor((jnp.log2(jnp.maximum(size, 1e-30)) + LOWEST) * OCTAVE + 0.5)
    level = jnp.clip(level, 0.0, 32767.0)
    return jnp.where(values < 0.0, -level, level)


def decode(level):
    size = jnp.exp2(jnp.abs(level) * (1.0 / OCTAVE) - LOWEST)
    return jnp.where(level > 0.0, size, jnp.where(level < 0.0, -size, 0.0))


def picked(matrix, values):
    high = values.astype(jnp.bfloat16)
    low = (values - high.astype(jnp.float32)).astype(jnp.bfloat16)
    width = values.shape[1]
    if width == LANES:
        both = jnp.dot(
            matrix, jnp.concatenate([high, low], axis=1), preferred_element_type=jnp.float32
        )
        return both[:, :width] + both[:, width:]
    return jnp.dot(matrix, high, preferred_element_type=jnp.float32) + jnp.dot(
        matrix, low, preferred_element_type=jnp.float32
    )


def turn(block, shift, axis=1):
    size = block.shape[axis]
    shift = shift % size
    return pltpu.roll(block, shift, axis) if shift else block


class Grid:
    def __init__(self, joined):
        lane = lax.broadcasted_iota(jnp.int32, (SUB, LANES), 1)
        row = lax.broadcasted_iota(jnp.int32, (SUB, LANES), 0)
        self.first_y = lane < EDGE
        self.last_y = lane >= LANES - EDGE
        self.bottom = lane % EDGE == 0
        self.top = lane % EDGE == EDGE - 1
        self.odd = row % 2 == 1
        self.strip = lane // EDGE
        upper = jnp.where(self.odd, 1.0, 0.0)
        self.joined_down = joined * upper
        self.joined_up = joined * (1.0 - upper)

    def along_z(self, block):
        partner = jnp.where(self.odd, turn(block, 1, 0), turn(block, -1, 0))
        below = jnp.where(
            self.bottom, turn(partner, 1 - EDGE) * self.joined_down, turn(block, 1)
        )
        above = jnp.where(self.top, turn(partner, EDGE - 1) * self.joined_up, turn(block, -1))
        return below + above

    def total(self, plane, x, ghost_x, ghost_y):
        first, second = plane(x)
        sides = [plane(at) for at in (x - 1, x + 1) if 0 <= at < EDGE]
        if ghost_x is not None and x in (0, EDGE - 1):
            sides.append(ghost_x(x))
        along_x = [sum(side[half] for side in sides) for half in range(2)]
        up_first, up_second = turn(first, EDGE), turn(second, EDGE)
        down_first, down_second = turn(first, -EDGE), turn(second, -EDGE)
        low, high = ghost_y(x)
        total_first = (
            along_x[0]
            + (jnp.where(self.first_y, low, up_first) + jnp.where(self.last_y, down_second, down_first))
            + self.along_z(first)
        )
        total_second = (
            along_x[1]
            + (jnp.where(self.first_y, up_first, up_second) + jnp.where(self.last_y, high, down_second))
            + self.along_z(second)
        )
        return total_first, total_second


def pieces(ref, rows, x):
    at = x * FACE
    return ref[rows, at : at + LANES], ref[rows, at + LANES : at + FACE]


def plane(ref, ends_ref, rows, x):
    if x in (0, EDGE - 1):
        return pieces(ends_ref, rows, 1 if x else 0)
    return pieces(ref, rows, x)


def at_rows(base, group):
    return pl.ds(pl.multiple_of(base + group * SUB, SUB), SUB)


def pack_faces_x(ref, owned, group, x, first, second):
    direction = 1 if x else 0
    ref[at_rows(direction * owned, group), :] = first
    ref[at_rows((2 + direction) * owned, group), :] = second


def pack_faces_y(ref, owned, grid, state_ref, group):
    rows = at_rows(0, group)
    for half in range(2):
        low, high = None, None
        for place in range(SUB):
            first, second = pieces(state_ref, rows, half * SUB + place)
            here = grid.strip == place
            first, second = turn(first, EDGE * place), turn(second, EDGE * (place + 1))
            low = first if place == 0 else jnp.where(here, first, low)
            high = second if place == 0 else jnp.where(here, second, high)
        ref[at_rows(2 * half * owned, group), :] = low
        ref[at_rows((2 * half + 1) * owned, group), :] = high


def placed(send_ref, faces, coded):
    if coded:
        rows = picked(send_ref[...], encode(faces))
    else:
        rows = jnp.dot(
            send_ref[...], faces.astype(jnp.bfloat16), preferred_element_type=jnp.float32
        )
    return rows.reshape(rows.shape[0] // ROWS, ROWS, LANES)


def taken(matrix, message, coded):
    rows = message.shape[0] * ROWS
    if coded:
        level = message.astype(jnp.int32).astype(jnp.float32).reshape(rows, LANES)
        return decode(picked(matrix, level))
    return jnp.dot(
        matrix,
        message.astype(jnp.float32).reshape(rows, LANES).astype(jnp.bfloat16),
        preferred_element_type=jnp.float32,
    )


def as_codes(parts):
    return jnp.concatenate(parts, axis=1).astype(jnp.int32).astype(jnp.int16)


def groups(owned, body):
    def step(group, carry):
        body(group)
        return carry

    lax.fori_loop(0, owned // SUB, step, 0)


def pack_kernel(incoming, members, dest_ref, now_hbm, old_hbm, out_ref, held, arrived):
    slots = dest_ref.shape[1]
    cells = now_hbm.shape[1]
    width = cells // CHUNKS
    copies = []
    for chunk in range(CHUNKS):
        for index, ref in ((0, now_hbm), (1, old_hbm)):
            number = 2 * chunk + index
            copy = pltpu.make_async_copy(
                ref.at[:, pl.ds(chunk * width, width)], held.at[number], arrived.at[number]
            )
            copy.start()
            copies.append(copy)
    dest = dest_ref[...]
    src = lax.broadcasted_iota(jnp.int32, (slots, slots), 1)
    other = lax.broadcasted_iota(jnp.int32, (slots, slots), 0)
    across = jnp.broadcast_to(dest, (slots, slots))
    down = jnp.sum(jnp.where(src == other, across, 0), axis=1, keepdims=True)
    receiver = jnp.zeros((1, slots), jnp.int32)
    for member in range(1, members):
        receiver = receiver + (dest >= member * incoming).astype(jnp.int32)
    earlier = (down >= receiver * incoming) & (down < dest)
    place = jnp.sum(earlier.astype(jnp.int32), axis=0, keepdims=True)
    spot = jnp.where(dest >= 0, receiver * CAP + place, -1)
    chosen = jnp.where(other == spot, 1.0, 0.0).astype(jnp.bfloat16)
    for number, copy in enumerate(copies):
        copy.wait()
        rows = jnp.dot(chosen, held[number], preferred_element_type=jnp.float32)
        out_ref[:, :, number * width : (number + 1) * width] = rows.astype(jnp.bfloat16).reshape(
            members, CAP, width
        )


def prepare_kernel(height_ref, column_ref, count_ref, mask_ref):
    owned = height_ref.shape[0]
    row = lax.broadcasted_iota(jnp.int32, (FACE, FACE), 0)
    column = lax.broadcasted_iota(jnp.int32, (FACE, FACE), 1)
    level = (lax.broadcasted_iota(jnp.int32, (owned, FACE), 1) % EDGE).astype(jnp.float32)
    heights = height_ref[...].astype(jnp.bfloat16)
    for x in range(EDGE):
        spread = jnp.where(row == column // EDGE + x * EDGE, 1.0, 0.0).astype(jnp.bfloat16)
        floor = jnp.dot(heights, spread, preferred_element_type=jnp.float32)
        mask_ref[:, x * FACE : (x + 1) * FACE] = jnp.where(level >= floor, 1.0, 0.0)

    def count(group):
        rows = at_rows(0, group)
        columns = column_ref[rows, :]
        near = [
            jnp.broadcast_to(columns[:, at : at + 1], (SUB, LANES))
            for at in range(NEAR, NEAR + 6)
        ]
        grid = Grid(near[4] + near[5])
        for x in range(EDGE):
            total = grid.total(
                lambda at: pieces(mask_ref, rows, at),
                x,
                lambda at: (near[1], near[1]) if at else (near[0], near[0]),
                lambda at: (near[2], near[3]),
            )
            air = pieces(mask_ref, rows, x)
            for half in range(2):
                at = slice(x * FACE + half * LANES, x * FACE + (half + 1) * LANES)
                count_ref[rows, at] = jnp.where(air[half] > 0.0, total[half], -1.0)

    groups(owned, count)


def one_hot(numbers, shape, axis):
    at = lax.broadcasted_iota(jnp.int32, shape, axis).astype(jnp.float32)
    return jnp.where(numbers == at, 1.0, 0.0).astype(jnp.bfloat16)


def begin_kernel(
    got_hbm,
    own_hbm,
    count_hbm,
    column_ref,
    send_at_ref,
    p_ref,
    p_ends_ref,
    q_ref,
    q_ends_ref,
    out_ref,
    send_x_ref,
    send_y_ref,
    got,
    own,
    count,
    x_ref,
    y_ref,
    arrived,
):
    members = got_hbm.shape[0]
    owned, cells = p_ref.shape
    kept = own_hbm.shape[0] // 2
    width = cells // CHUNKS
    copies = [
        pltpu.make_async_copy(own_hbm, own, arrived.at[2 * CHUNKS]),
        pltpu.make_async_copy(count_hbm, count, arrived.at[2 * CHUNKS + 1]),
    ]
    for number in range(2 * CHUNKS):
        copies.append(
            pltpu.make_async_copy(
                got_hbm.at[:, :, pl.ds(number * width, width)], got.at[number], arrived.at[number]
            )
        )
    for copy in copies:
        copy.start()
    columns = column_ref[...]
    chosen = one_hot(columns[:, INBOX : INBOX + 1], (owned, members * CAP), 1)
    order = columns[:, ORDER : ORDER + 1]
    stay = [
        one_hot(jnp.where(order < kept, order + index * kept, -1.0), (owned, 2 * kept), 1)
        for index in range(2)
    ]
    number = 2 * 2 * owned
    for index, ref in enumerate((send_x_ref, send_y_ref)):
        ref[...] = one_hot(send_at_ref[index : index + 1, :], (members * ROWS, number), 0)
    copies[0].wait()
    copies[1].wait()
    for chunk in range(CHUNKS):
        at = slice(chunk * width, (chunk + 1) * width)
        air = jnp.where(count[:, at] >= 0.0, 1.0, 0.0)
        for index, to_ref in enumerate((p_ref, q_ref)):
            copies[2 + 2 * chunk + index].wait()
            rows = jnp.dot(
                chosen,
                got[2 * chunk + index].reshape(members * CAP, width),
                preferred_element_type=jnp.float32,
            )
            rows = rows + jnp.dot(stay[index], own[:, at], preferred_element_type=jnp.float32)
            to_ref[:, at] = air * rows
    for ref, ends_ref in ((p_ref, p_ends_ref), (q_ref, q_ends_ref)):
        ends_ref[:, :FACE] = ref[:, :FACE]
        ends_ref[:, FACE:] = ref[:, cells - FACE :]
    grid = Grid(jnp.ones((SUB, LANES), jnp.float32))

    def faces(group):
        for x in (0, EDGE - 1):
            pack_faces_x(x_ref, owned, group, x, *pieces(p_ref, at_rows(0, group), x))
        pack_faces_y(y_ref, owned, grid, p_ref, group)

    groups(owned, faces)
    parts = [placed(send_x_ref, x_ref[...], False), placed(send_y_ref, y_ref[...], False)]
    out_ref[...] = jnp.concatenate(parts, axis=1).astype(jnp.bfloat16)


def inner_kernel(
    coded,
    last,
    here_ref,
    take_ref,
    column_ref,
    p_ref,
    p_ends_ref,
    q_ref,
    q_ends_ref,
    keep_ref,
    gain_ref,
    lag_ref,
    new_ref,
    y_ref,
    ghost_ref,
):
    owned = p_ref.shape[0]
    ghost_ref[...] = taken(take_ref[...], here_ref[:, ROWS:, :], coded)

    def advance(group):
        rows = at_rows(0, group)
        grid = Grid(jnp.broadcast_to(column_ref[rows, JOINED : JOINED + 1], (SUB, LANES)))
        low, high = (
            [ghost_ref[at_rows((2 * half + d) * owned, group), :] for half in range(2)]
            for d in range(2)
        )

        def ghost_y(x):
            half, place = x // SUB, x % SUB
            return turn(low[half], -EDGE * place), turn(high[half], -EDGE * (place + 1))

        for x in range(EDGE):
            total = grid.total(lambda at: plane(p_ref, p_ends_ref, rows, at), x, None, ghost_y)
            state = plane(p_ref, p_ends_ref, rows, x)
            lagging = plane(q_ref, q_ends_ref, rows, x)
            keep = pieces(keep_ref, rows, x)
            gain = pieces(gain_ref, rows, x)
            lag = pieces(lag_ref, rows, x)
            for h in range(2):
                new_ref[rows, x * FACE + h * LANES : x * FACE + (h + 1) * LANES] = (
                    keep[h] * state[h] + gain[h] * total[h] - lag[h] * lagging[h]
                )

    groups(owned, advance)
    if not last:
        grid = Grid(jnp.ones((SUB, LANES), jnp.float32))
        groups(owned, lambda group: pack_faces_y(y_ref, owned, grid, new_ref, group))


def first_inner_kernel(
    here_ref,
    take_at_ref,
    column_ref,
    count_hbm,
    p_ref,
    p_ends_ref,
    q_ref,
    q_ends_ref,
    part_ref,
    y_ref,
    take_y_ref,
    take_low_ref,
    take_high_ref,
    keep_ref,
    gain_ref,
    lag_ref,
    count,
    ghost_ref,
    arrived,
):
    owned = p_ref.shape[0]
    copy = pltpu.make_async_copy(count_hbm, count, arrived.at[0])
    copy.start()
    message_rows = here_ref.shape[0] * ROWS
    first = 0
    for ref in (take_y_ref, take_low_ref, take_high_ref):
        number = ref.shape[0]
        ref[...] = one_hot(take_at_ref[first : first + number, :], (number, message_rows), 1)
        first += number
    copy.wait()

    def fields(group):
        rows = at_rows(0, group)
        rate = jnp.broadcast_to(column_ref[rows, RATE : RATE + 1], (SUB, LANES))
        for x in range(EDGE):
            for half, opened in enumerate(pieces(count, rows, x)):
                air = jnp.where(opened >= 0.0, 1.0, 0.0)
                damping = courant * (6.0 - opened) * rate / 2.0
                share = air / (1.0 + damping)
                at = slice(x * FACE + half * LANES, x * FACE + (half + 1) * LANES)
                keep_ref[rows, at] = (2.0 - opened * courant_sq) * share
                gain_ref[rows, at] = courant_sq * share
                lag_ref[rows, at] = (1.0 - damping) * share

    groups(owned, fields)
    inner_kernel(
        False, False, here_ref, take_y_ref, column_ref, p_ref, p_ends_ref, q_ref, q_ends_ref,
        keep_ref, gain_ref, lag_ref, part_ref, y_ref, ghost_ref,
    )


def last_inner_kernel(*refs):
    inner_kernel(True, True, *refs[:-1], None, refs[-1])


def outer_kernel(
    coded,
    last,
    low_ref,
    high_ref,
    take_low_ref,
    take_high_ref,
    gain_ref,
    part_ref,
    y_ref,
    send_x_ref,
    send_y_ref,
    ends_ref,
    out_ref,
    ghost_low,
    ghost_high,
    x_ref,
    y_out,
):
    owned = part_ref.shape[0]
    ghost_low[...] = taken(take_low_ref[...], low_ref[...], coded)
    ghost_high[...] = taken(take_high_ref[...], high_ref[...], coded)
    grid = Grid(jnp.ones((SUB, LANES), jnp.float32))
    if not last:
        y_out[...] = y_ref[...]

    def finish(group):
        rows = at_rows(0, group)
        for x, ghost in ((0, ghost_low), (EDGE - 1, ghost_high)):
            part = pieces(part_ref, rows, x)
            gain = pieces(gain_ref, rows, x)
            done = [
                part[h] + gain[h] * ghost[at_rows(h * owned, group), :] for h in range(2)
            ]
            for h in range(2):
                at = (FACE if x else 0) + h * LANES
                ends_ref[rows, at : at + LANES] = done[h]
            if last:
                continue
            pack_faces_x(x_ref, owned, group, x, *done)
            half, place = x // SUB, x % SUB
            here = grid.strip == place
            for d, face in enumerate(
                (turn(done[0], EDGE * place), turn(done[1], EDGE * (place + 1)))
            ):
                at = at_rows((2 * half + d) * owned, group)
                y_out[at, :] = jnp.where(here, face, y_out[at, :])

    groups(owned, finish)
    if not last:
        out_ref[...] = as_codes(
            [placed(send_x_ref, x_ref[...], True), placed(send_y_ref, y_out[...], True)]
        )


def last_outer_kernel(
    low_ref, high_ref, take_low_ref, take_high_ref, gain_ref, part_ref, place_ref, out_ref, a, b, ends
):
    outer_kernel(
        True, True, low_ref, high_ref, take_low_ref, take_high_ref, gain_ref, part_ref,
        None, None, None, ends, None, a, b, None, None,
    )
    owned, cells = part_ref.shape
    back = one_hot(place_ref[...], (owned, owned), 1)
    out_ref[:, FACE : cells - FACE] = picked(back, part_ref[:, FACE : cells - FACE])
    out_ref[:, :FACE] = picked(back, ends[:, :FACE])
    out_ref[:, cells - FACE :] = picked(back, ends[:, FACE:])


def on_device(
    resident_now,
    resident_old,
    source_now,
    source_old,
    destination,
    anchor,
    floor_height,
    admit_class,
    admittance,
    neighbours,
):
    members = lax.axis_size("dom")
    slabs = lax.axis_size("slab")
    owned = floor_height.shape[0]
    incoming = anchor.shape[0]
    cells = source_now.shape[1]
    kept = owned - incoming
    f32, bf16, i32 = jnp.float32, jnp.bfloat16, jnp.int32

    width = cells // CHUNKS
    outgoing = pl.pallas_call(
        functools.partial(pack_kernel, incoming, members),
        out_shape=jax.ShapeDtypeStruct((members, CAP, 2 * cells), bf16),
        in_specs=[
            pl.BlockSpec(memory_space=pltpu.VMEM),
            pl.BlockSpec(memory_space=pltpu.HBM),
            pl.BlockSpec(memory_space=pltpu.HBM),
        ],
        scratch_shapes=[
            pltpu.VMEM((2 * CHUNKS, source_now.shape[0], width), bf16),
            pltpu.SemaphoreType.DMA((2 * CHUNKS,)),
        ],
        compiler_params=pltpu.CompilerParams(vmem_limit_bytes=60 * 1024 * 1024),
    )(destination[None, :], source_now, source_old)
    got = lax.all_to_all(outgoing, "dom", split_axis=0, concat_axis=0, tiled=True)

    present = neighbours >= 0
    peer_dev = neighbours // owned % members
    peer_slot = neighbours % owned
    slot_ids = jnp.arange(owned, dtype=i32)
    lower = present[5]
    upper = present[4]
    lower_rank = jnp.sum((lower[None, :] & (slot_ids[None, :] < slot_ids[:, None])).astype(i32), axis=1)
    partner_rank = jnp.sum(
        (lower[None, :] & (slot_ids[None, :] < peer_slot[4][:, None])).astype(i32), axis=1
    )
    alone = ~(lower | upper)
    alone_rank = jnp.sum((alone[None, :] & (slot_ids[None, :] < slot_ids[:, None])).astype(i32), axis=1)
    pairs = jnp.sum(lower.astype(i32))
    position = jnp.where(
        lower, 2 * lower_rank, jnp.where(upper, 2 * partner_rank + 1, 2 * pairs + alone_rank)
    )
    order_is = position[None, :] == slot_ids[:, None]
    order = jnp.sum(jnp.where(order_is, slot_ids[None, :], 0), axis=1)
    seat = rank_within(anchor, jnp.arange(incoming, dtype=i32), anchor >= 0)
    inbox = jnp.concatenate([jnp.full((kept,), -1, i32), anchor * CAP + seat])
    class_ids = jnp.arange(admittance.shape[0], dtype=i32)
    send_at = []
    take_at = []
    for d in range(DIRS):
        order_out = rank_within(peer_dev[d], peer_slot[d], present[d])
        order_in = rank_within(peer_dev[d], slot_ids, present[d])
        send_at.append(jnp.where(present[d], peer_dev[d] * ROWS + d % 2 * CAP + order_out, -ROWS))
        take_at.append(jnp.where(present[d], peer_dev[d] * ROWS + (d + 1) % 2 * CAP + order_in, -ROWS))
    rates = jnp.sum(
        jnp.where(admit_class[:, None] == class_ids[None, :], admittance[None, :], 0.0), axis=1
    )
    near = [present[d].astype(f32) for d in range(6)]
    table = jnp.stack(
        [number.astype(f32) for number in send_at + take_at + [inbox, slot_ids]]
        + [rates, near[4] + near[5]]
        + near
    )
    table = jnp.sum(jnp.where(order_is[None], table[:, None, :], 0.0), axis=2)
    columns = table[2 * DIRS :].T
    halved = jnp.arange(2, dtype=i32).astype(f32) * (2 * CAP)
    send_at = (table[:DIRS].reshape(2, 1, 2, owned) + halved[None, :, None, None]).reshape(2, -1)
    take_at = jnp.concatenate(
        [
            (table[DIRS + 2 : DIRS + 4][None] + halved[:, None, None]).reshape(-1, 1),
            (table[DIRS : DIRS + 1] + halved[:, None]).reshape(-1, 1),
            (table[DIRS + 1 : DIRS + 2] + halved[:, None]).reshape(-1, 1),
        ]
    )
    place = position[:, None].astype(f32)
    heights = floor_height[order].astype(f32)
    own = jnp.concatenate([resident_now, resident_old])

    hbm = pl.BlockSpec(memory_space=pltpu.HBM)
    near_by = pl.BlockSpec(memory_space=pltpu.VMEM)
    grid_shape = jax.ShapeDtypeStruct((owned, cells), f32)
    count = pl.pallas_call(
        prepare_kernel,
        out_shape=grid_shape,
        scratch_shapes=[pltpu.VMEM((owned, cells), f32)],
        compiler_params=VMEM,
    )(heights, columns)
    got, own, count, columns, send_at, take_at, place = lax.optimization_barrier(
        (got, own, count, columns, send_at, take_at, place)
    )

    message = (members, 2 * ROWS, LANES)
    faces_shape = (2 * 2 * owned, LANES)
    faces_scratch = pltpu.VMEM(faces_shape, f32)
    ghost_scratch = pltpu.VMEM((2 * owned, LANES), f32)
    ends_shape = jax.ShapeDtypeStruct((owned, 2 * FACE), f32)
    message_rows = members * ROWS
    *fields, outbox, send_x, send_y = pl.pallas_call(
        begin_kernel,
        out_shape=[grid_shape, ends_shape] * 2
        + [jax.ShapeDtypeStruct(message, bf16)]
        + [jax.ShapeDtypeStruct((message_rows, faces_shape[0]), bf16)] * 2,
        in_specs=[hbm] * 3 + [near_by] * 2,
        scratch_shapes=[
            pltpu.VMEM((2 * CHUNKS, members, CAP, width), bf16),
            pltpu.VMEM(own.shape, bf16),
            pltpu.VMEM((owned, cells), f32),
            faces_scratch,
            faces_scratch,
            pltpu.SemaphoreType.DMA((2 * CHUNKS + 2,)),
        ],
        compiler_params=VMEM,
    )(got, own, count, columns, send_at)
    state, lagging = fields[:2], fields[2:]
    ends = slabs - 1
    cost = pl.CostEstimate(flops=60 * owned * cells, bytes_accessed=48 * owned * cells, transcendentals=0)
    for sweep in range(ITERS):
        coded = sweep > 0
        here = lax.all_to_all(outbox, "dom", split_axis=0, concat_axis=0, tiled=True)
        across_x = lax.slice_in_dim(here, 0, ROWS, axis=1)
        from_low = lax.ppermute(across_x, "slab", [(i, i + 1) for i in range(ends)])
        from_high = lax.ppermute(across_x, "slab", [(i + 1, i) for i in range(ends)])
        if sweep == 0:
            part, faces, take_y, take_low, take_high, keep, gain, lag = pl.pallas_call(
                first_inner_kernel,
                out_shape=[grid_shape, jax.ShapeDtypeStruct(faces_shape, f32)]
                + [
                    jax.ShapeDtypeStruct((number, message_rows), bf16)
                    for number in (4 * owned, 2 * owned, 2 * owned)
                ]
                + [grid_shape] * 3,
                in_specs=[near_by] * 3 + [hbm] + [near_by] * 4,
                scratch_shapes=[
                    pltpu.VMEM((owned, cells), f32),
                    faces_scratch,
                    pltpu.SemaphoreType.DMA((1,)),
                ],
                compiler_params=VMEM,
                cost_estimate=cost,
            )(here, take_at, columns, count, *state, *lagging)
        fields = (here, take_y, columns, *state, *lagging, keep, gain, lag)
        if 0 < sweep < ITERS - 1:
            part, faces = pl.pallas_call(
                functools.partial(inner_kernel, coded, False),
                out_shape=[grid_shape, jax.ShapeDtypeStruct(faces_shape, f32)],
                scratch_shapes=[faces_scratch],
                compiler_params=VMEM,
                cost_estimate=cost,
            )(*fields)
        if sweep < ITERS - 1:
            edges, outbox = pl.pallas_call(
                functools.partial(outer_kernel, coded, False),
                out_shape=[ends_shape, jax.ShapeDtypeStruct(message, jnp.int16)],
                scratch_shapes=[ghost_scratch, ghost_scratch, faces_scratch, faces_scratch],
                compiler_params=VMEM,
            )(from_low, from_high, take_low, take_high, gain, part, faces, send_x, send_y)
        else:
            part = pl.pallas_call(
                last_inner_kernel,
                out_shape=grid_shape,
                scratch_shapes=[faces_scratch],
                compiler_params=VMEM,
                cost_estimate=cost,
            )(*fields)
            return pl.pallas_call(
                last_outer_kernel,
                out_shape=grid_shape,
                scratch_shapes=[ghost_scratch, ghost_scratch, pltpu.VMEM((owned, 2 * FACE), f32)],
                compiler_params=VMEM,
            )(from_low, from_high, take_low, take_high, gain, part, place)
        lagging, state = state, (part, edges)


def solution(mesh):
    split = P(("slab", "dom"), None)
    line = P(("slab", "dom"))
    return jax.shard_map(
        on_device,
        mesh=mesh,
        in_specs=(split, split, split, split, line, line, split, line, P(), P(None, ("slab", "dom"))),
        out_specs=split,
        check_vma=False,
    )
```

time: 249 us -> 220 us (0.88)
  blocking collectives: 37 us -> 81.5 us
  waiting for transfers between devices: 91.4 us -> 47.6 us
  starting transfers between devices: 63.9 us -> 49.3 us
  Pallas kernels: 35.3 us -> 28.2 us
  local copies, waits for them, and re-layouts: 14.4 us -> 8.2 us
    all_to_all x2 -> x4, blocking collectives: 37 us -> 81.5 us  [on_device(): lax.all_to_all(outbox, 'dom', split_axis=0, concat_axis=0, tiled=True)]
    all_to_all x2 -> x0, waiting for transfers between devices: 26.9 us -> none  [on_device(): lax.all_to_all(outbox, 'dom', split_axis=0, concat_axis=0, tiled=True)]
    all_to_all x2 -> x0, starting transfers between devices: 17.6 us -> none  [on_device(): lax.all_to_all(outbox, 'dom', split_axis=0, concat_axis=0, tiled=True)]
    ppermute x8, waiting for transfers between devices: 20.1 us -> 3.46 us  [the longest x4 3.45 us: on_device(): lax.ppermute(across_x, 'slab', [(i + 1, i) for i in range(ends)])]
    pallas_call x6 -> x10, Pallas kernels: 33.5 us -> 23.7 us  [the longest x2 6.13 us: on_device(): pl.pallas_call(functools.partial(inner_kernel, coded, False), out_shape=[...]
    unnamed x42 -> x37, local copies, waits for them, and re-layouts: 13.2 us -> 6.29 us
    ppermute x8, starting transfers between devices: 27.1 us -> 30.3 us  [the longest x4 22.6 us: on_device(): from_low = lax.ppermute(across_x, 'slab', [(i, i + 1) for i in range(ends)])]
    pallas_call x1, Pallas kernels: 1.87 us -> 4.43 us  [on_device(): pl.pallas_call(functools.partial(pack_kernel, incoming, members), out_sha...]
  transfers between devices with their start and end apart: 11 -> 9, of which waited for: 11 -> 4; matrix products, arithmetic and copies ran while one was open for 2% -> 2% of each run, Pallas kernels for 1% -> 7%
where the time goes in v1:
time: 220 us; the launch traced here: 219 us
  blocking collectives  81.5 us (37%)
  starting transfers between devices  49.3 us (22%)
  waiting for transfers between devices  47.6 us (22%)
  Pallas kernels  28.2 us (13%)
  local copies, waits for them, and re-layouts  8.2 us (4%)
  other arithmetic  3.34 us (2%)
    all_to_all x4, blocking collectives, on_device(): lax.all_to_all(outbox, 'dom', split_axis=0, concat_axis=0, tiled=True)  81.5 us
    all_to_all x1, waiting for transfers between devices, on_device(): lax.all_to_all(outgoing, 'dom', split_axis=0, concat_axis=0, tiled=True)  44.1 us
    ppermute x4, starting transfers between devices, on_device(): from_low = lax.ppermute(across_x, 'slab', [(i, i + 1) for i in range(ends)])  22.6 us
    all_to_all x1, starting transfers between devices, on_device(): lax.all_to_all(outgoing, 'dom', split_axis=0, concat_axis=0, tiled=True)  19 us
    ppermute x4, starting transfers between devices, on_device(): lax.ppermute(across_x, 'slab', [(i + 1, i) for i in range(ends)])  7.68 us
    unnamed x37, local copies, waits for them, and re-layouts  6.29 us
    pallas_call x2, Pallas kernels, on_device(): pl.pallas_call(functools.partial(inner_kernel, coded, False), out_shape=[...  6.13 us
    pallas_call x1, Pallas kernels, on_device(): pl.pallas_call(functools.partial(pack_kernel, incoming, members), out_sha...  4.43 us
  transfers between devices with their start and end apart: 9, of which 4 were waited for; matrix products, arithmetic and copies ran while one was open for 2% of the time, Pallas kernels for 7%

profile of v1, /device:TPU:1, one launch (start us, length us, event | category | flops | bytes accessed | tf_op | source)
XLA Modules:
  0.0 219.2 jit_solution(13204458249627126627)
XLA Ops:
  0.0 4.4 %shard_map.100 = bf16[48,2,8192]{2,1,0:T(2,128)(2,1)} custom-call(s32[1,96]{1,0:T(1,128)} %bitcast.123, bf16[96,4096]{1,0:T(8,128)(2,1)} %now_hbm.1, bf16[96,4096]{1,0:T(8,128)(2,1)} %old_hbm.1), custom_call_target="tpu_custom_call" | custom-call | tf_op jit(solution)/shard_map/pallas_call | solution.py:529
  4.5 19.0 %all-to-all-start = ((bf16[48,2,8192]{2,1,0:T(2,128)(2,1)}), bf16[48,2,8192]{2,1,0:T(2,128)(2,1)S(1)}, u32[]{:S(2)}, u32[]{:S(2)}) async-start(bf16[48,2,8192]{2,1,0:T(2,128)(2,1)} %shard_map.100), calls=%async_computation | async-start | bytes 3145728 | tf_op jit(solution)/shard_map/all_to_all | solution.py:543
  28.8 2.5 %shard_map.101.count_hbm = f32[56,4096]{1,0:T(8,128)S(1)} custom-call(f32[56,256]{1,0:T(8,128)S(1)} %convert_element_type.149.height_ref, f32[56,10]{1,0:T(8,128)S(1)} %bitcast.115), custom_call_target="tpu_custom_call" | custom-call | tf_op jit(solution)/shard_map/pallas_call | solution.py:600
  32.0 44.1 %all-to-all-done.got_hbm = bf16[48,2,8192]{2,1,0:T(2,128)(2,1)S(1)} async-done(((bf16[48,2,8192]{2,1,0:T(2,128)(2,1)}), bf16[48,2,8192]{2,1,0:T(2,128)(2,1)S(1)}, u32[]{:S(2)}, u32[]{:S(2)}) %all-to-all-start) | async-done | bytes 1572896 | tf_op jit(solution)/shard_map/all_to_all | solution.py:543
  77.0 3.5 %shard_map.102 = (f32[56,4096]{1,0:T(8,128)S(1)}, f32[56,512]{1,0:T(8,128)S(1)}, f32[56,4096]{1,0:T(8,128)S(1)}, f32[56,512]{1,0:T(8,128)S(1)}, bf16[48,16,128]{...) custom-call(bf16[48,2,8192]{2,1,0:T(2,128)(2,1)S(1)} %all-to-all-done.got_hbm, ...), custom_call_target="tpu_custom_call" | custom-call | tf_op jit(solution)/shard_map/pallas_call | solution.py:616
  82.8 25.3 %all_to_all.25.here_ref = bf16[48,16,128]{2,1,0:T(8,128)(2,1)S(1)} all-to-all(bf16[48,16,128]{2,1,0:T(8,128)(2,1)S(1)} %get-tuple-element.42), channel_id=1, replica_groups=mesh['slab'=16,'dom'=48] {'dom'}, dimensions={0} | all-to-all | bytes 393216 | tf_op jit(solution)/shard_map/all_to_all | solution.py:637
  108.1 6.2 %collective-permute-start = (bf16[48,8,128]{2,1,0:T(8,128)(2,1)S(1)}, bf16[48,8,128]{2,1,0:T(8,128)(2,1)S(1)}, u32[]{:S(2)}, u32[]{:S(2)}) collective-permute-start(bf16[48,8,128]{2,1,0:T(8,128)(2,1)S(1)} %slice.133), channel_id=1, source_target_pairs={{0,48},{48,96},{96,144},{144,192},{192,240},{240,288},{288,336},{3... | collective-permute-start | bytes 294920 | tf_op jit(solution)/shard_map/ppermute | solution.py:639
  114.3 1.9 collective-permute-start.1
  116.4 1.2 copy-done.6
  119.4 4.2 %shard_map.103 = (f32[56,4096]{1,0:T(8,128)S(1)}, f32[224,128]{1,0:T(8,128)S(1)}, bf16[224,384]{1,0:T(8,128)(2,1)S(1)}, bf16[112,384]{1,0:T(8,128)(2,1)S(1)}, bf...) custom-call(bf16[48,16,128]{2,1,0:T(8,128)(2,1)S(1)} %all_to_all.25.here_r, ...), custom_call_target="tpu_custom_call" | custom-call | flops 13762560 | bytes 11010048 | tf_op jit(solution)/shard_map/pallas_call | solution.py:642
  124.7 18.8 %all_to_all.26.here_ref = s16[48,16,128]{2,1,0:T(8,128)(2,1)S(1)} all-to-all(s16[48,16,128]{2,1,0:T(8,128)(2,1)S(1)} %get-tuple-element.55), channel_id=1, replica_groups=mesh['slab'=16,'dom'=48] {'dom'}, dimensions={0} | all-to-all | bytes 393216 | tf_op jit(solution)/shard_map/all_to_all | solution.py:637
  143.6 5.5 %collective-permute-start.2 = (s16[48,8,128]{2,1,0:T(8,128)(2,1)S(1)}, s16[48,8,128]{2,1,0:T(8,128)(2,1)S(1)}, u32[]{:S(2)}, u32[]{:S(2)}) collective-permute-start(s16[48,8,128]{2,1,0:T(8,128)(2,1)S(1)} %slice.134), channel_id=1, source_target_pairs={{0,48},{48,96},{96,144},{144,192},{192,240},{240,288},{288,336},{3... | collective-permute-start | bytes 294920 | tf_op jit(solution)/shard_map/ppermute | solution.py:639
  149.1 1.9 collective-permute-start.3
  151.0 3.1 %shard_map.105 = (f32[56,4096]{1,0:T(8,128)S(1)}, f32[224,128]{1,0:T(8,128)S(1)}) custom-call(s16[48,16,128]{2,1,0:T(8,128)(2,1)S(1)} %all_to_all.26.here_ref, bf16[224,384]{1,0:T(8,128)(2,1)S(1)} %get-tuple-element.56.take_ref.refs_1_, f32[56,10]{1,0:T(8,128)S(1)} %bitcast.118, f32[56,4096]{1,0:T(8,128)S(1)} %get-tuple-element.51.part_ref.p_ref.q_ref, ...), custom_call_target="tpu_custom_call" | custom-call | flops 13762560 | bytes 11010048 | tf_op jit(solution)/shard_map/pallas_call | solution.py:661
  156.1 18.6 %all_to_all.27.here_ref = s16[48,16,128]{2,1,0:T(8,128)(2,1)S(1)} all-to-all(s16[48,16,128]{2,1,0:T(8,128)(2,1)S(1)} %get-tuple-element.62), channel_id=1, replica_groups=mesh['slab'=16,'dom'=48] {'dom'}, dimensions={0} | all-to-all | bytes 393216 | tf_op jit(solution)/shard_map/all_to_all | solution.py:637
  174.7 5.5 %collective-permute-start.4 = (s16[48,8,128]{2,1,0:T(8,128)(2,1)S(1)}, s16[48,8,128]{2,1,0:T(8,128)(2,1)S(1)}, u32[]{:S(2)}, u32[]{:S(2)}) collective-permute-start(s16[48,8,128]{2,1,0:T(8,128)(2,1)S(1)} %slice.135), channel_id=1, source_target_pairs={{0,48},{48,96},{96,144},{144,192},{192,240},{240,288},{288,336},{3... | collective-permute-start | bytes 294920 | tf_op jit(solution)/shard_map/ppermute | solution.py:639
  180.3 1.9 collective-permute-start.5
  182.2 3.1 %shard_map.107 = (f32[56,4096]{1,0:T(8,128)S(1)}, f32[224,128]{1,0:T(8,128)S(1)}) custom-call(s16[48,16,128]{2,1,0:T(8,128)(2,1)S(1)} %all_to_all.27.here_ref, bf16[224,384]{1,0:T(8,128)(2,1)S(1)} %get-tuple-element.56.take_ref.refs_1_, f32[56,10]{1,0:T(8,128)S(1)} %bitcast.119, f32[56,4096]{1,0:T(8,128)S(1)} %get-tuple-element.60.part_ref.p_ref.refs_5_, ...), custom_call_target="tpu_custom_call" | custom-call | flops 13762560 | bytes 11010048 | tf_op jit(solution)/shard_map/pallas_call | solution.py:661
  187.3 18.7 %all_to_all.28.refs_0_ = s16[48,16,128]{2,1,0:T(8,128)(2,1)S(1)} all-to-all(s16[48,16,128]{2,1,0:T(8,128)(2,1)S(1)} %get-tuple-element.66), channel_id=1, replica_groups=mesh['slab'=16,'dom'=48] {'dom'}, dimensions={0} | all-to-all | bytes 393216 | tf_op jit(solution)/shard_map/all_to_all | solution.py:637
  206.1 5.5 %collective-permute-start.6 = (s16[48,8,128]{2,1,0:T(8,128)(2,1)S(1)}, s16[48,8,128]{2,1,0:T(8,128)(2,1)S(1)}, u32[]{:S(2)}, u32[]{:S(2)}) collective-permute-start(s16[48,8,128]{2,1,0:T(8,128)(2,1)S(1)} %slice.136), channel_id=1, source_target_pairs={{0,48},{48,96},{96,144},{144,192},{192,240},{240,288},{288,336},{3... | collective-permute-start | bytes 294920 | tf_op jit(solution)/shard_map/ppermute | solution.py:639
  211.6 1.9 collective-permute-start.7
  213.5 2.4 %shard_map.109.part_ref = f32[56,4096]{1,0:T(8,128)S(1)} custom-call(s16[48,16,128]{2,1,0:T(8,128)(2,1)S(1)} %all_to_all.28.refs_0_, bf16[224,384]{1,0:T(8,128)(2,1)S(1)} %get-tuple-element.56.take_ref.refs_1_, f32[56,10]{1,0:T(8,128)S(1)} %bitcast.120, f32[56,4096]{1,0:T(8,128)S(1)} %get-tuple-element.64.part_ref.refs_3_, ...), custom_call_target="tpu_custom_call" | custom-call | flops 13762560 | bytes 11010048 | tf_op jit(solution)/shard_map/pallas_call | solution.py:676
  215.9 1.6 collective-permute-done.7.high_ref
  217.5 1.7 shard_map.110
  (105 shorter events, 15.6 us)
Async XLA Ops:
  0.0 27.3 %copy-start = (s32[56,256]{1,0:T(8,128)S(1)}, s32[56,256]{1,0:T(8,128)}, u32[]{:S(2)}) copy-start(s32[56,256]{1,0:T(8,128)} %param.16) | copy-start | bytes 172036
  4.4 19.0 %copy-start.14 = (s32[6,56]{1,0:T(8,128)S(1)}, s32[6,56]{1,0:T(8,128)}, u32[]{:S(2)}) copy-start(s32[6,56]{1,0:T(8,128)} %param.19) | copy-start | bytes 4036
  4.5 19.9 %copy-start.15 = (s32[48]{0:T(128)S(1)}, s32[48]{0:T(128)}, u32[]{:S(2)}) copy-start(s32[48]{0:T(128)} %param.15) | copy-start | bytes 580
  4.5 21.0 %copy-start.16 = (f32[8]{0:T(128)S(1)}, f32[8]{0:T(128)}, u32[]{:S(2)}) copy-start(f32[8]{0:T(128)} %param.18) | copy-start | bytes 100
  4.5 21.0 %copy-start.17 = (s32[56]{0:T(128)S(1)}, s32[56]{0:T(128)}, u32[]{:S(2)}) copy-start(s32[56]{0:T(128)} %param.17) | copy-start | bytes 676
  4.5 71.6 %all-to-all-start = ((bf16[48,2,8192]{2,1,0:T(2,128)(2,1)}), bf16[48,2,8192]{2,1,0:T(2,128)(2,1)S(1)}, u32[]{:S(2)}, u32[]{:S(2)}) async-start(bf16[48,2,8192]{2,1,0:T(2,128)(2,1)} %shard_map.100), calls=%async_computation | async-start | bytes 3145728 | tf_op jit(solution)/shard_map/all_to_all | solution.py:543
  23.5 7.9 %copy-start.12 = (bf16[8,4096]{1,0:T(8,128)(2,1)S(1)}, bf16[8,4096]{1,0:T(8,128)(2,1)}, u32[]{:S(2)}) copy-start(bf16[8,4096]{1,0:T(8,128)(2,1)} %param.11) | copy-start | bytes 196612
  23.5 7.9 %copy-start.13 = (bf16[8,4096]{1,0:T(8,128)(2,1)S(1)}, bf16[8,4096]{1,0:T(8,128)(2,1)}, u32[]{:S(2)}) copy-start(bf16[8,4096]{1,0:T(8,128)(2,1)} %param.10) | copy-start | bytes 196612
  76.1 0.9 copy-start.7
  81.9 0.9 copy-start.5
  82.8 31.5 %copy-start.8 = (f32[56,512]{1,0:T(8,128)}, f32[56,512]{1,0:T(8,128)S(1)}, u32[]{:S(2)}) copy-start(f32[56,512]{1,0:T(8,128)S(1)} %get-tuple-element.45.p_ends_ref.q_ends_ref) | copy-start | bytes 344068
  82.8 31.6 %copy-start.10 = (f32[56,512]{1,0:T(8,128)}, f32[56,512]{1,0:T(8,128)S(1)}, u32[]{:S(2)}) copy-start(f32[56,512]{1,0:T(8,128)S(1)} %get-tuple-element.47.q_ends_ref) | copy-start | bytes 344068
  108.1 15.5 %collective-permute-start = (bf16[48,8,128]{2,1,0:T(8,128)(2,1)S(1)}, bf16[48,8,128]{2,1,0:T(8,128)(2,1)S(1)}, u32[]{:S(2)}, u32[]{:S(2)}) collective-permute-start(bf16[48,8,128]{2,1,0:T(8,128)(2,1)S(1)} %slice.133), channel_id=1, source_target_pairs={{0,48},{48,96},{96,144},{144,192},{192,240},{240,288},{288,336},{3... | collective-permute-start | bytes 294920 | tf_op jit(solution)/shard_map/ppermute | solution.py:639
  114.3 9.3 %collective-permute-start.1 = (bf16[48,8,128]{2,1,0:T(8,128)(2,1)S(1)}, bf16[48,8,128]{2,1,0:T(8,128)(2,1)S(1)}, u32[]{:S(2)}, u32[]{:S(2)}) collective-permute-start(bf16[48,8,128]{2,1,0:T(8,128)(2,1)S(1)} %slice.133), channel_id=1, source_target_pairs={{48,0},{96,48},{144,96},{192,144},{240,192},{288,240},{336,288},{3... | collective-permute-start | bytes 294920 | tf_op jit(solution)/shard_map/ppermute | solution.py:640
  116.4 1.2 copy-start.6
  117.6 0.9 copy-start.9
  119.4 4.2 %copy-start.2 = (bf16[384,224]{1,0:T(8,128)(2,1)S(1)}, bf16[384,224]{1,0:T(8,128)(2,1)}, u32[]{:S(2)}) copy-start(bf16[384,224]{1,0:T(8,128)(2,1)} %copy-done.1) | copy-start | bytes 516100
  119.4 4.2 %copy-start.4 = (bf16[384,224]{1,0:T(8,128)(2,1)S(1)}, bf16[384,224]{1,0:T(8,128)(2,1)}, u32[]{:S(2)}) copy-start(bf16[384,224]{1,0:T(8,128)(2,1)} %copy-done.3) | copy-start | bytes 516100
  143.6 10.5 %collective-permute-start.2 = (s16[48,8,128]{2,1,0:T(8,128)(2,1)S(1)}, s16[48,8,128]{2,1,0:T(8,128)(2,1)S(1)}, u32[]{:S(2)}, u32[]{:S(2)}) collective-permute-start(s16[48,8,128]{2,1,0:T(8,128)(2,1)S(1)} %slice.134), channel_id=1, source_target_pairs={{0,48},{48,96},{96,144},{144,192},{192,240},{240,288},{288,336},{3... | collective-permute-start | bytes 294920 | tf_op jit(solution)/shard_map/ppermute | solution.py:639
  149.1 5.9 %collective-permute-start.3 = (s16[48,8,128]{2,1,0:T(8,128)(2,1)S(1)}, s16[48,8,128]{2,1,0:T(8,128)(2,1)S(1)}, u32[]{:S(2)}, u32[]{:S(2)}) collective-permute-start(s16[48,8,128]{2,1,0:T(8,128)(2,1)S(1)} %slice.134), channel_id=1, source_target_pairs={{48,0},{96,48},{144,96},{192,144},{240,192},{288,240},{336,288},{3... | collective-permute-start | bytes 294920 | tf_op jit(solution)/shard_map/ppermute | solution.py:640
  174.7 10.5 %collective-permute-start.4 = (s16[48,8,128]{2,1,0:T(8,128)(2,1)S(1)}, s16[48,8,128]{2,1,0:T(8,128)(2,1)S(1)}, u32[]{:S(2)}, u32[]{:S(2)}) collective-permute-start(s16[48,8,128]{2,1,0:T(8,128)(2,1)S(1)} %slice.135), channel_id=1, source_target_pairs={{0,48},{48,96},{96,144},{144,192},{192,240},{240,288},{288,336},{3... | collective-permute-start | bytes 294920 | tf_op jit(solution)/shard_map/ppermute | solution.py:639
  180.3 5.9 %collective-permute-start.5 = (s16[48,8,128]{2,1,0:T(8,128)(2,1)S(1)}, s16[48,8,128]{2,1,0:T(8,128)(2,1)S(1)}, u32[]{:S(2)}, u32[]{:S(2)}) collective-permute-start(s16[48,8,128]{2,1,0:T(8,128)(2,1)S(1)} %slice.135), channel_id=1, source_target_pairs={{48,0},{96,48},{144,96},{192,144},{240,192},{288,240},{336,288},{3... | collective-permute-start | bytes 294920 | tf_op jit(solution)/shard_map/ppermute | solution.py:640
  206.1 9.8 %collective-permute-start.6 = (s16[48,8,128]{2,1,0:T(8,128)(2,1)S(1)}, s16[48,8,128]{2,1,0:T(8,128)(2,1)S(1)}, u32[]{:S(2)}, u32[]{:S(2)}) collective-permute-start(s16[48,8,128]{2,1,0:T(8,128)(2,1)S(1)} %slice.136), channel_id=1, source_target_pairs={{0,48},{48,96},{96,144},{144,192},{192,240},{240,288},{288,336},{3... | collective-permute-start | bytes 294920 | tf_op jit(solution)/shard_map/ppermute | solution.py:639
  211.6 5.9 %collective-permute-start.7 = (s16[48,8,128]{2,1,0:T(8,128)(2,1)S(1)}, s16[48,8,128]{2,1,0:T(8,128)(2,1)S(1)}, u32[]{:S(2)}, u32[]{:S(2)}) collective-permute-start(s16[48,8,128]{2,1,0:T(8,128)(2,1)S(1)} %slice.136), channel_id=1, source_target_pairs={{48,0},{96,48},{144,96},{192,144},{240,192},{288,240},{336,288},{3... | collective-permute-start | bytes 294920 | tf_op jit(solution)/shard_map/ppermute | solution.py:640
  (3 other events, 2.2 us)

commit v2 on v1

--- a/solution.py
+++ b/solution.py
@@ -18,7 +18,7 @@
 ROWS = DIRS * CAP
 CHUNKS = 4
 
-INBOX, ORDER, RATE, JOINED, NEAR = 0, 1, 2, 3, 4
+TAKE, INBOX, ORDER, RATE, JOINED, NEAR = 0, 4, 5, 6, 7, 8
 
 courant_sq = 0.3
 courant = 0.3**0.5
@@ -149,12 +149,17 @@
         ref[at_rows((2 * half + 1) * owned, group), :] = high
 
 
-def placed(send_ref, faces, coded):
+def one_hot(numbers, shape, axis):
+    at = lax.broadcasted_iota(jnp.int32, shape, axis).astype(jnp.float32)
+    return jnp.where(numbers == at, 1.0, 0.0).astype(jnp.bfloat16)
+
+
+def placed(matrix, faces, coded):
     if coded:
-        rows = picked(send_ref[...], encode(faces))
+        rows = picked(matrix, encode(faces))
     else:
         rows = jnp.dot(
-            send_ref[...], faces.astype(jnp.bfloat16), preferred_element_type=jnp.float32
+            matrix, faces.astype(jnp.bfloat16), preferred_element_type=jnp.float32
         )
     return rows.reshape(rows.shape[0] // ROWS, ROWS, LANES)
 
@@ -250,74 +255,32 @@
     groups(owned, count)
 
 
-def one_hot(numbers, shape, axis):
-    at = lax.broadcasted_iota(jnp.int32, shape, axis).astype(jnp.float32)
-    return jnp.where(numbers == at, 1.0, 0.0).astype(jnp.bfloat16)
-
-
-def begin_kernel(
-    got_hbm,
-    own_hbm,
-    count_hbm,
-    column_ref,
-    send_at_ref,
-    p_ref,
-    p_ends_ref,
-    q_ref,
-    q_ends_ref,
-    out_ref,
-    send_x_ref,
-    send_y_ref,
-    got,
-    own,
-    count,
-    x_ref,
-    y_ref,
-    arrived,
-):
-    members = got_hbm.shape[0]
-    owned, cells = p_ref.shape
-    kept = own_hbm.shape[0] // 2
+def settled(got_ref, own_ref, columns, index, to_ref, ends_ref, count_ref):
+    owned, cells = to_ref.shape
+    members = got_ref.shape[0]
     width = cells // CHUNKS
-    copies = [
-        pltpu.make_async_copy(own_hbm, own, arrived.at[2 * CHUNKS]),
-        pltpu.make_async_copy(count_hbm, count, arrived.at[2 * CHUNKS + 1]),
-    ]
-    for number in range(2 * CHUNKS):
-        copies.append(
-            pltpu.make_async_copy(
-                got_hbm.at[:, :, pl.ds(number * width, width)], got.at[number], arrived.at[number]
-            )
-        )
-    for copy in copies:
-        copy.start()
-    columns = column_ref[...]
     chosen = one_hot(columns[:, INBOX : INBOX + 1], (owned, members * CAP), 1)
-    order = columns[:, ORDER : ORDER + 1]
-    stay = [
-        one_hot(jnp.where(order < kept, order + index * kept, -1.0), (owned, 2 * kept), 1)
-        for index in range(2)
-    ]
-    number = 2 * 2 * owned
-    for index, ref in enumerate((send_x_ref, send_y_ref)):
-        ref[...] = one_hot(send_at_ref[index : index + 1, :], (members * ROWS, number), 0)
-    copies[0].wait()
-    copies[1].wait()
+    stay = one_hot(columns[:, ORDER : ORDER + 1], (owned, own_ref.shape[0]), 1)
     for chunk in range(CHUNKS):
         at = slice(chunk * width, (chunk + 1) * width)
-        air = jnp.where(count[:, at] >= 0.0, 1.0, 0.0)
-        for index, to_ref in enumerate((p_ref, q_ref)):
-            copies[2 + 2 * chunk + index].wait()
-            rows = jnp.dot(
-                chosen,
-                got[2 * chunk + index].reshape(members * CAP, width),
-                preferred_element_type=jnp.float32,
-            )
-            rows = rows + jnp.dot(stay[index], own[:, at], preferred_element_type=jnp.float32)
-            to_ref[:, at] = air * rows
-    for ref, ends_ref in ((p_ref, p_ends_ref), (q_ref, q_ends_ref)):
-        ends_ref[:, :FACE] = ref[:, :FACE]
-        ends_ref[:, FACE:] = ref[:, cells - FACE :]
+        first = (2 * chunk + index) * width
+        rows = jnp.dot(
+            chosen,
+            got_ref[:, :, first : first + width].reshape(members * CAP, width),
+            preferred_element_type=jnp.float32,
+        )
+        rows = rows + jnp.dot(stay, own_ref[:, at], preferred_element_type=jnp.float32)
+        to_ref[:, at] = jnp.where(count_ref[:, at] >= 0.0, rows, 0.0)
+    ends_ref[:, :FACE] = to_ref[:, :FACE]
+    ends_ref[:, FACE:] = to_ref[:, cells - FACE :]
+
+
+def begin_kernel(
+    got_ref, own_ref, count_ref, column_ref, send_at_ref, p_ref, ends_ref, out_ref, x_ref, y_ref
+):
+    members = got_ref.shape[0]
+    owned = p_ref.shape[0]
+    settled(got_ref, own_ref, column_ref[...], 0, p_ref, ends_ref, count_ref)
     grid = Grid(jnp.ones((SUB, LANES), jnp.float32))
 
     def faces(group):
@@ -326,7 +289,11 @@
         pack_faces_y(y_ref, owned, grid, p_ref, group)
 
     groups(owned, faces)
-    parts = [placed(send_x_ref, x_ref[...], False), placed(send_y_ref, y_ref[...], False)]
+    shape = (members * ROWS, 4 * owned)
+    parts = [
+        placed(one_hot(send_at_ref[index : index + 1, :], shape, 0), ref[...], False)
+        for index, ref in enumerate((x_ref, y_ref))
+    ]
     out_ref[...] = jnp.concatenate(parts, axis=1).astype(jnp.bfloat16)
 
 
@@ -382,41 +349,45 @@
 
 def first_inner_kernel(
     here_ref,
-    take_at_ref,
     column_ref,
-    count_hbm,
+    send_at_ref,
+    got_ref,
+    own_ref,
+    count_ref,
     p_ref,
     p_ends_ref,
+    part_ref,
+    y_ref,
     q_ref,
     q_ends_ref,
-    part_ref,
-    y_ref,
     take_y_ref,
     take_low_ref,
     take_high_ref,
+    send_x_ref,
+    send_y_ref,
     keep_ref,
     gain_ref,
     lag_ref,
-    count,
     ghost_ref,
-    arrived,
 ):
     owned = p_ref.shape[0]
-    copy = pltpu.make_async_copy(count_hbm, count, arrived.at[0])
-    copy.start()
-    message_rows = here_ref.shape[0] * ROWS
-    first = 0
-    for ref in (take_y_ref, take_low_ref, take_high_ref):
-        number = ref.shape[0]
-        ref[...] = one_hot(take_at_ref[first : first + number, :], (number, message_rows), 1)
-        first += number
-    copy.wait()
+    columns = column_ref[...]
+    settled(got_ref, own_ref, columns, 1, q_ref, q_ends_ref, count_ref)
+    for ref, directions in ((take_y_ref, (2, 3)), (take_low_ref, (0,)), (take_high_ref, (1,))):
+        numbers = [
+            columns[:, TAKE + d : TAKE + d + 1] + 2 * CAP * half
+            for half in range(2)
+            for d in directions
+        ]
+        ref[...] = one_hot(jnp.concatenate(numbers, axis=0), ref.shape, 1)
+    for index, ref in enumerate((send_x_ref, send_y_ref)):
+        ref[...] = one_hot(send_at_ref[index : index + 1, :], ref.shape, 0)
 
     def fields(group):
         rows = at_rows(0, group)
         rate = jnp.broadcast_to(column_ref[rows, RATE : RATE + 1], (SUB, LANES))
         for x in range(EDGE):
-            for half, opened in enumerate(pieces(count, rows, x)):
+            for half, opened in enumerate(pieces(count_ref, rows, x)):
                 air = jnp.where(opened >= 0.0, 1.0, 0.0)
                 damping = courant * (6.0 - opened) * rate / 2.0
                 share = air / (1.0 + damping)
@@ -487,7 +458,7 @@
     groups(owned, finish)
     if not last:
         out_ref[...] = as_codes(
-            [placed(send_x_ref, x_ref[...], True), placed(send_y_ref, y_out[...], True)]
+            [placed(send_x_ref[...], x_ref[...], True), placed(send_y_ref[...], y_out[...], True)]
         )
 
 
@@ -580,22 +551,12 @@
         + near
     )
     table = jnp.sum(jnp.where(order_is[None], table[:, None, :], 0.0), axis=2)
-    columns = table[2 * DIRS :].T
+    columns = table[DIRS:].T
     halved = jnp.arange(2, dtype=i32).astype(f32) * (2 * CAP)
     send_at = (table[:DIRS].reshape(2, 1, 2, owned) + halved[None, :, None, None]).reshape(2, -1)
-    take_at = jnp.concatenate(
-        [
-            (table[DIRS + 2 : DIRS + 4][None] + halved[:, None, None]).reshape(-1, 1),
-            (table[DIRS : DIRS + 1] + halved[:, None]).reshape(-1, 1),
-            (table[DIRS + 1 : DIRS + 2] + halved[:, None]).reshape(-1, 1),
-        ]
-    )
     place = position[:, None].astype(f32)
     heights = floor_height[order].astype(f32)
-    own = jnp.concatenate([resident_now, resident_old])
-
-    hbm = pl.BlockSpec(memory_space=pltpu.HBM)
-    near_by = pl.BlockSpec(memory_space=pltpu.VMEM)
+
     grid_shape = jax.ShapeDtypeStruct((owned, cells), f32)
     count = pl.pallas_call(
         prepare_kernel,
@@ -603,8 +564,8 @@
         scratch_shapes=[pltpu.VMEM((owned, cells), f32)],
         compiler_params=VMEM,
     )(heights, columns)
-    got, own, count, columns, send_at, take_at, place = lax.optimization_barrier(
-        (got, own, count, columns, send_at, take_at, place)
+    got, count, columns, send_at, place = lax.optimization_barrier(
+        (got, count, columns, send_at, place)
     )
 
     message = (members, 2 * ROWS, LANES)
@@ -613,50 +574,39 @@
     ghost_scratch = pltpu.VMEM((2 * owned, LANES), f32)
     ends_shape = jax.ShapeDtypeStruct((owned, 2 * FACE), f32)
     message_rows = members * ROWS
-    *fields, outbox, send_x, send_y = pl.pallas_call(
+    *state, outbox = pl.pallas_call(
         begin_kernel,
-        out_shape=[grid_shape, ends_shape] * 2
-        + [jax.ShapeDtypeStruct(message, bf16)]
-        + [jax.ShapeDtypeStruct((message_rows, faces_shape[0]), bf16)] * 2,
-        in_specs=[hbm] * 3 + [near_by] * 2,
-        scratch_shapes=[
-            pltpu.VMEM((2 * CHUNKS, members, CAP, width), bf16),
-            pltpu.VMEM(own.shape, bf16),
-            pltpu.VMEM((owned, cells), f32),
-            faces_scratch,
-            faces_scratch,
-            pltpu.SemaphoreType.DMA((2 * CHUNKS + 2,)),
-        ],
+        out_shape=[grid_shape, ends_shape, jax.ShapeDtypeStruct(message, bf16)],
+        scratch_shapes=[faces_scratch, faces_scratch],
         compiler_params=VMEM,
-    )(got, own, count, columns, send_at)
-    state, lagging = fields[:2], fields[2:]
-    ends = slabs - 1
+    )(got, resident_now, count, columns, send_at)
+
     cost = pl.CostEstimate(flops=60 * owned * cells, bytes_accessed=48 * owned * cells, transcendentals=0)
     for sweep in range(ITERS):
         coded = sweep > 0
         here = lax.all_to_all(outbox, "dom", split_axis=0, concat_axis=0, tiled=True)
         across_x = lax.slice_in_dim(here, 0, ROWS, axis=1)
-        from_low = lax.ppermute(across_x, "slab", [(i, i + 1) for i in range(ends)])
-        from_high = lax.ppermute(across_x, "slab", [(i + 1, i) for i in range(ends)])
+        from_low = lax.ppermute(across_x, "slab", [(i, (i + 1) % slabs) for i in range(slabs)])
+        from_high = lax.ppermute(across_x, "slab", [((i + 1) % slabs, i) for i in range(slabs)])
         if sweep == 0:
-            part, faces, take_y, take_low, take_high, keep, gain, lag = pl.pallas_call(
-                first_inner_kernel,
-                out_shape=[grid_shape, jax.ShapeDtypeStruct(faces_shape, f32)]
-                + [
-                    jax.ShapeDtypeStruct((number, message_rows), bf16)
-                    for number in (4 * owned, 2 * owned, 2 * owned)
-                ]
-                + [grid_shape] * 3,
-                in_specs=[near_by] * 3 + [hbm] + [near_by] * 4,
-                scratch_shapes=[
-                    pltpu.VMEM((owned, cells), f32),
-                    faces_scratch,
-                    pltpu.SemaphoreType.DMA((1,)),
-                ],
-                compiler_params=VMEM,
-                cost_estimate=cost,
-            )(here, take_at, columns, count, *state, *lagging)
-        fields = (here, take_y, columns, *state, *lagging, keep, gain, lag)
+            part, faces, *lagging, take_y, take_low, take_high, send_x, send_y, keep, gain, lag = (
+                pl.pallas_call(
+                    first_inner_kernel,
+                    out_shape=[grid_shape, jax.ShapeDtypeStruct(faces_shape, f32)]
+                    + [grid_shape, ends_shape]
+                    + [
+                        jax.ShapeDtypeStruct((number, message_rows), bf16)
+                        for number in (4 * owned, 2 * owned, 2 * owned)
+                    ]
+                    + [jax.ShapeDtypeStruct((message_rows, 4 * owned), bf16)] * 2
+                    + [grid_shape] * 3,
+                    scratch_shapes=[faces_scratch],
+                    compiler_params=VMEM,
+                    cost_estimate=cost,
+                )(here, columns, send_at, got, resident_old, count, *state)
+            )
+        if sweep:
+            fields = (here, take_y, columns, *state, *lagging, keep, gain, lag)
         if 0 < sweep < ITERS - 1:
             part, faces = pl.pallas_call(
                 functools.partial(inner_kernel, coded, False),

time: 220 us -> 197 us (0.90)
  starting transfers between devices: 49.3 us -> 35.6 us
  local copies, waits for them, and re-layouts: 8.2 us -> 1.66 us
    ppermute x8, starting transfers between devices: 30.3 us -> 16.6 us  [the longest x4 16.6 us: on_device(): lax.ppermute(across_x, 'slab', [(i, (i + 1) % slabs) for i in range(slabs)])]
    unnamed x37 -> x15, local copies, waits for them, and re-layouts: 6.29 us -> 0.13 us
  transfers between devices with their start and end apart: 9 -> 9, of which waited for: 4 -> 4; matrix products, arithmetic and copies ran while one was open for 2% -> 2% of each run, Pallas kernels for 7% -> 8%
where the time goes in v2:
time: 197 us
  blocking collectives  79.7 us (40%)
  waiting for transfers between devices  48.9 us (25%)
  starting transfers between devices  35.6 us (18%)
  Pallas kernels  27.2 us (14%)
  other arithmetic  2.46 us (1%)
    all_to_all x4, blocking collectives, on_device(): lax.all_to_all(outbox, 'dom', split_axis=0, concat_axis=0, tiled=True)  79.7 us
    all_to_all x1, waiting for transfers between devices, on_device(): lax.all_to_all(outgoing, 'dom', split_axis=0, concat_axis=0, tiled=True)  45.3 us
    all_to_all x1, starting transfers between devices, on_device(): lax.all_to_all(outgoing, 'dom', split_axis=0, concat_axis=0, tiled=True)  19 us
    ppermute x4, starting transfers between devices, on_device(): lax.ppermute(across_x, 'slab', [(i, (i + 1) % slabs) for i in range(slabs)])  16.6 us
    pallas_call x2, Pallas kernels, on_device(): pl.pallas_call(functools.partial(inner_kernel, coded, False), out_shape=[...  6.12 us
    pallas_call x1, Pallas kernels, on_device(): pl.pallas_call(first_inner_kernel, out_shape=[grid_shape, jax.ShapeDtypeS...  5.25 us
    pallas_call x1, Pallas kernels, on_device(): pl.pallas_call(functools.partial(pack_kernel, incoming, members), out_sha...  4.43 us
  transfers between devices with their start and end apart: 9, of which 4 were waited for; matrix products, arithmetic and copies ran while one was open for 2% of the time, Pallas kernels for 8%

profile of v2, /device:TPU:1, one launch (start us, length us, event | category | flops | bytes accessed | tf_op | source)
XLA Modules:
  0.0 196.6 jit_solution(12410803617270770199)
XLA Ops:
  0.0 4.4 %shard_map.100 = bf16[48,2,8192]{2,1,0:T(2,128)(2,1)} custom-call(s32[1,96]{1,0:T(1,128)} %bitcast.119, bf16[96,4096]{1,0:T(8,128)(2,1)} %now_hbm.1, bf16[96,4096]{1,0:T(8,128)(2,1)} %old_hbm.1), custom_call_target="tpu_custom_call" | custom-call | tf_op jit(solution)/shard_map/pallas_call | solution.py:500
  4.5 19.0 %all-to-all-start = ((bf16[48,2,8192]{2,1,0:T(2,128)(2,1)}), bf16[48,2,8192]{2,1,0:T(2,128)(2,1)S(1)}, u32[]{:S(2)}, u32[]{:S(2)}) async-start(bf16[48,2,8192]{2,1,0:T(2,128)(2,1)} %shard_map.100), calls=%async_computation | async-start | bytes 3145728 | tf_op jit(solution)/shard_map/all_to_all | solution.py:514
  28.4 2.5 %shard_map.101.count_ref = f32[56,4096]{1,0:T(8,128)S(1)} custom-call(f32[56,256]{1,0:T(8,128)S(1)} %convert_element_type.135.height_ref, f32[56,14]{1,0:T(8,128)S(1)} %bitcast.111), custom_call_target="tpu_custom_call" | custom-call | tf_op jit(solution)/shard_map/pallas_call | solution.py:561
  30.9 45.3 %all-to-all-done.got_ref = bf16[48,2,8192]{2,1,0:T(2,128)(2,1)S(1)} async-done(((bf16[48,2,8192]{2,1,0:T(2,128)(2,1)}), bf16[48,2,8192]{2,1,0:T(2,128)(2,1)S(1)}, u32[]{:S(2)}, u32[]{:S(2)}) %all-to-all-start) | async-done | bytes 1572896 | tf_op jit(solution)/shard_map/all_to_all | solution.py:514
  76.1 1.4 shard_map.102
  77.6 25.4 %all_to_all.25.here_ref = bf16[48,16,128]{2,1,0:T(8,128)(2,1)S(1)} all-to-all(bf16[48,16,128]{2,1,0:T(8,128)(2,1)S(1)} %get-tuple-element.37), channel_id=1, replica_groups=mesh['slab'=16,'dom'=48] {'dom'}, dimensions={0} | all-to-all | bytes 393216 | tf_op jit(solution)/shard_map/all_to_all | solution.py:587
  102.9 4.3 %collective-permute-start = (bf16[48,8,128]{2,1,0:T(8,128)(2,1)S(1)}, bf16[48,8,128]{2,1,0:T(8,128)(2,1)S(1)}, u32[]{:S(2)}, u32[]{:S(2)}) collective-permute-start(bf16[48,8,128]{2,1,0:T(8,128)(2,1)S(1)} %slice.118), channel_id=1, source_target_pairs={{0,48},{48,96},{96,144},{144,192},{192,240},{240,288},{288,336},{3... | collective-permute-start | bytes 294920 | tf_op jit(solution)/shard_map/ppermute | solution.py:589
  107.2 5.3 %shard_map.103 = (f32[56,4096]{1,0:T(8,128)S(1)}, f32[224,128]{1,0:T(8,128)S(1)}, f32[56,4096]{1,0:T(8,128)}, f32[56,512]{1,0:T(8,128)}, bf16[224,384]{1,0:T(8,1...) custom-call(bf16[48,16,128]{2,1,0:T(8,128)(2,1)S(1)} %all_to_all.25., ...), custom_call_target="tpu_custom_call" | custom-call | flops 13762560 | bytes 11010048 | tf_op jit(solution)/shard_map/pallas_call | solution.py:593
  112.5 1.1 shard_map.104
  113.6 17.4 %all_to_all.26.here_ref = s16[48,16,128]{2,1,0:T(8,128)(2,1)S(1)} all-to-all(s16[48,16,128]{2,1,0:T(8,128)(2,1)S(1)} %get-tuple-element.47), channel_id=1, replica_groups=mesh['slab'=16,'dom'=48] {'dom'}, dimensions={0} | all-to-all | bytes 393216 | tf_op jit(solution)/shard_map/all_to_all | solution.py:587
  131.0 4.9 %collective-permute-start.2 = (s16[48,8,128]{2,1,0:T(8,128)(2,1)S(1)}, s16[48,8,128]{2,1,0:T(8,128)(2,1)S(1)}, u32[]{:S(2)}, u32[]{:S(2)}) collective-permute-start(s16[48,8,128]{2,1,0:T(8,128)(2,1)S(1)} %slice.119), channel_id=1, source_target_pairs={{0,48},{48,96},{96,144},{144,192},{192,240},{240,288},{288,336},{3... | collective-permute-start | bytes 294920 | tf_op jit(solution)/shard_map/ppermute | solution.py:589
  136.0 3.1 %shard_map.105 = (f32[56,4096]{1,0:T(8,128)S(1)}, f32[224,128]{1,0:T(8,128)S(1)}) custom-call(s16[48,16,128]{2,1,0:T(8,128)(2,1)S(1)} %all_to_all.26.here_ref, bf16[224,384]{1,0:T(8,128)(2,1)S(1)} %get-tuple-element.48.take_ref.refs_1_, f32[56,14]{1,0:T(8,128)S(1)} %bitcast.114, f32[56,4096]{1,0:T(8,128)S(1)} %get-tuple-element.43.part_ref.p_ref.q_ref, ...), custom_call_target="tpu_custom_call" | custom-call | flops 13762560 | bytes 11010048 | tf_op jit(solution)/shard_map/pallas_call | solution.py:611
  139.1 1.1 collective-permute-done.3.high_ref
  140.2 1.1 shard_map.106
  141.3 18.8 %all_to_all.27.here_ref = s16[48,16,128]{2,1,0:T(8,128)(2,1)S(1)} all-to-all(s16[48,16,128]{2,1,0:T(8,128)(2,1)S(1)} %get-tuple-element.54), channel_id=1, replica_groups=mesh['slab'=16,'dom'=48] {'dom'}, dimensions={0} | all-to-all | bytes 393216 | tf_op jit(solution)/shard_map/all_to_all | solution.py:587
  160.1 3.2 %collective-permute-start.4 = (s16[48,8,128]{2,1,0:T(8,128)(2,1)S(1)}, s16[48,8,128]{2,1,0:T(8,128)(2,1)S(1)}, u32[]{:S(2)}, u32[]{:S(2)}) collective-permute-start(s16[48,8,128]{2,1,0:T(8,128)(2,1)S(1)} %slice.120), channel_id=1, source_target_pairs={{0,48},{48,96},{96,144},{144,192},{192,240},{240,288},{288,336},{3... | collective-permute-start | bytes 294920 | tf_op jit(solution)/shard_map/ppermute | solution.py:589
  163.4 3.1 %shard_map.107 = (f32[56,4096]{1,0:T(8,128)S(1)}, f32[224,128]{1,0:T(8,128)S(1)}) custom-call(s16[48,16,128]{2,1,0:T(8,128)(2,1)S(1)} %all_to_all.27.here_ref, bf16[224,384]{1,0:T(8,128)(2,1)S(1)} %get-tuple-element.48.take_ref.refs_1_, f32[56,14]{1,0:T(8,128)S(1)} %bitcast.115, f32[56,4096]{1,0:T(8,128)S(1)} %get-tuple-element.52.part_ref.p_ref.refs_5_, ...), custom_call_target="tpu_custom_call" | custom-call | flops 13762560 | bytes 11010048 | tf_op jit(solution)/shard_map/pallas_call | solution.py:611
  166.4 1.0 collective-permute-done.5.high_ref
  167.4 1.1 shard_map.108
  168.5 18.1 %all_to_all.28.refs_0_ = s16[48,16,128]{2,1,0:T(8,128)(2,1)S(1)} all-to-all(s16[48,16,128]{2,1,0:T(8,128)(2,1)S(1)} %get-tuple-element.58), channel_id=1, replica_groups=mesh['slab'=16,'dom'=48] {'dom'}, dimensions={0} | all-to-all | bytes 393216 | tf_op jit(solution)/shard_map/all_to_all | solution.py:587
  186.7 4.2 %collective-permute-start.6 = (s16[48,8,128]{2,1,0:T(8,128)(2,1)S(1)}, s16[48,8,128]{2,1,0:T(8,128)(2,1)S(1)}, u32[]{:S(2)}, u32[]{:S(2)}) collective-permute-start(s16[48,8,128]{2,1,0:T(8,128)(2,1)S(1)} %slice.121), channel_id=1, source_target_pairs={{0,48},{48,96},{96,144},{144,192},{192,240},{240,288},{288,336},{3... | collective-permute-start | bytes 294920 | tf_op jit(solution)/shard_map/ppermute | solution.py:589
  190.8 2.4 %shard_map.109.part_ref = f32[56,4096]{1,0:T(8,128)S(1)} custom-call(s16[48,16,128]{2,1,0:T(8,128)(2,1)S(1)} %all_to_all.28.refs_0_, bf16[224,384]{1,0:T(8,128)(2,1)S(1)} %get-tuple-element.48.take_ref.refs_1_, f32[56,14]{1,0:T(8,128)S(1)} %bitcast.116, f32[56,4096]{1,0:T(8,128)S(1)} %get-tuple-element.56.part_ref.refs_3_, ...), custom_call_target="tpu_custom_call" | custom-call | flops 13762560 | bytes 11010048 | tf_op jit(solution)/shard_map/pallas_call | solution.py:626
  193.2 1.6 collective-permute-done.7.high_ref
  194.9 1.7 shard_map.110
  (73 shorter events, 4.1 us)
Async XLA Ops:
  0.0 26.9 %copy-start = (s32[56,256]{1,0:T(8,128)S(1)}, s32[56,256]{1,0:T(8,128)}, u32[]{:S(2)}) copy-start(s32[56,256]{1,0:T(8,128)} %param.16) | copy-start | bytes 172036
  4.4 19.0 %copy-start.3 = (s32[6,56]{1,0:T(8,128)S(1)}, s32[6,56]{1,0:T(8,128)}, u32[]{:S(2)}) copy-start(s32[6,56]{1,0:T(8,128)} %param.19) | copy-start | bytes 4036
  4.5 19.7 %copy-start.4 = (s32[48]{0:T(128)S(1)}, s32[48]{0:T(128)}, u32[]{:S(2)}) copy-start(s32[48]{0:T(128)} %param.15) | copy-start | bytes 580
  4.5 21.0 %copy-start.5 = (f32[8]{0:T(128)S(1)}, f32[8]{0:T(128)}, u32[]{:S(2)}) copy-start(f32[8]{0:T(128)} %param.18) | copy-start | bytes 100
  4.5 21.0 %copy-start.6 = (s32[56]{0:T(128)S(1)}, s32[56]{0:T(128)}, u32[]{:S(2)}) copy-start(s32[56]{0:T(128)} %param.17) | copy-start | bytes 676
  4.5 71.6 %all-to-all-start = ((bf16[48,2,8192]{2,1,0:T(2,128)(2,1)}), bf16[48,2,8192]{2,1,0:T(2,128)(2,1)S(1)}, u32[]{:S(2)}, u32[]{:S(2)}) async-start(bf16[48,2,8192]{2,1,0:T(2,128)(2,1)} %shard_map.100), calls=%async_computation | async-start | bytes 3145728 | tf_op jit(solution)/shard_map/all_to_all | solution.py:514
  23.5 52.6 %copy-start.2 = (bf16[8,4096]{1,0:T(8,128)(2,1)S(1)}, bf16[8,4096]{1,0:T(8,128)(2,1)}, u32[]{:S(2)}) copy-start(bf16[8,4096]{1,0:T(8,128)(2,1)} %own_ref.2) | copy-start | bytes 196612
  30.9 76.4 %copy-start.1 = (bf16[8,4096]{1,0:T(8,128)(2,1)S(1)}, bf16[8,4096]{1,0:T(8,128)(2,1)}, u32[]{:S(2)}) copy-start(bf16[8,4096]{1,0:T(8,128)(2,1)} %own_ref.3) | copy-start | bytes 196612
  102.9 9.6 %collective-permute-start = (bf16[48,8,128]{2,1,0:T(8,128)(2,1)S(1)}, bf16[48,8,128]{2,1,0:T(8,128)(2,1)S(1)}, u32[]{:S(2)}, u32[]{:S(2)}) collective-permute-start(bf16[48,8,128]{2,1,0:T(8,128)(2,1)S(1)} %slice.118), channel_id=1, source_target_pairs={{0,48},{48,96},{96,144},{144,192},{192,240},{240,288},{288,336},{3... | collective-permute-start | bytes 294920 | tf_op jit(solution)/shard_map/ppermute | solution.py:589
  107.2 5.3 %collective-permute-start.1 = (bf16[48,8,128]{2,1,0:T(8,128)(2,1)S(1)}, bf16[48,8,128]{2,1,0:T(8,128)(2,1)S(1)}, u32[]{:S(2)}, u32[]{:S(2)}) collective-permute-start(bf16[48,8,128]{2,1,0:T(8,128)(2,1)S(1)} %slice.118), channel_id=1, source_target_pairs={{48,0},{96,48},{144,96},{192,144},{240,192},{288,240},{336,288},{3... | collective-permute-start | bytes 294920 | tf_op jit(solution)/shard_map/ppermute | solution.py:590
  131.0 8.0 %collective-permute-start.2 = (s16[48,8,128]{2,1,0:T(8,128)(2,1)S(1)}, s16[48,8,128]{2,1,0:T(8,128)(2,1)S(1)}, u32[]{:S(2)}, u32[]{:S(2)}) collective-permute-start(s16[48,8,128]{2,1,0:T(8,128)(2,1)S(1)} %slice.119), channel_id=1, source_target_pairs={{0,48},{48,96},{96,144},{144,192},{192,240},{240,288},{288,336},{3... | collective-permute-start | bytes 294920 | tf_op jit(solution)/shard_map/ppermute | solution.py:589
  136.0 4.2 %collective-permute-start.3 = (s16[48,8,128]{2,1,0:T(8,128)(2,1)S(1)}, s16[48,8,128]{2,1,0:T(8,128)(2,1)S(1)}, u32[]{:S(2)}, u32[]{:S(2)}) collective-permute-start(s16[48,8,128]{2,1,0:T(8,128)(2,1)S(1)} %slice.119), channel_id=1, source_target_pairs={{48,0},{96,48},{144,96},{192,144},{240,192},{288,240},{336,288},{3... | collective-permute-start | bytes 294920 | tf_op jit(solution)/shard_map/ppermute | solution.py:590
  160.1 6.3 %collective-permute-start.4 = (s16[48,8,128]{2,1,0:T(8,128)(2,1)S(1)}, s16[48,8,128]{2,1,0:T(8,128)(2,1)S(1)}, u32[]{:S(2)}, u32[]{:S(2)}) collective-permute-start(s16[48,8,128]{2,1,0:T(8,128)(2,1)S(1)} %slice.120), channel_id=1, source_target_pairs={{0,48},{48,96},{96,144},{144,192},{192,240},{240,288},{288,336},{3... | collective-permute-start | bytes 294920 | tf_op jit(solution)/shard_map/ppermute | solution.py:589
  163.4 4.0 %collective-permute-start.5 = (s16[48,8,128]{2,1,0:T(8,128)(2,1)S(1)}, s16[48,8,128]{2,1,0:T(8,128)(2,1)S(1)}, u32[]{:S(2)}, u32[]{:S(2)}) collective-permute-start(s16[48,8,128]{2,1,0:T(8,128)(2,1)S(1)} %slice.120), channel_id=1, source_target_pairs={{48,0},{96,48},{144,96},{192,144},{240,192},{288,240},{336,288},{3... | collective-permute-start | bytes 294920 | tf_op jit(solution)/shard_map/ppermute | solution.py:590
  186.7 6.6 %collective-permute-start.6 = (s16[48,8,128]{2,1,0:T(8,128)(2,1)S(1)}, s16[48,8,128]{2,1,0:T(8,128)(2,1)S(1)}, u32[]{:S(2)}, u32[]{:S(2)}) collective-permute-start(s16[48,8,128]{2,1,0:T(8,128)(2,1)S(1)} %slice.121), channel_id=1, source_target_pairs={{0,48},{48,96},{96,144},{144,192},{192,240},{240,288},{288,336},{3... | collective-permute-start | bytes 294920 | tf_op jit(solution)/shard_map/ppermute | solution.py:589
  190.8 4.0 %collective-permute-start.7 = (s16[48,8,128]{2,1,0:T(8,128)(2,1)S(1)}, s16[48,8,128]{2,1,0:T(8,128)(2,1)S(1)}, u32[]{:S(2)}, u32[]{:S(2)}) collective-permute-start(s16[48,8,128]{2,1,0:T(8,128)(2,1)S(1)} %slice.121), channel_id=1, source_target_pairs={{48,0},{96,48},{144,96},{192,144},{240,192},{288,240},{336,288},{3... | collective-permute-start | bytes 294920 | tf_op jit(solution)/shard_map/ppermute | solution.py:590

commit v3 on v2

--- a/solution.py
+++ b/solution.py
@@ -17,6 +17,10 @@
 DIRS = 4
 ROWS = DIRS * CAP
 CHUNKS = 4
+
+STEP = (2 * CAP, CAP)
+HALF = (CAP, 2 * CAP)
+PITCH = (ROWS // 2, ROWS)
 
 TAKE, INBOX, ORDER, RATE, JOINED, NEAR = 0, 4, 5, 6, 7, 8
 
@@ -164,16 +168,14 @@
     return rows.reshape(rows.shape[0] // ROWS, ROWS, LANES)
 
 
-def taken(matrix, message, coded):
-    rows = message.shape[0] * ROWS
+def taken(matrix, message, coded, first=0):
     if coded:
-        level = message.astype(jnp.int32).astype(jnp.float32).reshape(rows, LANES)
-        return decode(picked(matrix, level))
-    return jnp.dot(
-        matrix,
-        message.astype(jnp.float32).reshape(rows, LANES).astype(jnp.bfloat16),
-        preferred_element_type=jnp.float32,
-    )
+        message = message.astype(jnp.int32)
+    message = message.astype(jnp.float32)[:, first:, :]
+    message = message.reshape(message.shape[0] * message.shape[1], LANES)
+    if coded:
+        return decode(picked(matrix, message))
+    return jnp.dot(matrix, message.astype(jnp.bfloat16), preferred_element_type=jnp.float32)
 
 
 def as_codes(parts):
@@ -188,11 +190,15 @@
     lax.fori_loop(0, owned // SUB, step, 0)
 
 
-def pack_kernel(incoming, members, dest_ref, now_hbm, old_hbm, out_ref, held, arrived):
+def pack_kernel(
+    incoming, members, dest_hbm, now_hbm, old_hbm, out_ref, dest_ref, held, arrived
+):
     slots = dest_ref.shape[1]
     cells = now_hbm.shape[1]
     width = cells // CHUNKS
     copies = []
+    first = pltpu.make_async_copy(dest_hbm, dest_ref, arrived.at[2 * CHUNKS])
+    first.start()
     for chunk in range(CHUNKS):
         for index, ref in ((0, now_hbm), (1, old_hbm)):
             number = 2 * chunk + index
@@ -201,6 +207,7 @@
             )
             copy.start()
             copies.append(copy)
+    first.wait()
     dest = dest_ref[...]
     src = lax.broadcasted_iota(jnp.int32, (slots, slots), 1)
     other = lax.broadcasted_iota(jnp.int32, (slots, slots), 0)
@@ -315,7 +322,7 @@
     ghost_ref,
 ):
     owned = p_ref.shape[0]
-    ghost_ref[...] = taken(take_ref[...], here_ref[:, ROWS:, :], coded)
+    ghost_ref[...] = taken(take_ref[...], here_ref[...], coded, ROWS)
 
     def advance(group):
         rows = at_rows(0, group)
@@ -375,7 +382,7 @@
     settled(got_ref, own_ref, columns, 1, q_ref, q_ends_ref, count_ref)
     for ref, directions in ((take_y_ref, (2, 3)), (take_low_ref, (0,)), (take_high_ref, (1,))):
         numbers = [
-            columns[:, TAKE + d : TAKE + d + 1] + 2 * CAP * half
+            columns[:, TAKE + d : TAKE + d + 1] + HALF[d // 2] * half
             for half in range(2)
             for d in directions
         ]
@@ -500,14 +507,11 @@
     outgoing = pl.pallas_call(
         functools.partial(pack_kernel, incoming, members),
         out_shape=jax.ShapeDtypeStruct((members, CAP, 2 * cells), bf16),
-        in_specs=[
-            pl.BlockSpec(memory_space=pltpu.VMEM),
-            pl.BlockSpec(memory_space=pltpu.HBM),
-            pl.BlockSpec(memory_space=pltpu.HBM),
-        ],
+        in_specs=[pl.BlockSpec(memory_space=pltpu.HBM)] * 3,
         scratch_shapes=[
+            pltpu.VMEM((1, source_now.shape[0]), i32),
             pltpu.VMEM((2 * CHUNKS, source_now.shape[0], width), bf16),
-            pltpu.SemaphoreType.DMA((2 * CHUNKS,)),
+            pltpu.SemaphoreType.DMA((2 * CHUNKS + 1,)),
         ],
         compiler_params=pltpu.CompilerParams(vmem_limit_bytes=60 * 1024 * 1024),
     )(destination[None, :], source_now, source_old)
@@ -539,8 +543,8 @@
     for d in range(DIRS):
         order_out = rank_within(peer_dev[d], peer_slot[d], present[d])
         order_in = rank_within(peer_dev[d], slot_ids, present[d])
-        send_at.append(jnp.where(present[d], peer_dev[d] * ROWS + d % 2 * CAP + order_out, -ROWS))
-        take_at.append(jnp.where(present[d], peer_dev[d] * ROWS + (d + 1) % 2 * CAP + order_in, -ROWS))
+        send_at.append(jnp.where(present[d], peer_dev[d] * ROWS + d % 2 * STEP[d // 2] + order_out, -ROWS))
+        take_at.append(jnp.where(present[d], peer_dev[d] * PITCH[d // 2] + (d + 1) % 2 * (d // 2) * CAP + order_in, -ROWS))
     rates = jnp.sum(
         jnp.where(admit_class[:, None] == class_ids[None, :], admittance[None, :], 0.0), axis=1
     )
@@ -552,8 +556,8 @@
     )
     table = jnp.sum(jnp.where(order_is[None], table[:, None, :], 0.0), axis=2)
     columns = table[DIRS:].T
-    halved = jnp.arange(2, dtype=i32).astype(f32) * (2 * CAP)
-    send_at = (table[:DIRS].reshape(2, 1, 2, owned) + halved[None, :, None, None]).reshape(2, -1)
+    halved = jnp.arange(2, dtype=i32).astype(f32)[None, :] * jnp.array(HALF, f32)[:, None]
+    send_at = (table[:DIRS].reshape(2, 1, 2, owned) + halved[:, :, None, None]).reshape(2, -1)
     place = position[:, None].astype(f32)
     heights = floor_height[order].astype(f32)
 
@@ -585,9 +589,10 @@
     for sweep in range(ITERS):
         coded = sweep > 0
         here = lax.all_to_all(outbox, "dom", split_axis=0, concat_axis=0, tiled=True)
-        across_x = lax.slice_in_dim(here, 0, ROWS, axis=1)
-        from_low = lax.ppermute(across_x, "slab", [(i, (i + 1) % slabs) for i in range(slabs)])
-        from_high = lax.ppermute(across_x, "slab", [((i + 1) % slabs, i) for i in range(slabs)])
+        down = lax.slice_in_dim(here, 0, ROWS // 2, axis=1)
+        up = lax.slice_in_dim(here, ROWS // 2, ROWS, axis=1)
+        from_low = lax.ppermute(up, "slab", [(i, (i + 1) % slabs) for i in range(slabs)])
+        from_high = lax.ppermute(down, "slab", [((i + 1) % slabs, i) for i in range(slabs)])
         if sweep == 0:
             part, faces, *lagging, take_y, take_low, take_high, send_x, send_y, keep, gain, lag = (
                 pl.pallas_call(
@@ -595,8 +600,8 @@
                     out_shape=[grid_shape, jax.ShapeDtypeStruct(faces_shape, f32)]
                     + [grid_shape, ends_shape]
                     + [
-                        jax.ShapeDtypeStruct((number, message_rows), bf16)
-                        for number in (4 * owned, 2 * owned, 2 * owned)
+                        jax.ShapeDtypeStruct((number * owned, message_rows // share), bf16)
+                        for number, share in ((4, 1), (2, 2), (2, 2))
                     ]
                     + [jax.ShapeDtypeStruct((message_rows, 4 * owned), bf16)] * 2
                     + [grid_shape] * 3,

time: 197 us -> 195 us (0.990)
  no operation moved by 1% of the time
where the time goes in v3:
time: 195 us
  blocking collectives  78 us (40%)
  waiting for transfers between devices  47.4 us (24%)
  starting transfers between devices  37.5 us (19%)
  Pallas kernels  26.4 us (14%)
  other arithmetic  2.61 us (1%)
    all_to_all x4, blocking collectives, on_device(): lax.all_to_all(outbox, 'dom', split_axis=0, concat_axis=0, tiled=True)  78 us
    all_to_all x1, waiting for transfers between devices, on_device(): lax.all_to_all(outgoing, 'dom', split_axis=0, concat_axis=0, tiled=True)  45.3 us
    all_to_all x1, starting transfers between devices, on_device(): lax.all_to_all(outgoing, 'dom', split_axis=0, concat_axis=0, tiled=True)  19 us
    ppermute x4, starting transfers between devices, on_device(): lax.ppermute(up, 'slab', [(i, (i + 1) % slabs) for i in range(slabs)])  18.6 us
    pallas_call x2, Pallas kernels, on_device(): pl.pallas_call(functools.partial(inner_kernel, coded, False), out_shape=[...  6.12 us
    pallas_call x1, Pallas kernels, on_device(): pl.pallas_call(first_inner_kernel, out_shape=[grid_shape, jax.ShapeDtypeS...  5.25 us
  transfers between devices with their start and end apart: 9, of which 4 were waited for; matrix products, arithmetic and copies ran while one was open for 2% of the time, Pallas kernels for 8%

profile of v3, /device:TPU:1, one launch (start us, length us, event | category | flops | bytes accessed | tf_op | source)
XLA Modules:
  0.0 194.6 jit_solution(9394713656961095669)
XLA Ops:
  0.0 3.8 %shard_map.109 = bf16[48,2,8192]{2,1,0:T(2,128)(2,1)} custom-call(s32[1,96]{1,0:T(1,128)} %bitcast.119, bf16[96,4096]{1,0:T(8,128)(2,1)} %now_hbm.1, bf16[96,4096]{1,0:T(8,128)(2,1)} %old_hbm.1), custom_call_target="tpu_custom_call" | custom-call | tf_op jit(solution)/shard_map/pallas_call | solution.py:507
  3.9 19.0 %all-to-all-start = ((bf16[48,2,8192]{2,1,0:T(2,128)(2,1)}), bf16[48,2,8192]{2,1,0:T(2,128)(2,1)S(1)}, u32[]{:S(2)}, u32[]{:S(2)}) async-start(bf16[48,2,8192]{2,1,0:T(2,128)(2,1)} %shard_map.109), calls=%async_computation | async-start | bytes 3145728 | tf_op jit(solution)/shard_map/all_to_all | solution.py:518
  22.9 0.6 convert_reduce_fusion.12
  26.3 0.6 gather_fusion
  27.7 2.5 %shard_map.110.count_ref = f32[56,4096]{1,0:T(8,128)S(1)} custom-call(f32[56,256]{1,0:T(8,128)S(1)} %convert_element_type.135.height_ref, f32[56,14]{1,0:T(8,128)S(1)} %bitcast.111), custom_call_target="tpu_custom_call" | custom-call | tf_op jit(solution)/shard_map/pallas_call | solution.py:565
  30.2 45.3 %all-to-all-done.got_ref = bf16[48,2,8192]{2,1,0:T(2,128)(2,1)S(1)} async-done(((bf16[48,2,8192]{2,1,0:T(2,128)(2,1)}), bf16[48,2,8192]{2,1,0:T(2,128)(2,1)S(1)}, u32[]{:S(2)}, u32[]{:S(2)}) %all-to-all-start) | async-done | bytes 1572896 | tf_op jit(solution)/shard_map/all_to_all | solution.py:518
  75.5 1.4 shard_map.111
  76.9 25.4 %all_to_all.25.here_ref = bf16[48,16,128]{2,1,0:T(8,128)(2,1)S(1)} all-to-all(bf16[48,16,128]{2,1,0:T(8,128)(2,1)S(1)} %get-tuple-element.37), channel_id=1, replica_groups=mesh['slab'=16,'dom'=48] {'dom'}, dimensions={0} | all-to-all | bytes 393216 | tf_op jit(solution)/shard_map/all_to_all | solution.py:591
  102.3 4.3 %collective-permute-start = (bf16[48,4,128]{2,1,0:T(4,128)(2,1)S(1)}, bf16[48,4,128]{2,1,0:T(4,128)(2,1)S(1)}, u32[]{:S(2)}, u32[]{:S(2)}) collective-permute-start(bf16[48,4,128]{2,1,0:T(4,128)(2,1)S(1)} %get-tuple-element.78), channel_id=1, source_target_pairs={{0,48},{48,96},{96,144},{144,192},{192,240},{240,288},{288,336},{3... | collective-permute-start | bytes 147464 | tf_op jit(solution)/shard_map/ppermute | solution.py:594
  106.6 5.3 %shard_map.112 = (f32[56,4096]{1,0:T(8,128)S(1)}, f32[224,128]{1,0:T(8,128)S(1)}, f32[56,4096]{1,0:T(8,128)}, f32[56,512]{1,0:T(8,128)}, bf16[224,384]{1,0:T(8,1...) custom-call(bf16[48,16,128]{2,1,0:T(8,128)(2,1)S(1)} %all_to_all.25., ...), custom_call_target="tpu_custom_call" | custom-call | flops 13762560 | bytes 11010048 | tf_op jit(solution)/shard_map/pallas_call | solution.py:598
  111.9 1.1 shard_map.113
  113.0 17.4 %all_to_all.26.here_ref = s16[48,16,128]{2,1,0:T(8,128)(2,1)S(1)} all-to-all(s16[48,16,128]{2,1,0:T(8,128)(2,1)S(1)} %get-tuple-element.47), channel_id=1, replica_groups=mesh['slab'=16,'dom'=48] {'dom'}, dimensions={0} | all-to-all | bytes 393216 | tf_op jit(solution)/shard_map/all_to_all | solution.py:591
  130.4 4.9 %collective-permute-start.2 = (s16[48,4,128]{2,1,0:T(4,128)(2,1)S(1)}, s16[48,4,128]{2,1,0:T(4,128)(2,1)S(1)}, u32[]{:S(2)}, u32[]{:S(2)}) collective-permute-start(s16[48,4,128]{2,1,0:T(4,128)(2,1)S(1)} %get-tuple-element.76), channel_id=1, source_target_pairs={{0,48},{48,96},{96,144},{144,192},{192,240},{240,288},{288,336},{3... | collective-permute-start | bytes 147464 | tf_op jit(solution)/shard_map/ppermute | solution.py:594
  135.4 3.1 %shard_map.114 = (f32[56,4096]{1,0:T(8,128)S(1)}, f32[224,128]{1,0:T(8,128)S(1)}) custom-call(s16[48,16,128]{2,1,0:T(8,128)(2,1)S(1)} %all_to_all.26.here_ref, bf16[224,384]{1,0:T(8,128)(2,1)S(1)} %get-tuple-element.48.take_ref.refs_1_, f32[56,14]{1,0:T(8,128)S(1)} %bitcast.114, f32[56,4096]{1,0:T(8,128)S(1)} %get-tuple-element.43.part_ref.p_ref.q_ref, ...), custom_call_target="tpu_custom_call" | custom-call | flops 13762560 | bytes 11010048 | tf_op jit(solution)/shard_map/pallas_call | solution.py:616
  139.0 1.1 shard_map.115
  140.1 18.3 %all_to_all.27.here_ref = s16[48,16,128]{2,1,0:T(8,128)(2,1)S(1)} all-to-all(s16[48,16,128]{2,1,0:T(8,128)(2,1)S(1)} %get-tuple-element.54), channel_id=1, replica_groups=mesh['slab'=16,'dom'=48] {'dom'}, dimensions={0} | all-to-all | bytes 393216 | tf_op jit(solution)/shard_map/all_to_all | solution.py:591
  158.5 4.0 %collective-permute-start.4 = (s16[48,4,128]{2,1,0:T(4,128)(2,1)S(1)}, s16[48,4,128]{2,1,0:T(4,128)(2,1)S(1)}, u32[]{:S(2)}, u32[]{:S(2)}) collective-permute-start(s16[48,4,128]{2,1,0:T(4,128)(2,1)S(1)} %get-tuple-element.74), channel_id=1, source_target_pairs={{0,48},{48,96},{96,144},{144,192},{192,240},{240,288},{288,336},{3... | collective-permute-start | bytes 147464 | tf_op jit(solution)/shard_map/ppermute | solution.py:594
  162.5 3.1 %shard_map.116 = (f32[56,4096]{1,0:T(8,128)S(1)}, f32[224,128]{1,0:T(8,128)S(1)}) custom-call(s16[48,16,128]{2,1,0:T(8,128)(2,1)S(1)} %all_to_all.27.here_ref, bf16[224,384]{1,0:T(8,128)(2,1)S(1)} %get-tuple-element.48.take_ref.refs_1_, f32[56,14]{1,0:T(8,128)S(1)} %bitcast.115, f32[56,4096]{1,0:T(8,128)S(1)} %get-tuple-element.52.part_ref.p_ref.refs_5_, ...), custom_call_target="tpu_custom_call" | custom-call | flops 13762560 | bytes 11010048 | tf_op jit(solution)/shard_map/pallas_call | solution.py:616
  166.0 1.1 shard_map.117
  167.2 16.9 %all_to_all.28.refs_0_ = s16[48,16,128]{2,1,0:T(8,128)(2,1)S(1)} all-to-all(s16[48,16,128]{2,1,0:T(8,128)(2,1)S(1)} %get-tuple-element.58), channel_id=1, replica_groups=mesh['slab'=16,'dom'=48] {'dom'}, dimensions={0} | all-to-all | bytes 393216 | tf_op jit(solution)/shard_map/all_to_all | solution.py:591
  184.1 5.3 %collective-permute-start.6 = (s16[48,4,128]{2,1,0:T(4,128)(2,1)S(1)}, s16[48,4,128]{2,1,0:T(4,128)(2,1)S(1)}, u32[]{:S(2)}, u32[]{:S(2)}) collective-permute-start(s16[48,4,128]{2,1,0:T(4,128)(2,1)S(1)} %get-tuple-element.72), channel_id=1, source_target_pairs={{0,48},{48,96},{96,144},{144,192},{192,240},{240,288},{288,336},{3... | collective-permute-start | bytes 147464 | tf_op jit(solution)/shard_map/ppermute | solution.py:594
  189.4 2.4 %shard_map.118.part_ref = f32[56,4096]{1,0:T(8,128)S(1)} custom-call(s16[48,16,128]{2,1,0:T(8,128)(2,1)S(1)} %all_to_all.28.refs_0_, bf16[224,384]{1,0:T(8,128)(2,1)S(1)} %get-tuple-element.48.take_ref.refs_1_, f32[56,14]{1,0:T(8,128)S(1)} %bitcast.116, f32[56,4096]{1,0:T(8,128)S(1)} %get-tuple-element.56.part_ref.refs_3_, ...), custom_call_target="tpu_custom_call" | custom-call | flops 13762560 | bytes 11010048 | tf_op jit(solution)/shard_map/pallas_call | solution.py:631
  191.8 1.1 collective-permute-done.7.high_ref
  192.9 1.7 shard_map.119
  (73 shorter events, 4.0 us)
Async XLA Ops:
  0.0 26.3 %copy-start = (s32[56,256]{1,0:T(8,128)S(1)}, s32[56,256]{1,0:T(8,128)}, u32[]{:S(2)}) copy-start(s32[56,256]{1,0:T(8,128)} %param.17) | copy-start | bytes 172036
  3.8 19.1 %copy-start.3 = (s32[6,56]{1,0:T(8,128)S(1)}, s32[6,56]{1,0:T(8,128)}, u32[]{:S(2)}) copy-start(s32[6,56]{1,0:T(8,128)} %param.20) | copy-start | bytes 4036
  3.8 19.7 %copy-start.4 = (s32[48]{0:T(128)S(1)}, s32[48]{0:T(128)}, u32[]{:S(2)}) copy-start(s32[48]{0:T(128)} %param.16) | copy-start | bytes 580
  3.8 21.0 %copy-start.6 = (f32[8]{0:T(128)S(1)}, f32[8]{0:T(128)}, u32[]{:S(2)}) copy-start(f32[8]{0:T(128)} %param.19) | copy-start | bytes 100
  3.8 21.0 %copy-start.7 = (s32[56]{0:T(128)S(1)}, s32[56]{0:T(128)}, u32[]{:S(2)}) copy-start(s32[56]{0:T(128)} %param.18) | copy-start | bytes 676
  3.8 23.1 %copy-start.5 = (f32[2]{0:T(128)S(1)}, f32[2]{0:T(128)}, u32[]{:S(2)}) copy-start(f32[2]{0:T(128)} %constant.49.clone) | copy-start | bytes 28
  3.9 71.6 %all-to-all-start = ((bf16[48,2,8192]{2,1,0:T(2,128)(2,1)}), bf16[48,2,8192]{2,1,0:T(2,128)(2,1)S(1)}, u32[]{:S(2)}, u32[]{:S(2)}) async-start(bf16[48,2,8192]{2,1,0:T(2,128)(2,1)} %shard_map.109), calls=%async_computation | async-start | bytes 3145728 | tf_op jit(solution)/shard_map/all_to_all | solution.py:518
  22.9 52.6 %copy-start.2 = (bf16[8,4096]{1,0:T(8,128)(2,1)S(1)}, bf16[8,4096]{1,0:T(8,128)(2,1)}, u32[]{:S(2)}) copy-start(bf16[8,4096]{1,0:T(8,128)(2,1)} %own_ref.2) | copy-start | bytes 196612
  30.2 76.4 %copy-start.1 = (bf16[8,4096]{1,0:T(8,128)(2,1)S(1)}, bf16[8,4096]{1,0:T(8,128)(2,1)}, u32[]{:S(2)}) copy-start(bf16[8,4096]{1,0:T(8,128)(2,1)} %own_ref.3) | copy-start | bytes 196612
  102.3 9.6 %collective-permute-start = (bf16[48,4,128]{2,1,0:T(4,128)(2,1)S(1)}, bf16[48,4,128]{2,1,0:T(4,128)(2,1)S(1)}, u32[]{:S(2)}, u32[]{:S(2)}) collective-permute-start(bf16[48,4,128]{2,1,0:T(4,128)(2,1)S(1)} %get-tuple-element.78), channel_id=1, source_target_pairs={{0,48},{48,96},{96,144},{144,192},{192,240},{240,288},{288,336},{3... | collective-permute-start | bytes 147464 | tf_op jit(solution)/shard_map/ppermute | solution.py:594
  106.6 5.3 %collective-permute-start.1 = (bf16[48,4,128]{2,1,0:T(4,128)(2,1)S(1)}, bf16[48,4,128]{2,1,0:T(4,128)(2,1)S(1)}, u32[]{:S(2)}, u32[]{:S(2)}) collective-permute-start(bf16[48,4,128]{2,1,0:T(4,128)(2,1)S(1)} %get-tuple-element.77), channel_id=1, source_target_pairs={{48,0},{96,48},{144,96},{192,144},{240,192},{288,240},{336,288},{3... | collective-permute-start | bytes 147464 | tf_op jit(solution)/shard_map/ppermute | solution.py:595
  130.4 8.0 %collective-permute-start.2 = (s16[48,4,128]{2,1,0:T(4,128)(2,1)S(1)}, s16[48,4,128]{2,1,0:T(4,128)(2,1)S(1)}, u32[]{:S(2)}, u32[]{:S(2)}) collective-permute-start(s16[48,4,128]{2,1,0:T(4,128)(2,1)S(1)} %get-tuple-element.76), channel_id=1, source_target_pairs={{0,48},{48,96},{96,144},{144,192},{192,240},{240,288},{288,336},{3... | collective-permute-start | bytes 147464 | tf_op jit(solution)/shard_map/ppermute | solution.py:594
  135.4 3.6 %collective-permute-start.3 = (s16[48,4,128]{2,1,0:T(4,128)(2,1)S(1)}, s16[48,4,128]{2,1,0:T(4,128)(2,1)S(1)}, u32[]{:S(2)}, u32[]{:S(2)}) collective-permute-start(s16[48,4,128]{2,1,0:T(4,128)(2,1)S(1)} %get-tuple-element.75), channel_id=1, source_target_pairs={{48,0},{96,48},{144,96},{192,144},{240,192},{288,240},{336,288},{3... | collective-permute-start | bytes 147464 | tf_op jit(solution)/shard_map/ppermute | solution.py:595
  158.5 7.1 %collective-permute-start.4 = (s16[48,4,128]{2,1,0:T(4,128)(2,1)S(1)}, s16[48,4,128]{2,1,0:T(4,128)(2,1)S(1)}, u32[]{:S(2)}, u32[]{:S(2)}) collective-permute-start(s16[48,4,128]{2,1,0:T(4,128)(2,1)S(1)} %get-tuple-element.74), channel_id=1, source_target_pairs={{0,48},{48,96},{96,144},{144,192},{192,240},{240,288},{288,336},{3... | collective-permute-start | bytes 147464 | tf_op jit(solution)/shard_map/ppermute | solution.py:594
  162.5 3.5 %collective-permute-start.5 = (s16[48,4,128]{2,1,0:T(4,128)(2,1)S(1)}, s16[48,4,128]{2,1,0:T(4,128)(2,1)S(1)}, u32[]{:S(2)}, u32[]{:S(2)}) collective-permute-start(s16[48,4,128]{2,1,0:T(4,128)(2,1)S(1)} %get-tuple-element.73), channel_id=1, source_target_pairs={{48,0},{96,48},{144,96},{192,144},{240,192},{288,240},{336,288},{3... | collective-permute-start | bytes 147464 | tf_op jit(solution)/shard_map/ppermute | solution.py:595
  184.1 7.7 %collective-permute-start.6 = (s16[48,4,128]{2,1,0:T(4,128)(2,1)S(1)}, s16[48,4,128]{2,1,0:T(4,128)(2,1)S(1)}, u32[]{:S(2)}, u32[]{:S(2)}) collective-permute-start(s16[48,4,128]{2,1,0:T(4,128)(2,1)S(1)} %get-tuple-element.72), channel_id=1, source_target_pairs={{0,48},{48,96},{96,144},{144,192},{192,240},{240,288},{288,336},{3... | collective-permute-start | bytes 147464 | tf_op jit(solution)/shard_map/ppermute | solution.py:594
  189.4 3.5 %collective-permute-start.7 = (s16[48,4,128]{2,1,0:T(4,128)(2,1)S(1)}, s16[48,4,128]{2,1,0:T(4,128)(2,1)S(1)}, u32[]{:S(2)}, u32[]{:S(2)}) collective-permute-start(s16[48,4,128]{2,1,0:T(4,128)(2,1)S(1)} %get-tuple-element.71), channel_id=1, source_target_pairs={{48,0},{96,48},{144,96},{192,144},{240,192},{288,240},{336,288},{3... | collective-permute-start | bytes 147464 | tf_op jit(solution)/shard_map/ppermute | solution.py:595

commit v4 on v3

--- a/solution.py
+++ b/solution.py
@@ -1,4 +1,5 @@
 import functools
+import math
 
 import jax
 import jax.numpy as jnp
@@ -22,13 +23,16 @@
 HALF = (CAP, 2 * CAP)
 PITCH = (ROWS // 2, ROWS)
 
-TAKE, INBOX, ORDER, RATE, JOINED, NEAR = 0, 4, 5, 6, 7, 8
+TAKE, INBOX, ORDER, RATE, WEIGHT, JOINED, NEAR = 0, 4, 5, 6, 7, 8, 9
 
 courant_sq = 0.3
 courant = 0.3**0.5
 
 OCTAVE = 1024.0
-LOWEST = 23.5
+
+
+def lowest(steps):
+    return 32767.0 / OCTAVE - 0.01 - math.log2(6.0 * 3.0**steps)
 
 VMEM = pltpu.CompilerParams(vmem_limit_bytes=16 * 1024 * 1024)
 
@@ -42,15 +46,15 @@
     return jnp.sum(earlier.astype(jnp.int32), axis=1)
 
 
-def encode(values):
+def encode(values, low):
     size = jnp.abs(values)
-    level = jnp.floor((jnp.log2(jnp.maximum(size, 1e-30)) + LOWEST) * OCTAVE + 0.5)
+    level = jnp.floor((jnp.log2(jnp.maximum(size, 1e-30)) + low) * OCTAVE + 0.5)
     level = jnp.clip(level, 0.0, 32767.0)
     return jnp.where(values < 0.0, -level, level)
 
 
-def decode(level):
-    size = jnp.exp2(jnp.abs(level) * (1.0 / OCTAVE) - LOWEST)
+def decode(level, low):
+    size = jnp.exp2(jnp.abs(level) * (1.0 / OCTAVE) - low)
     return jnp.where(level > 0.0, size, jnp.where(level < 0.0, -size, 0.0))
 
 
@@ -85,16 +89,16 @@
         self.odd = row % 2 == 1
         self.strip = lane // EDGE
         upper = jnp.where(self.odd, 1.0, 0.0)
-        self.joined_down = joined * upper
-        self.joined_up = joined * (1.0 - upper)
+        self.partner = joined * jnp.where(
+            self.bottom, upper, jnp.where(self.top, 1.0 - upper, 0.0)
+        )
 
     def along_z(self, block):
-        partner = jnp.where(self.odd, turn(block, 1, 0), turn(block, -1, 0))
-        below = jnp.where(
-            self.bottom, turn(partner, 1 - EDGE) * self.joined_down, turn(block, 1)
-        )
-        above = jnp.where(self.top, turn(partner, EDGE - 1) * self.joined_up, turn(block, -1))
-        return below + above
+        given = jnp.where(self.odd, turn(block, EDGE - 1), turn(block, 1 - EDGE))
+        across = jnp.where(self.odd, turn(given, 1, 0), turn(given, -1, 0))
+        below = jnp.where(self.bottom, 0.0, turn(block, 1))
+        above = jnp.where(self.top, 0.0, turn(block, -1))
+        return (below + above) + across * self.partner
 
     def total(self, plane, x, ghost_x, ghost_y):
         first, second = plane(x)
@@ -160,7 +164,7 @@
 
 def placed(matrix, faces, coded):
     if coded:
-        rows = picked(matrix, encode(faces))
+        rows = picked(matrix, encode(faces, lowest(coded)))
     else:
         rows = jnp.dot(
             matrix, faces.astype(jnp.bfloat16), preferred_element_type=jnp.float32
@@ -174,7 +178,7 @@
     message = message.astype(jnp.float32)[:, first:, :]
     message = message.reshape(message.shape[0] * message.shape[1], LANES)
     if coded:
-        return decode(picked(matrix, message))
+        return decode(picked(matrix, message), lowest(coded))
     return jnp.dot(matrix, message.astype(jnp.bfloat16), preferred_element_type=jnp.float32)
 
 
@@ -228,7 +232,7 @@
         )
 
 
-def prepare_kernel(height_ref, column_ref, count_ref, mask_ref):
+def prepare_kernel(height_ref, column_ref, share_ref, mask_ref):
     owned = height_ref.shape[0]
     row = lax.broadcasted_iota(jnp.int32, (FACE, FACE), 0)
     column = lax.broadcasted_iota(jnp.int32, (FACE, FACE), 1)
@@ -246,6 +250,7 @@
             jnp.broadcast_to(columns[:, at : at + 1], (SUB, LANES))
             for at in range(NEAR, NEAR + 6)
         ]
+        rate = jnp.broadcast_to(columns[:, RATE : RATE + 1], (SUB, LANES))
         grid = Grid(near[4] + near[5])
         for x in range(EDGE):
             total = grid.total(
@@ -257,12 +262,13 @@
             air = pieces(mask_ref, rows, x)
             for half in range(2):
                 at = slice(x * FACE + half * LANES, x * FACE + (half + 1) * LANES)
-                count_ref[rows, at] = jnp.where(air[half] > 0.0, total[half], -1.0)
+                damping = courant * (6.0 - total[half]) * rate / 2.0
+                share_ref[rows, at] = air[half] / (1.0 + damping)
 
     groups(owned, count)
 
 
-def settled(got_ref, own_ref, columns, index, to_ref, ends_ref, count_ref):
+def settled(got_ref, own_ref, columns, index, to_ref, ends_ref, share_ref):
     owned, cells = to_ref.shape
     members = got_ref.shape[0]
     width = cells // CHUNKS
@@ -277,17 +283,17 @@
             preferred_element_type=jnp.float32,
         )
         rows = rows + jnp.dot(stay, own_ref[:, at], preferred_element_type=jnp.float32)
-        to_ref[:, at] = jnp.where(count_ref[:, at] >= 0.0, rows, 0.0)
+        to_ref[:, at] = jnp.where(share_ref[:, at] > 0.0, rows, 0.0)
     ends_ref[:, :FACE] = to_ref[:, :FACE]
     ends_ref[:, FACE:] = to_ref[:, cells - FACE :]
 
 
 def begin_kernel(
-    got_ref, own_ref, count_ref, column_ref, send_at_ref, p_ref, ends_ref, out_ref, x_ref, y_ref
+    got_ref, own_ref, share_ref, column_ref, send_at_ref, p_ref, ends_ref, out_ref, x_ref, y_ref
 ):
     members = got_ref.shape[0]
     owned = p_ref.shape[0]
-    settled(got_ref, own_ref, column_ref[...], 0, p_ref, ends_ref, count_ref)
+    settled(got_ref, own_ref, column_ref[...], 0, p_ref, ends_ref, share_ref)
     grid = Grid(jnp.ones((SUB, LANES), jnp.float32))
 
     def faces(group):
@@ -298,7 +304,7 @@
     groups(owned, faces)
     shape = (members * ROWS, 4 * owned)
     parts = [
-        placed(one_hot(send_at_ref[index : index + 1, :], shape, 0), ref[...], False)
+        placed(one_hot(send_at_ref[index : index + 1, :], shape, 0), ref[...], 0)
         for index, ref in enumerate((x_ref, y_ref))
     ]
     out_ref[...] = jnp.concatenate(parts, axis=1).astype(jnp.bfloat16)
@@ -314,9 +320,7 @@
     p_ends_ref,
     q_ref,
     q_ends_ref,
-    keep_ref,
-    gain_ref,
-    lag_ref,
+    share_ref,
     new_ref,
     y_ref,
     ghost_ref,
@@ -327,6 +331,8 @@
     def advance(group):
         rows = at_rows(0, group)
         grid = Grid(jnp.broadcast_to(column_ref[rows, JOINED : JOINED + 1], (SUB, LANES)))
+        weight = jnp.broadcast_to(column_ref[rows, WEIGHT : WEIGHT + 1], (SUB, LANES))
+        inward = (2.0 - 6.0 * courant_sq) - weight
         low, high = (
             [ghost_ref[at_rows((2 * half + d) * owned, group), :] for half in range(2)]
             for d in range(2)
@@ -340,13 +346,11 @@
             total = grid.total(lambda at: plane(p_ref, p_ends_ref, rows, at), x, None, ghost_y)
             state = plane(p_ref, p_ends_ref, rows, x)
             lagging = plane(q_ref, q_ends_ref, rows, x)
-            keep = pieces(keep_ref, rows, x)
-            gain = pieces(gain_ref, rows, x)
-            lag = pieces(lag_ref, rows, x)
+            share = pieces(share_ref, rows, x)
             for h in range(2):
-                new_ref[rows, x * FACE + h * LANES : x * FACE + (h + 1) * LANES] = (
-                    keep[h] * state[h] + gain[h] * total[h] - lag[h] * lagging[h]
-                )
+                new_ref[rows, x * FACE + h * LANES : x * FACE + (h + 1) * LANES] = share[h] * (
+                    inward * state[h] + courant_sq * total[h] - 2.0 * lagging[h]
+                ) + (lagging[h] + weight * state[h])
 
     groups(owned, advance)
     if not last:
@@ -360,7 +364,7 @@
     send_at_ref,
     got_ref,
     own_ref,
-    count_ref,
+    share_ref,
     p_ref,
     p_ends_ref,
     part_ref,
@@ -372,14 +376,11 @@
     take_high_ref,
     send_x_ref,
     send_y_ref,
-    keep_ref,
-    gain_ref,
-    lag_ref,
     ghost_ref,
 ):
     owned = p_ref.shape[0]
     columns = column_ref[...]
-    settled(got_ref, own_ref, columns, 1, q_ref, q_ends_ref, count_ref)
+    settled(got_ref, own_ref, columns, 1, q_ref, q_ends_ref, share_ref)
     for ref, directions in ((take_y_ref, (2, 3)), (take_low_ref, (0,)), (take_high_ref, (1,))):
         numbers = [
             columns[:, TAKE + d : TAKE + d + 1] + HALF[d // 2] * half
@@ -390,28 +391,14 @@
     for index, ref in enumerate((send_x_ref, send_y_ref)):
         ref[...] = one_hot(send_at_ref[index : index + 1, :], ref.shape, 0)
 
-    def fields(group):
-        rows = at_rows(0, group)
-        rate = jnp.broadcast_to(column_ref[rows, RATE : RATE + 1], (SUB, LANES))
-        for x in range(EDGE):
-            for half, opened in enumerate(pieces(count_ref, rows, x)):
-                air = jnp.where(opened >= 0.0, 1.0, 0.0)
-                damping = courant * (6.0 - opened) * rate / 2.0
-                share = air / (1.0 + damping)
-                at = slice(x * FACE + half * LANES, x * FACE + (half + 1) * LANES)
-                keep_ref[rows, at] = (2.0 - opened * courant_sq) * share
-                gain_ref[rows, at] = courant_sq * share
-                lag_ref[rows, at] = (1.0 - damping) * share
-
-    groups(owned, fields)
     inner_kernel(
-        False, False, here_ref, take_y_ref, column_ref, p_ref, p_ends_ref, q_ref, q_ends_ref,
-        keep_ref, gain_ref, lag_ref, part_ref, y_ref, ghost_ref,
+        0, False, here_ref, take_y_ref, column_ref, p_ref, p_ends_ref, q_ref, q_ends_ref,
+        share_ref, part_ref, y_ref, ghost_ref,
     )
 
 
 def last_inner_kernel(*refs):
-    inner_kernel(True, True, *refs[:-1], None, refs[-1])
+    inner_kernel(ITERS - 1, True, *refs[:-1], None, refs[-1])
 
 
 def outer_kernel(
@@ -421,7 +408,7 @@
     high_ref,
     take_low_ref,
     take_high_ref,
-    gain_ref,
+    share_ref,
     part_ref,
     y_ref,
     send_x_ref,
@@ -444,9 +431,9 @@
         rows = at_rows(0, group)
         for x, ghost in ((0, ghost_low), (EDGE - 1, ghost_high)):
             part = pieces(part_ref, rows, x)
-            gain = pieces(gain_ref, rows, x)
+            share = pieces(share_ref, rows, x)
             done = [
-                part[h] + gain[h] * ghost[at_rows(h * owned, group), :] for h in range(2)
+                part[h] + courant_sq * share[h] * ghost[at_rows(h * owned, group), :] for h in range(2)
             ]
             for h in range(2):
                 at = (FACE if x else 0) + h * LANES
@@ -465,15 +452,18 @@
     groups(owned, finish)
     if not last:
         out_ref[...] = as_codes(
-            [placed(send_x_ref[...], x_ref[...], True), placed(send_y_ref[...], y_out[...], True)]
+            [
+                placed(send_x_ref[...], x_ref[...], coded + 1),
+                placed(send_y_ref[...], y_out[...], coded + 1),
+            ]
         )
 
 
 def last_outer_kernel(
-    low_ref, high_ref, take_low_ref, take_high_ref, gain_ref, part_ref, place_ref, out_ref, a, b, ends
+    low_ref, high_ref, take_low_ref, take_high_ref, share_ref, part_ref, place_ref, out_ref, a, b, ends
 ):
     outer_kernel(
-        True, True, low_ref, high_ref, take_low_ref, take_high_ref, gain_ref, part_ref,
+        ITERS - 1, True, low_ref, high_ref, take_low_ref, take_high_ref, share_ref, part_ref,
         None, None, None, ends, None, a, b, None, None,
     )
     owned, cells = part_ref.shape
@@ -551,7 +541,7 @@
     near = [present[d].astype(f32) for d in range(6)]
     table = jnp.stack(
         [number.astype(f32) for number in send_at + take_at + [inbox, slot_ids]]
-        + [rates, near[4] + near[5]]
+        + [rates, 2.0 * courant_sq / (courant * rates), near[4] + near[5]]
         + near
     )
     table = jnp.sum(jnp.where(order_is[None], table[:, None, :], 0.0), axis=2)
@@ -562,14 +552,14 @@
     heights = floor_height[order].astype(f32)
 
     grid_shape = jax.ShapeDtypeStruct((owned, cells), f32)
-    count = pl.pallas_call(
+    share = pl.pallas_call(
         prepare_kernel,
         out_shape=grid_shape,
         scratch_shapes=[pltpu.VMEM((owned, cells), f32)],
         compiler_params=VMEM,
     )(heights, columns)
-    got, count, columns, send_at, place = lax.optimization_barrier(
-        (got, count, columns, send_at, place)
+    got, share, columns, send_at, place = lax.optimization_barrier(
+        (got, share, columns, send_at, place)
     )
 
     message = (members, 2 * ROWS, LANES)
@@ -583,18 +573,17 @@
         out_shape=[grid_shape, ends_shape, jax.ShapeDtypeStruct(message, bf16)],
         scratch_shapes=[faces_scratch, faces_scratch],
         compiler_params=VMEM,
-    )(got, resident_now, count, columns, send_at)
+    )(got, resident_now, share, columns, send_at)
 
     cost = pl.CostEstimate(flops=60 * owned * cells, bytes_accessed=48 * owned * cells, transcendentals=0)
     for sweep in range(ITERS):
-        coded = sweep > 0
         here = lax.all_to_all(outbox, "dom", split_axis=0, concat_axis=0, tiled=True)
         down = lax.slice_in_dim(here, 0, ROWS // 2, axis=1)
         up = lax.slice_in_dim(here, ROWS // 2, ROWS, axis=1)
         from_low = lax.ppermute(up, "slab", [(i, (i + 1) % slabs) for i in range(slabs)])
         from_high = lax.ppermute(down, "slab", [((i + 1) % slabs, i) for i in range(slabs)])
         if sweep == 0:
-            part, faces, *lagging, take_y, take_low, take_high, send_x, send_y, keep, gain, lag = (
+            part, faces, *lagging, take_y, take_low, take_high, send_x, send_y = (
                 pl.pallas_call(
                     first_inner_kernel,
                     out_shape=[grid_shape, jax.ShapeDtypeStruct(faces_shape, f32)]
@@ -603,18 +592,17 @@
                         jax.ShapeDtypeStruct((number * owned, message_rows // share), bf16)
                         for number, share in ((4, 1), (2, 2), (2, 2))
                     ]
-                    + [jax.ShapeDtypeStruct((message_rows, 4 * owned), bf16)] * 2
-                    + [grid_shape] * 3,
+                    + [jax.ShapeDtypeStruct((message_rows, 4 * owned), bf16)] * 2,
                     scratch_shapes=[faces_scratch],
                     compiler_params=VMEM,
                     cost_estimate=cost,
-                )(here, columns, send_at, got, resident_old, count, *state)
+                )(here, columns, send_at, got, resident_old, share, *state)
             )
         if sweep:
-            fields = (here, take_y, columns, *state, *lagging, keep, gain, lag)
+            fields = (here, take_y, columns, *state, *lagging, share)
         if 0 < sweep < ITERS - 1:
             part, faces = pl.pallas_call(
-                functools.partial(inner_kernel, coded, False),
+                functools.partial(inner_kernel, sweep, False),
                 out_shape=[grid_shape, jax.ShapeDtypeStruct(faces_shape, f32)],
                 scratch_shapes=[faces_scratch],
                 compiler_params=VMEM,
@@ -622,11 +610,11 @@
             )(*fields)
         if sweep < ITERS - 1:
             edges, outbox = pl.pallas_call(
-                functools.partial(outer_kernel, coded, False),
+                functools.partial(outer_kernel, sweep, False),
                 out_shape=[ends_shape, jax.ShapeDtypeStruct(message, jnp.int16)],
                 scratch_shapes=[ghost_scratch, ghost_scratch, faces_scratch, faces_scratch],
                 compiler_params=VMEM,
-            )(from_low, from_high, take_low, take_high, gain, part, faces, send_x, send_y)
+            )(from_low, from_high, take_low, take_high, share, part, faces, send_x, send_y)
         else:
             part = pl.pallas_call(
                 last_inner_kernel,
@@ -640,7 +628,7 @@
                 out_shape=grid_shape,
                 scratch_shapes=[ghost_scratch, ghost_scratch, pltpu.VMEM((owned, 2 * FACE), f32)],
                 compiler_params=VMEM,
-            )(from_low, from_high, take_low, take_high, gain, part, place)
+            )(from_low, from_high, take_low, take_high, share, part, place)
         lagging, state = state, (part, edges)
 
 

time: 195 us -> 194 us (level)
  no operation moved by 1% of the time
where the time goes in v4:
time: 194 us
  blocking collectives  78.6 us (41%)
  waiting for transfers between devices  47.2 us (24%)
  starting transfers between devices  37.4 us (19%)
  Pallas kernels  25.7 us (13%)
  other arithmetic  2.62 us (1%)
    all_to_all x4, blocking collectives, on_device(): lax.all_to_all(outbox, 'dom', split_axis=0, concat_axis=0, tiled=True)  78.6 us
    all_to_all x1, waiting for transfers between devices, on_device(): lax.all_to_all(outgoing, 'dom', split_axis=0, concat_axis=0, tiled=True)  45.2 us
    all_to_all x1, starting transfers between devices, on_device(): lax.all_to_all(outgoing, 'dom', split_axis=0, concat_axis=0, tiled=True)  19 us
    ppermute x4, starting transfers between devices, on_device(): lax.ppermute(up, 'slab', [(i, (i + 1) % slabs) for i in range(slabs)])  18.4 us
    pallas_call x2, Pallas kernels, on_device(): pl.pallas_call(functools.partial(inner_kernel, sweep, False), out_shape=[...  6.18 us
    pallas_call x1, Pallas kernels, on_device(): pl.pallas_call(first_inner_kernel, out_shape=[grid_shape, jax.ShapeDtypeS...  4.3 us
  transfers between devices with their start and end apart: 9, of which 4 were waited for; matrix products, arithmetic and copies ran while one was open for 2% of the time, Pallas kernels for 8%

profile of v4, /device:TPU:1, one launch (start us, length us, event | category | flops | bytes accessed | tf_op | source)
XLA Modules:
  0.0 194.1 jit_solution(928587875719654331)
XLA Ops:
  0.0 3.8 %shard_map.109 = bf16[48,2,8192]{2,1,0:T(2,128)(2,1)} custom-call(s32[1,96]{1,0:T(1,128)} %bitcast.120, bf16[96,4096]{1,0:T(8,128)(2,1)} %now_hbm.1, bf16[96,4096]{1,0:T(8,128)(2,1)} %old_hbm.1), custom_call_target="tpu_custom_call" | custom-call | tf_op jit(solution)/shard_map/pallas_call | solution.py:497
  3.9 19.0 %all-to-all-start = ((bf16[48,2,8192]{2,1,0:T(2,128)(2,1)}), bf16[48,2,8192]{2,1,0:T(2,128)(2,1)S(1)}, u32[]{:S(2)}, u32[]{:S(2)}) async-start(bf16[48,2,8192]{2,1,0:T(2,128)(2,1)} %shard_map.109), calls=%async_computation | async-start | bytes 3145728 | tf_op jit(solution)/shard_map/all_to_all | solution.py:508
  22.9 0.6 convert_reduce_fusion.12
  26.3 0.6 gather_fusion
  27.7 2.6 %shard_map.110.share_ref.refs_7_ = f32[56,4096]{1,0:T(8,128)S(1)} custom-call(f32[56,256]{1,0:T(8,128)S(1)} %convert_element_type.135.height_ref, f32[56,15]{1,0:T(8,128)S(1)} %bitcast.112), custom_call_target="tpu_custom_call" | custom-call | tf_op jit(solution)/shard_map/pallas_call | solution.py:555
  30.3 45.2 %all-to-all-done.got_ref = bf16[48,2,8192]{2,1,0:T(2,128)(2,1)S(1)} async-done(((bf16[48,2,8192]{2,1,0:T(2,128)(2,1)}), bf16[48,2,8192]{2,1,0:T(2,128)(2,1)S(1)}, u32[]{:S(2)}, u32[]{:S(2)}) %all-to-all-start) | async-done | bytes 1572896 | tf_op jit(solution)/shard_map/all_to_all | solution.py:508
  75.5 1.4 shard_map.111
  76.9 25.4 %all_to_all.25.here_ref = bf16[48,16,128]{2,1,0:T(8,128)(2,1)S(1)} all-to-all(bf16[48,16,128]{2,1,0:T(8,128)(2,1)S(1)} %get-tuple-element.34), channel_id=1, replica_groups=mesh['slab'=16,'dom'=48] {'dom'}, dimensions={0} | all-to-all | bytes 393216 | tf_op jit(solution)/shard_map/all_to_all | solution.py:580
  102.3 4.3 %collective-permute-start = (bf16[48,4,128]{2,1,0:T(4,128)(2,1)S(1)}, bf16[48,4,128]{2,1,0:T(4,128)(2,1)S(1)}, u32[]{:S(2)}, u32[]{:S(2)}) collective-permute-start(bf16[48,4,128]{2,1,0:T(4,128)(2,1)S(1)} %get-tuple-element.72), channel_id=1, source_target_pairs={{0,48},{48,96},{96,144},{144,192},{192,240},{240,288},{288,336},{3... | collective-permute-start | bytes 147464 | tf_op jit(solution)/shard_map/ppermute | solution.py:583
  106.6 4.3 %shard_map.112 = (f32[56,4096]{1,0:T(8,128)S(1)}, f32[224,128]{1,0:T(8,128)S(1)}, f32[56,4096]{1,0:T(8,128)}, f32[56,512]{1,0:T(8,128)}, bf16[224,384]{1,0:T(8,1...) custom-call(bf16[48,16,128]{2,1,0:T(8,128)(2,1)S(1)} %all_to_all.25., ...), custom_call_target="tpu_custom_call" | custom-call | flops 13762560 | bytes 11010048 | tf_op jit(solution)/shard_map/pallas_call | solution.py:587
  110.9 1.1 shard_map.113
  112.0 17.4 %all_to_all.26.here_ref = s16[48,16,128]{2,1,0:T(8,128)(2,1)S(1)} all-to-all(s16[48,16,128]{2,1,0:T(8,128)(2,1)S(1)} %get-tuple-element.43), channel_id=1, replica_groups=mesh['slab'=16,'dom'=48] {'dom'}, dimensions={0} | all-to-all | bytes 393216 | tf_op jit(solution)/shard_map/all_to_all | solution.py:580
  129.5 4.9 %collective-permute-start.2 = (s16[48,4,128]{2,1,0:T(4,128)(2,1)S(1)}, s16[48,4,128]{2,1,0:T(4,128)(2,1)S(1)}, u32[]{:S(2)}, u32[]{:S(2)}) collective-permute-start(s16[48,4,128]{2,1,0:T(4,128)(2,1)S(1)} %get-tuple-element.70), channel_id=1, source_target_pairs={{0,48},{48,96},{96,144},{144,192},{192,240},{240,288},{288,336},{3... | collective-permute-start | bytes 147464 | tf_op jit(solution)/shard_map/ppermute | solution.py:583
  134.4 3.1 %shard_map.114 = (f32[56,4096]{1,0:T(8,128)S(1)}, f32[224,128]{1,0:T(8,128)S(1)}) custom-call(s16[48,16,128]{2,1,0:T(8,128)(2,1)S(1)} %all_to_all.26.here_ref, bf16[224,384]{1,0:T(8,128)(2,1)S(1)} %get-tuple-element.44.take_ref.refs_1_, f32[56,15]{1,0:T(8,128)S(1)} %bitcast.115, f32[56,4096]{1,0:T(8,128)S(1)} %get-tuple-element.39.part_ref.p_ref.q_ref, ...), custom_call_target="tpu_custom_call" | custom-call | flops 13762560 | bytes 11010048 | tf_op jit(solution)/shard_map/pallas_call | solution.py:604
  138.1 1.1 shard_map.115
  139.2 18.1 %all_to_all.27.here_ref = s16[48,16,128]{2,1,0:T(8,128)(2,1)S(1)} all-to-all(s16[48,16,128]{2,1,0:T(8,128)(2,1)S(1)} %get-tuple-element.48), channel_id=1, replica_groups=mesh['slab'=16,'dom'=48] {'dom'}, dimensions={0} | all-to-all | bytes 393216 | tf_op jit(solution)/shard_map/all_to_all | solution.py:580
  157.4 4.2 %collective-permute-start.4 = (s16[48,4,128]{2,1,0:T(4,128)(2,1)S(1)}, s16[48,4,128]{2,1,0:T(4,128)(2,1)S(1)}, u32[]{:S(2)}, u32[]{:S(2)}) collective-permute-start(s16[48,4,128]{2,1,0:T(4,128)(2,1)S(1)} %get-tuple-element.68), channel_id=1, source_target_pairs={{0,48},{48,96},{96,144},{144,192},{192,240},{240,288},{288,336},{3... | collective-permute-start | bytes 147464 | tf_op jit(solution)/shard_map/ppermute | solution.py:583
  161.6 3.1 %shard_map.116 = (f32[56,4096]{1,0:T(8,128)S(1)}, f32[224,128]{1,0:T(8,128)S(1)}) custom-call(s16[48,16,128]{2,1,0:T(8,128)(2,1)S(1)} %all_to_all.27.here_ref, bf16[224,384]{1,0:T(8,128)(2,1)S(1)} %get-tuple-element.44.take_ref.refs_1_, f32[56,15]{1,0:T(8,128)S(1)} %bitcast.116, f32[56,4096]{1,0:T(8,128)S(1)} %get-tuple-element.46.part_ref.p_ref.refs_5_, ...), custom_call_target="tpu_custom_call" | custom-call | flops 13762560 | bytes 11010048 | tf_op jit(solution)/shard_map/pallas_call | solution.py:604
  165.1 1.1 shard_map.117
  166.2 17.7 %all_to_all.28.refs_0_ = s16[48,16,128]{2,1,0:T(8,128)(2,1)S(1)} all-to-all(s16[48,16,128]{2,1,0:T(8,128)(2,1)S(1)} %get-tuple-element.52), channel_id=1, replica_groups=mesh['slab'=16,'dom'=48] {'dom'}, dimensions={0} | all-to-all | bytes 393216 | tf_op jit(solution)/shard_map/all_to_all | solution.py:580
  183.9 5.0 %collective-permute-start.6 = (s16[48,4,128]{2,1,0:T(4,128)(2,1)S(1)}, s16[48,4,128]{2,1,0:T(4,128)(2,1)S(1)}, u32[]{:S(2)}, u32[]{:S(2)}) collective-permute-start(s16[48,4,128]{2,1,0:T(4,128)(2,1)S(1)} %get-tuple-element.66), channel_id=1, source_target_pairs={{0,48},{48,96},{96,144},{144,192},{192,240},{240,288},{288,336},{3... | collective-permute-start | bytes 147464 | tf_op jit(solution)/shard_map/ppermute | solution.py:583
  188.9 2.4 %shard_map.118.part_ref = f32[56,4096]{1,0:T(8,128)S(1)} custom-call(s16[48,16,128]{2,1,0:T(8,128)(2,1)S(1)} %all_to_all.28.refs_0_, bf16[224,384]{1,0:T(8,128)(2,1)S(1)} %get-tuple-element.44.take_ref.refs_1_, f32[56,15]{1,0:T(8,128)S(1)} %bitcast.117, f32[56,4096]{1,0:T(8,128)S(1)} %get-tuple-element.50.part_ref.refs_3_, ...), custom_call_target="tpu_custom_call" | custom-call | flops 13762560 | bytes 11010048 | tf_op jit(solution)/shard_map/pallas_call | solution.py:619
  191.3 1.1 collective-permute-done.7.high_ref
  192.4 1.7 shard_map.119
  (73 shorter events, 3.9 us)
Async XLA Ops:
  0.0 26.3 %copy-start = (s32[56,256]{1,0:T(8,128)S(1)}, s32[56,256]{1,0:T(8,128)}, u32[]{:S(2)}) copy-start(s32[56,256]{1,0:T(8,128)} %param.17) | copy-start | bytes 172036
  3.8 19.1 %copy-start.3 = (s32[6,56]{1,0:T(8,128)S(1)}, s32[6,56]{1,0:T(8,128)}, u32[]{:S(2)}) copy-start(s32[6,56]{1,0:T(8,128)} %param.20) | copy-start | bytes 4036
  3.8 19.7 %copy-start.4 = (s32[48]{0:T(128)S(1)}, s32[48]{0:T(128)}, u32[]{:S(2)}) copy-start(s32[48]{0:T(128)} %param.16) | copy-start | bytes 580
  3.8 21.0 %copy-start.6 = (f32[8]{0:T(128)S(1)}, f32[8]{0:T(128)}, u32[]{:S(2)}) copy-start(f32[8]{0:T(128)} %param.19) | copy-start | bytes 100
  3.8 21.0 %copy-start.7 = (s32[56]{0:T(128)S(1)}, s32[56]{0:T(128)}, u32[]{:S(2)}) copy-start(s32[56]{0:T(128)} %param.18) | copy-start | bytes 676
  3.8 23.1 %copy-start.5 = (f32[2]{0:T(128)S(1)}, f32[2]{0:T(128)}, u32[]{:S(2)}) copy-start(f32[2]{0:T(128)} %constant.53.clone) | copy-start | bytes 28
  3.9 71.6 %all-to-all-start = ((bf16[48,2,8192]{2,1,0:T(2,128)(2,1)}), bf16[48,2,8192]{2,1,0:T(2,128)(2,1)S(1)}, u32[]{:S(2)}, u32[]{:S(2)}) async-start(bf16[48,2,8192]{2,1,0:T(2,128)(2,1)} %shard_map.109), calls=%async_computation | async-start | bytes 3145728 | tf_op jit(solution)/shard_map/all_to_all | solution.py:508
  22.9 52.6 %copy-start.2 = (bf16[8,4096]{1,0:T(8,128)(2,1)S(1)}, bf16[8,4096]{1,0:T(8,128)(2,1)}, u32[]{:S(2)}) copy-start(bf16[8,4096]{1,0:T(8,128)(2,1)} %own_ref.2) | copy-start | bytes 196612
  30.3 76.3 %copy-start.1 = (bf16[8,4096]{1,0:T(8,128)(2,1)S(1)}, bf16[8,4096]{1,0:T(8,128)(2,1)}, u32[]{:S(2)}) copy-start(bf16[8,4096]{1,0:T(8,128)(2,1)} %own_ref.3) | copy-start | bytes 196612
  102.3 8.6 %collective-permute-start = (bf16[48,4,128]{2,1,0:T(4,128)(2,1)S(1)}, bf16[48,4,128]{2,1,0:T(4,128)(2,1)S(1)}, u32[]{:S(2)}, u32[]{:S(2)}) collective-permute-start(bf16[48,4,128]{2,1,0:T(4,128)(2,1)S(1)} %get-tuple-element.72), channel_id=1, source_target_pairs={{0,48},{48,96},{96,144},{144,192},{192,240},{240,288},{288,336},{3... | collective-permute-start | bytes 147464 | tf_op jit(solution)/shard_map/ppermute | solution.py:583
  106.6 4.3 %collective-permute-start.1 = (bf16[48,4,128]{2,1,0:T(4,128)(2,1)S(1)}, bf16[48,4,128]{2,1,0:T(4,128)(2,1)S(1)}, u32[]{:S(2)}, u32[]{:S(2)}) collective-permute-start(bf16[48,4,128]{2,1,0:T(4,128)(2,1)S(1)} %get-tuple-element.71), channel_id=1, source_target_pairs={{48,0},{96,48},{144,96},{192,144},{240,192},{288,240},{336,288},{3... | collective-permute-start | bytes 147464 | tf_op jit(solution)/shard_map/ppermute | solution.py:584
  129.5 8.0 %collective-permute-start.2 = (s16[48,4,128]{2,1,0:T(4,128)(2,1)S(1)}, s16[48,4,128]{2,1,0:T(4,128)(2,1)S(1)}, u32[]{:S(2)}, u32[]{:S(2)}) collective-permute-start(s16[48,4,128]{2,1,0:T(4,128)(2,1)S(1)} %get-tuple-element.70), channel_id=1, source_target_pairs={{0,48},{48,96},{96,144},{144,192},{192,240},{240,288},{288,336},{3... | collective-permute-start | bytes 147464 | tf_op jit(solution)/shard_map/ppermute | solution.py:583
  134.4 3.6 %collective-permute-start.3 = (s16[48,4,128]{2,1,0:T(4,128)(2,1)S(1)}, s16[48,4,128]{2,1,0:T(4,128)(2,1)S(1)}, u32[]{:S(2)}, u32[]{:S(2)}) collective-permute-start(s16[48,4,128]{2,1,0:T(4,128)(2,1)S(1)} %get-tuple-element.69), channel_id=1, source_target_pairs={{48,0},{96,48},{144,96},{192,144},{240,192},{288,240},{336,288},{3... | collective-permute-start | bytes 147464 | tf_op jit(solution)/shard_map/ppermute | solution.py:584
  157.4 7.3 %collective-permute-start.4 = (s16[48,4,128]{2,1,0:T(4,128)(2,1)S(1)}, s16[48,4,128]{2,1,0:T(4,128)(2,1)S(1)}, u32[]{:S(2)}, u32[]{:S(2)}) collective-permute-start(s16[48,4,128]{2,1,0:T(4,128)(2,1)S(1)} %get-tuple-element.68), channel_id=1, source_target_pairs={{0,48},{48,96},{96,144},{144,192},{192,240},{240,288},{288,336},{3... | collective-permute-start | bytes 147464 | tf_op jit(solution)/shard_map/ppermute | solution.py:583
  161.6 3.5 %collective-permute-start.5 = (s16[48,4,128]{2,1,0:T(4,128)(2,1)S(1)}, s16[48,4,128]{2,1,0:T(4,128)(2,1)S(1)}, u32[]{:S(2)}, u32[]{:S(2)}) collective-permute-start(s16[48,4,128]{2,1,0:T(4,128)(2,1)S(1)} %get-tuple-element.67), channel_id=1, source_target_pairs={{48,0},{96,48},{144,96},{192,144},{240,192},{288,240},{336,288},{3... | collective-permute-start | bytes 147464 | tf_op jit(solution)/shard_map/ppermute | solution.py:584
  183.9 7.4 %collective-permute-start.6 = (s16[48,4,128]{2,1,0:T(4,128)(2,1)S(1)}, s16[48,4,128]{2,1,0:T(4,128)(2,1)S(1)}, u32[]{:S(2)}, u32[]{:S(2)}) collective-permute-start(s16[48,4,128]{2,1,0:T(4,128)(2,1)S(1)} %get-tuple-element.66), channel_id=1, source_target_pairs={{0,48},{48,96},{96,144},{144,192},{192,240},{240,288},{288,336},{3... | collective-permute-start | bytes 147464 | tf_op jit(solution)/shard_map/ppermute | solution.py:583
  188.9 3.5 %collective-permute-start.7 = (s16[48,4,128]{2,1,0:T(4,128)(2,1)S(1)}, s16[48,4,128]{2,1,0:T(4,128)(2,1)S(1)}, u32[]{:S(2)}, u32[]{:S(2)}) collective-permute-start(s16[48,4,128]{2,1,0:T(4,128)(2,1)S(1)} %get-tuple-element.65), channel_id=1, source_target_pairs={{48,0},{96,48},{144,96},{192,144},{240,192},{288,240},{336,288},{3... | collective-permute-start | bytes 147464 | tf_op jit(solution)/shard_map/ppermute | solution.py:584

commit v5 on v4

--- a/solution.py
+++ b/solution.py
@@ -17,7 +17,6 @@
 SUB = 8
 DIRS = 4
 ROWS = DIRS * CAP
-CHUNKS = 4
 
 STEP = (2 * CAP, CAP)
 HALF = (CAP, 2 * CAP)
@@ -195,41 +194,42 @@
 
 
 def pack_kernel(
-    incoming, members, dest_hbm, now_hbm, old_hbm, out_ref, dest_ref, held, arrived
+    incoming, members, dest_hbm, now_hbm, old_hbm, out_ref, dest_ref, chosen_ref, held, arrived
 ):
+    level = pl.program_id(0)
     slots = dest_ref.shape[1]
-    cells = now_hbm.shape[1]
-    width = cells // CHUNKS
-    copies = []
-    first = pltpu.make_async_copy(dest_hbm, dest_ref, arrived.at[2 * CHUNKS])
-    first.start()
-    for chunk in range(CHUNKS):
-        for index, ref in ((0, now_hbm), (1, old_hbm)):
-            number = 2 * chunk + index
-            copy = pltpu.make_async_copy(
-                ref.at[:, pl.ds(chunk * width, width)], held.at[number], arrived.at[number]
-            )
+    copies = [
+        pltpu.make_async_copy(now_hbm, held.at[0], arrived.at[0]),
+        pltpu.make_async_copy(old_hbm, held.at[1], arrived.at[1]),
+    ]
+
+    @pl.when(level == 0)
+    def _():
+        first = pltpu.make_async_copy(dest_hbm, dest_ref, arrived.at[2])
+        first.start()
+        for copy in copies:
             copy.start()
-            copies.append(copy)
-    first.wait()
-    dest = dest_ref[...]
-    src = lax.broadcasted_iota(jnp.int32, (slots, slots), 1)
-    other = lax.broadcasted_iota(jnp.int32, (slots, slots), 0)
-    across = jnp.broadcast_to(dest, (slots, slots))
-    down = jnp.sum(jnp.where(src == other, across, 0), axis=1, keepdims=True)
-    receiver = jnp.zeros((1, slots), jnp.int32)
-    for member in range(1, members):
-        receiver = receiver + (dest >= member * incoming).astype(jnp.int32)
-    earlier = (down >= receiver * incoming) & (down < dest)
-    place = jnp.sum(earlier.astype(jnp.int32), axis=0, keepdims=True)
-    spot = jnp.where(dest >= 0, receiver * CAP + place, -1)
-    chosen = jnp.where(other == spot, 1.0, 0.0).astype(jnp.bfloat16)
-    for number, copy in enumerate(copies):
-        copy.wait()
-        rows = jnp.dot(chosen, held[number], preferred_element_type=jnp.float32)
-        out_ref[:, :, number * width : (number + 1) * width] = rows.astype(jnp.bfloat16).reshape(
-            members, CAP, width
-        )
+        first.wait()
+        dest = dest_ref[...]
+        src = lax.broadcasted_iota(jnp.int32, (slots, slots), 1)
+        other = lax.broadcasted_iota(jnp.int32, (slots, slots), 0)
+        across = jnp.broadcast_to(dest, (slots, slots))
+        down = jnp.sum(jnp.where(src == other, across, 0), axis=1, keepdims=True)
+        receiver = jnp.zeros((1, slots), jnp.int32)
+        for member in range(1, members):
+            receiver = receiver + (dest >= member * incoming).astype(jnp.int32)
+        earlier = (down >= receiver * incoming) & (down < dest)
+        place = jnp.sum(earlier.astype(jnp.int32), axis=0, keepdims=True)
+        spot = jnp.where(dest >= 0, receiver * CAP + place, -1)
+        chosen_ref[...] = jnp.where(other == spot, 1.0, 0.0).astype(jnp.bfloat16)
+        copies[0].wait()
+
+    @pl.when(level == 1)
+    def _():
+        copies[1].wait()
+
+    rows = jnp.dot(chosen_ref[...], held[level], preferred_element_type=jnp.float32)
+    out_ref[...] = rows.astype(jnp.bfloat16).reshape(out_ref.shape)
 
 
 def prepare_kernel(height_ref, column_ref, share_ref, mask_ref):
@@ -271,19 +271,12 @@
 def settled(got_ref, own_ref, columns, index, to_ref, ends_ref, share_ref):
     owned, cells = to_ref.shape
     members = got_ref.shape[0]
-    width = cells // CHUNKS
     chosen = one_hot(columns[:, INBOX : INBOX + 1], (owned, members * CAP), 1)
     stay = one_hot(columns[:, ORDER : ORDER + 1], (owned, own_ref.shape[0]), 1)
-    for chunk in range(CHUNKS):
-        at = slice(chunk * width, (chunk + 1) * width)
-        first = (2 * chunk + index) * width
-        rows = jnp.dot(
-            chosen,
-            got_ref[:, :, first : first + width].reshape(members * CAP, width),
-            preferred_element_type=jnp.float32,
-        )
-        rows = rows + jnp.dot(stay, own_ref[:, at], preferred_element_type=jnp.float32)
-        to_ref[:, at] = jnp.where(share_ref[:, at] > 0.0, rows, 0.0)
+    arrived = got_ref[:, :, index * cells : (index + 1) * cells].reshape(members * CAP, cells)
+    rows = jnp.dot(chosen, arrived, preferred_element_type=jnp.float32)
+    rows = rows + jnp.dot(stay, own_ref[...], preferred_element_type=jnp.float32)
+    to_ref[...] = jnp.where(share_ref[...] > 0.0, rows, 0.0)
     ends_ref[:, :FACE] = to_ref[:, :FACE]
     ends_ref[:, FACE:] = to_ref[:, cells - FACE :]
 
@@ -493,15 +486,18 @@
     kept = owned - incoming
     f32, bf16, i32 = jnp.float32, jnp.bfloat16, jnp.int32
 
-    width = cells // CHUNKS
+    slots = source_now.shape[0]
     outgoing = pl.pallas_call(
         functools.partial(pack_kernel, incoming, members),
         out_shape=jax.ShapeDtypeStruct((members, CAP, 2 * cells), bf16),
+        grid=(2,),
         in_specs=[pl.BlockSpec(memory_space=pltpu.HBM)] * 3,
+        out_specs=pl.BlockSpec((members, CAP, cells), lambda level: (0, 0, level)),
         scratch_shapes=[
-            pltpu.VMEM((1, source_now.shape[0]), i32),
-            pltpu.VMEM((2 * CHUNKS, source_now.shape[0], width), bf16),
-            pltpu.SemaphoreType.DMA((2 * CHUNKS + 1,)),
+            pltpu.VMEM((1, slots), i32),
+            pltpu.VMEM((slots, slots), bf16),
+            pltpu.VMEM((2, slots, cells), bf16),
+            pltpu.SemaphoreType.DMA((3,)),
         ],
         compiler_params=pltpu.CompilerParams(vmem_limit_bytes=60 * 1024 * 1024),
     )(destination[None, :], source_now, source_old)

time: 194 us -> 193 us (level)
  no operation moved by 1% of the time
where the time goes in v5:
time: 193 us
  blocking collectives  77.8 us (40%)
  waiting for transfers between devices  47.2 us (24%)
  starting transfers between devices  37.7 us (20%)
  Pallas kernels  24.8 us (13%)
  other arithmetic  2.62 us (1%)
    all_to_all x4, blocking collectives, on_device(): lax.all_to_all(outbox, 'dom', split_axis=0, concat_axis=0, tiled=True)  77.8 us
    all_to_all x1, waiting for transfers between devices, on_device(): lax.all_to_all(outgoing, 'dom', split_axis=0, concat_axis=0, tiled=True)  45.2 us
    all_to_all x1, starting transfers between devices, on_device(): lax.all_to_all(outgoing, 'dom', split_axis=0, concat_axis=0, tiled=True)  19 us
    ppermute x4, starting transfers between devices, on_device(): lax.ppermute(up, 'slab', [(i, (i + 1) % slabs) for i in range(slabs)])  18.7 us
    pallas_call x2, Pallas kernels, on_device(): pl.pallas_call(functools.partial(inner_kernel, sweep, False), out_shape=[...  6.18 us
    pallas_call x1, Pallas kernels, on_device(): pl.pallas_call(first_inner_kernel, out_shape=[grid_shape, jax.ShapeDtypeS...  4.35 us
  transfers between devices with their start and end apart: 9, of which 4 were waited for; matrix products, arithmetic and copies ran while one was open for 2% of the time, Pallas kernels for 8%

profile of v5, /device:TPU:1, one launch (start us, length us, event | category | flops | bytes accessed | tf_op | source)
XLA Modules:
  0.0 192.7 jit_solution(16161559806678571869)
XLA Ops:
  0.0 2.9 %shard_map.109 = bf16[48,2,8192]{2,1,0:T(2,128)(2,1)} custom-call(s32[1,96]{1,0:T(1,128)} %bitcast.120, bf16[96,4096]{1,0:T(8,128)(2,1)} %now_hbm.1, bf16[96,4096]{1,0:T(8,128)(2,1)} %old_hbm.1), custom_call_target="tpu_custom_call" | custom-call | tf_op jit(solution)/shard_map/pallas_call | solution.py:490
  2.9 19.0 %all-to-all-start = ((bf16[48,2,8192]{2,1,0:T(2,128)(2,1)}), bf16[48,2,8192]{2,1,0:T(2,128)(2,1)S(1)}, u32[]{:S(2)}, u32[]{:S(2)}) async-start(bf16[48,2,8192]{2,1,0:T(2,128)(2,1)} %shard_map.109), calls=%async_computation | async-start | bytes 3145728 | tf_op jit(solution)/shard_map/all_to_all | solution.py:504
  22.0 0.6 convert_reduce_fusion.12
  25.4 0.6 gather_fusion
  26.8 2.6 %shard_map.110.share_ref.refs_7_ = f32[56,4096]{1,0:T(8,128)S(1)} custom-call(f32[56,256]{1,0:T(8,128)S(1)} %convert_element_type.135.height_ref, f32[56,15]{1,0:T(8,128)S(1)} %bitcast.112), custom_call_target="tpu_custom_call" | custom-call | tf_op jit(solution)/shard_map/pallas_call | solution.py:551
  29.4 45.2 %all-to-all-done.got_ref = bf16[48,2,8192]{2,1,0:T(2,128)(2,1)S(1)} async-done(((bf16[48,2,8192]{2,1,0:T(2,128)(2,1)}), bf16[48,2,8192]{2,1,0:T(2,128)(2,1)S(1)}, u32[]{:S(2)}, u32[]{:S(2)}) %all-to-all-start) | async-done | bytes 1572896 | tf_op jit(solution)/shard_map/all_to_all | solution.py:504
  74.6 1.4 shard_map.111
  76.0 25.4 %all_to_all.25.here_ref = bf16[48,16,128]{2,1,0:T(8,128)(2,1)S(1)} all-to-all(bf16[48,16,128]{2,1,0:T(8,128)(2,1)S(1)} %get-tuple-element.34), channel_id=1, replica_groups=mesh['slab'=16,'dom'=48] {'dom'}, dimensions={0} | all-to-all | bytes 393216 | tf_op jit(solution)/shard_map/all_to_all | solution.py:576
  101.4 4.3 %collective-permute-start = (bf16[48,4,128]{2,1,0:T(4,128)(2,1)S(1)}, bf16[48,4,128]{2,1,0:T(4,128)(2,1)S(1)}, u32[]{:S(2)}, u32[]{:S(2)}) collective-permute-start(bf16[48,4,128]{2,1,0:T(4,128)(2,1)S(1)} %get-tuple-element.72), channel_id=1, source_target_pairs={{0,48},{48,96},{96,144},{144,192},{192,240},{240,288},{288,336},{3... | collective-permute-start | bytes 147464 | tf_op jit(solution)/shard_map/ppermute | solution.py:579
  105.7 4.3 %shard_map.112 = (f32[56,4096]{1,0:T(8,128)S(1)}, f32[224,128]{1,0:T(8,128)S(1)}, f32[56,4096]{1,0:T(8,128)}, f32[56,512]{1,0:T(8,128)}, bf16[224,384]{1,0:T(8,1...) custom-call(bf16[48,16,128]{2,1,0:T(8,128)(2,1)S(1)} %all_to_all.25., ...), custom_call_target="tpu_custom_call" | custom-call | flops 13762560 | bytes 11010048 | tf_op jit(solution)/shard_map/pallas_call | solution.py:583
  110.1 1.1 shard_map.113
  111.1 17.4 %all_to_all.26.here_ref = s16[48,16,128]{2,1,0:T(8,128)(2,1)S(1)} all-to-all(s16[48,16,128]{2,1,0:T(8,128)(2,1)S(1)} %get-tuple-element.43), channel_id=1, replica_groups=mesh['slab'=16,'dom'=48] {'dom'}, dimensions={0} | all-to-all | bytes 393216 | tf_op jit(solution)/shard_map/all_to_all | solution.py:576
  128.6 4.9 %collective-permute-start.2 = (s16[48,4,128]{2,1,0:T(4,128)(2,1)S(1)}, s16[48,4,128]{2,1,0:T(4,128)(2,1)S(1)}, u32[]{:S(2)}, u32[]{:S(2)}) collective-permute-start(s16[48,4,128]{2,1,0:T(4,128)(2,1)S(1)} %get-tuple-element.70), channel_id=1, source_target_pairs={{0,48},{48,96},{96,144},{144,192},{192,240},{240,288},{288,336},{3... | collective-permute-start | bytes 147464 | tf_op jit(solution)/shard_map/ppermute | solution.py:579
  133.5 3.1 %shard_map.114 = (f32[56,4096]{1,0:T(8,128)S(1)}, f32[224,128]{1,0:T(8,128)S(1)}) custom-call(s16[48,16,128]{2,1,0:T(8,128)(2,1)S(1)} %all_to_all.26.here_ref, bf16[224,384]{1,0:T(8,128)(2,1)S(1)} %get-tuple-element.44.take_ref.refs_1_, f32[56,15]{1,0:T(8,128)S(1)} %bitcast.115, f32[56,4096]{1,0:T(8,128)S(1)} %get-tuple-element.39.part_ref.p_ref.q_ref, ...), custom_call_target="tpu_custom_call" | custom-call | flops 13762560 | bytes 11010048 | tf_op jit(solution)/shard_map/pallas_call | solution.py:600
  137.2 1.1 shard_map.115
  138.3 18.0 %all_to_all.27.here_ref = s16[48,16,128]{2,1,0:T(8,128)(2,1)S(1)} all-to-all(s16[48,16,128]{2,1,0:T(8,128)(2,1)S(1)} %get-tuple-element.48), channel_id=1, replica_groups=mesh['slab'=16,'dom'=48] {'dom'}, dimensions={0} | all-to-all | bytes 393216 | tf_op jit(solution)/shard_map/all_to_all | solution.py:576
  156.4 4.3 %collective-permute-start.4 = (s16[48,4,128]{2,1,0:T(4,128)(2,1)S(1)}, s16[48,4,128]{2,1,0:T(4,128)(2,1)S(1)}, u32[]{:S(2)}, u32[]{:S(2)}) collective-permute-start(s16[48,4,128]{2,1,0:T(4,128)(2,1)S(1)} %get-tuple-element.68), channel_id=1, source_target_pairs={{0,48},{48,96},{96,144},{144,192},{192,240},{240,288},{288,336},{3... | collective-permute-start | bytes 147464 | tf_op jit(solution)/shard_map/ppermute | solution.py:579
  160.7 3.1 %shard_map.116 = (f32[56,4096]{1,0:T(8,128)S(1)}, f32[224,128]{1,0:T(8,128)S(1)}) custom-call(s16[48,16,128]{2,1,0:T(8,128)(2,1)S(1)} %all_to_all.27.here_ref, bf16[224,384]{1,0:T(8,128)(2,1)S(1)} %get-tuple-element.44.take_ref.refs_1_, f32[56,15]{1,0:T(8,128)S(1)} %bitcast.116, f32[56,4096]{1,0:T(8,128)S(1)} %get-tuple-element.46.part_ref.p_ref.refs_5_, ...), custom_call_target="tpu_custom_call" | custom-call | flops 13762560 | bytes 11010048 | tf_op jit(solution)/shard_map/pallas_call | solution.py:600
  164.2 1.1 shard_map.117
  165.3 16.9 %all_to_all.28.refs_0_ = s16[48,16,128]{2,1,0:T(8,128)(2,1)S(1)} all-to-all(s16[48,16,128]{2,1,0:T(8,128)(2,1)S(1)} %get-tuple-element.52), channel_id=1, replica_groups=mesh['slab'=16,'dom'=48] {'dom'}, dimensions={0} | all-to-all | bytes 393216 | tf_op jit(solution)/shard_map/all_to_all | solution.py:576
  182.3 5.2 %collective-permute-start.6 = (s16[48,4,128]{2,1,0:T(4,128)(2,1)S(1)}, s16[48,4,128]{2,1,0:T(4,128)(2,1)S(1)}, u32[]{:S(2)}, u32[]{:S(2)}) collective-permute-start(s16[48,4,128]{2,1,0:T(4,128)(2,1)S(1)} %get-tuple-element.66), channel_id=1, source_target_pairs={{0,48},{48,96},{96,144},{144,192},{192,240},{240,288},{288,336},{3... | collective-permute-start | bytes 147464 | tf_op jit(solution)/shard_map/ppermute | solution.py:579
  187.5 2.4 %shard_map.118.part_ref = f32[56,4096]{1,0:T(8,128)S(1)} custom-call(s16[48,16,128]{2,1,0:T(8,128)(2,1)S(1)} %all_to_all.28.refs_0_, bf16[224,384]{1,0:T(8,128)(2,1)S(1)} %get-tuple-element.44.take_ref.refs_1_, f32[56,15]{1,0:T(8,128)S(1)} %bitcast.117, f32[56,4096]{1,0:T(8,128)S(1)} %get-tuple-element.50.part_ref.refs_3_, ...), custom_call_target="tpu_custom_call" | custom-call | flops 13762560 | bytes 11010048 | tf_op jit(solution)/shard_map/pallas_call | solution.py:615
  189.9 1.1 collective-permute-done.7.high_ref
  191.0 1.7 shard_map.119
  (73 shorter events, 3.9 us)
Async XLA Ops:
  0.0 25.3 %copy-start = (s32[56,256]{1,0:T(8,128)S(1)}, s32[56,256]{1,0:T(8,128)}, u32[]{:S(2)}) copy-start(s32[56,256]{1,0:T(8,128)} %param.17) | copy-start | bytes 172036
  2.9 19.1 %copy-start.3 = (s32[6,56]{1,0:T(8,128)S(1)}, s32[6,56]{1,0:T(8,128)}, u32[]{:S(2)}) copy-start(s32[6,56]{1,0:T(8,128)} %param.20) | copy-start | bytes 4036
  2.9 19.7 %copy-start.4 = (s32[48]{0:T(128)S(1)}, s32[48]{0:T(128)}, u32[]{:S(2)}) copy-start(s32[48]{0:T(128)} %param.16) | copy-start | bytes 580
  2.9 21.0 %copy-start.6 = (f32[8]{0:T(128)S(1)}, f32[8]{0:T(128)}, u32[]{:S(2)}) copy-start(f32[8]{0:T(128)} %param.19) | copy-start | bytes 100
  2.9 21.0 %copy-start.7 = (s32[56]{0:T(128)S(1)}, s32[56]{0:T(128)}, u32[]{:S(2)}) copy-start(s32[56]{0:T(128)} %param.18) | copy-start | bytes 676
  2.9 23.1 %copy-start.5 = (f32[2]{0:T(128)S(1)}, f32[2]{0:T(128)}, u32[]{:S(2)}) copy-start(f32[2]{0:T(128)} %constant.53.clone) | copy-start | bytes 28
  2.9 71.6 %all-to-all-start = ((bf16[48,2,8192]{2,1,0:T(2,128)(2,1)}), bf16[48,2,8192]{2,1,0:T(2,128)(2,1)S(1)}, u32[]{:S(2)}, u32[]{:S(2)}) async-start(bf16[48,2,8192]{2,1,0:T(2,128)(2,1)} %shard_map.109), calls=%async_computation | async-start | bytes 3145728 | tf_op jit(solution)/shard_map/all_to_all | solution.py:504
  21.9 52.6 %copy-start.2 = (bf16[8,4096]{1,0:T(8,128)(2,1)S(1)}, bf16[8,4096]{1,0:T(8,128)(2,1)}, u32[]{:S(2)}) copy-start(bf16[8,4096]{1,0:T(8,128)(2,1)} %own_ref.2) | copy-start | bytes 196612
  29.4 76.3 %copy-start.1 = (bf16[8,4096]{1,0:T(8,128)(2,1)S(1)}, bf16[8,4096]{1,0:T(8,128)(2,1)}, u32[]{:S(2)}) copy-start(bf16[8,4096]{1,0:T(8,128)(2,1)} %own_ref.3) | copy-start | bytes 196612
  101.4 8.7 %collective-permute-start = (bf16[48,4,128]{2,1,0:T(4,128)(2,1)S(1)}, bf16[48,4,128]{2,1,0:T(4,128)(2,1)S(1)}, u32[]{:S(2)}, u32[]{:S(2)}) collective-permute-start(bf16[48,4,128]{2,1,0:T(4,128)(2,1)S(1)} %get-tuple-element.72), channel_id=1, source_target_pairs={{0,48},{48,96},{96,144},{144,192},{192,240},{240,288},{288,336},{3... | collective-permute-start | bytes 147464 | tf_op jit(solution)/shard_map/ppermute | solution.py:579
  105.7 4.4 %collective-permute-start.1 = (bf16[48,4,128]{2,1,0:T(4,128)(2,1)S(1)}, bf16[48,4,128]{2,1,0:T(4,128)(2,1)S(1)}, u32[]{:S(2)}, u32[]{:S(2)}) collective-permute-start(bf16[48,4,128]{2,1,0:T(4,128)(2,1)S(1)} %get-tuple-element.71), channel_id=1, source_target_pairs={{48,0},{96,48},{144,96},{192,144},{240,192},{288,240},{336,288},{3... | collective-permute-start | bytes 147464 | tf_op jit(solution)/shard_map/ppermute | solution.py:580
  128.6 8.0 %collective-permute-start.2 = (s16[48,4,128]{2,1,0:T(4,128)(2,1)S(1)}, s16[48,4,128]{2,1,0:T(4,128)(2,1)S(1)}, u32[]{:S(2)}, u32[]{:S(2)}) collective-permute-start(s16[48,4,128]{2,1,0:T(4,128)(2,1)S(1)} %get-tuple-element.70), channel_id=1, source_target_pairs={{0,48},{48,96},{96,144},{144,192},{192,240},{240,288},{288,336},{3... | collective-permute-start | bytes 147464 | tf_op jit(solution)/shard_map/ppermute | solution.py:579
  133.5 3.7 %collective-permute-start.3 = (s16[48,4,128]{2,1,0:T(4,128)(2,1)S(1)}, s16[48,4,128]{2,1,0:T(4,128)(2,1)S(1)}, u32[]{:S(2)}, u32[]{:S(2)}) collective-permute-start(s16[48,4,128]{2,1,0:T(4,128)(2,1)S(1)} %get-tuple-element.69), channel_id=1, source_target_pairs={{48,0},{96,48},{144,96},{192,144},{240,192},{288,240},{336,288},{3... | collective-permute-start | bytes 147464 | tf_op jit(solution)/shard_map/ppermute | solution.py:580
  156.4 7.4 %collective-permute-start.4 = (s16[48,4,128]{2,1,0:T(4,128)(2,1)S(1)}, s16[48,4,128]{2,1,0:T(4,128)(2,1)S(1)}, u32[]{:S(2)}, u32[]{:S(2)}) collective-permute-start(s16[48,4,128]{2,1,0:T(4,128)(2,1)S(1)} %get-tuple-element.68), channel_id=1, source_target_pairs={{0,48},{48,96},{96,144},{144,192},{192,240},{240,288},{288,336},{3... | collective-permute-start | bytes 147464 | tf_op jit(solution)/shard_map/ppermute | solution.py:579
  160.7 3.5 %collective-permute-start.5 = (s16[48,4,128]{2,1,0:T(4,128)(2,1)S(1)}, s16[48,4,128]{2,1,0:T(4,128)(2,1)S(1)}, u32[]{:S(2)}, u32[]{:S(2)}) collective-permute-start(s16[48,4,128]{2,1,0:T(4,128)(2,1)S(1)} %get-tuple-element.67), channel_id=1, source_target_pairs={{48,0},{96,48},{144,96},{192,144},{240,192},{288,240},{336,288},{3... | collective-permute-start | bytes 147464 | tf_op jit(solution)/shard_map/ppermute | solution.py:580
  182.3 7.6 %collective-permute-start.6 = (s16[48,4,128]{2,1,0:T(4,128)(2,1)S(1)}, s16[48,4,128]{2,1,0:T(4,128)(2,1)S(1)}, u32[]{:S(2)}, u32[]{:S(2)}) collective-permute-start(s16[48,4,128]{2,1,0:T(4,128)(2,1)S(1)} %get-tuple-element.66), channel_id=1, source_target_pairs={{0,48},{48,96},{96,144},{144,192},{192,240},{240,288},{288,336},{3... | collective-permute-start | bytes 147464 | tf_op jit(solution)/shard_map/ppermute | solution.py:579
  187.5 3.5 %collective-permute-start.7 = (s16[48,4,128]{2,1,0:T(4,128)(2,1)S(1)}, s16[48,4,128]{2,1,0:T(4,128)(2,1)S(1)}, u32[]{:S(2)}, u32[]{:S(2)}) collective-permute-start(s16[48,4,128]{2,1,0:T(4,128)(2,1)S(1)} %get-tuple-element.65), channel_id=1, source_target_pairs={{48,0},{96,48},{144,96},{192,144},{240,192},{288,240},{336,288},{3... | collective-permute-start | bytes 147464 | tf_op jit(solution)/shard_map/ppermute | solution.py:580

commit v6 on v5

--- a/solution.py
+++ b/solution.py
@@ -22,7 +22,7 @@
 HALF = (CAP, 2 * CAP)
 PITCH = (ROWS // 2, ROWS)
 
-TAKE, INBOX, ORDER, RATE, WEIGHT, JOINED, NEAR = 0, 4, 5, 6, 7, 8, 9
+TAKE, INBOX, RATE, WEIGHT, JOINED, NEAR = 0, 4, 5, 6, 7, 8
 
 courant_sq = 0.3
 courant = 0.3**0.5
@@ -271,11 +271,10 @@
 def settled(got_ref, own_ref, columns, index, to_ref, ends_ref, share_ref):
     owned, cells = to_ref.shape
     members = got_ref.shape[0]
-    chosen = one_hot(columns[:, INBOX : INBOX + 1], (owned, members * CAP), 1)
-    stay = one_hot(columns[:, ORDER : ORDER + 1], (owned, own_ref.shape[0]), 1)
     arrived = got_ref[:, :, index * cells : (index + 1) * cells].reshape(members * CAP, cells)
-    rows = jnp.dot(chosen, arrived, preferred_element_type=jnp.float32)
-    rows = rows + jnp.dot(stay, own_ref[...], preferred_element_type=jnp.float32)
+    bricks = jnp.concatenate([arrived, own_ref[...]], axis=0)
+    chosen = one_hot(columns[:, INBOX : INBOX + 1], (owned, bricks.shape[0]), 1)
+    rows = jnp.dot(chosen, bricks, preferred_element_type=jnp.float32)
     to_ref[...] = jnp.where(share_ref[...] > 0.0, rows, 0.0)
     ends_ref[:, :FACE] = to_ref[:, :FACE]
     ends_ref[:, FACE:] = to_ref[:, cells - FACE :]
@@ -391,7 +390,13 @@
 
 
 def last_inner_kernel(*refs):
-    inner_kernel(ITERS - 1, True, *refs[:-1], None, refs[-1])
+    *ins, place_ref, middle_ref, ends_ref, part_ref, ghost_ref = refs
+    inner_kernel(ITERS - 1, True, *ins, part_ref, None, ghost_ref)
+    owned, cells = part_ref.shape
+    back = one_hot(place_ref[...], (owned, owned), 1)
+    middle_ref[...] = picked(back, part_ref[:, FACE : cells - FACE])
+    ends_ref[:, :FACE] = part_ref[:, :FACE]
+    ends_ref[:, FACE:] = part_ref[:, cells - FACE :]
 
 
 def outer_kernel(
@@ -423,7 +428,7 @@
     def finish(group):
         rows = at_rows(0, group)
         for x, ghost in ((0, ghost_low), (EDGE - 1, ghost_high)):
-            part = pieces(part_ref, rows, x)
+            part = pieces(part_ref, rows, int(x > 0) if last else x)
             share = pieces(share_ref, rows, x)
             done = [
                 part[h] + courant_sq * share[h] * ghost[at_rows(h * owned, group), :] for h in range(2)
@@ -453,15 +458,15 @@
 
 
 def last_outer_kernel(
-    low_ref, high_ref, take_low_ref, take_high_ref, share_ref, part_ref, place_ref, out_ref, a, b, ends
+    low_ref, high_ref, take_low_ref, take_high_ref, share_ref, part_ref, middle_ref, place_ref, out_ref, a, b, ends
 ):
     outer_kernel(
         ITERS - 1, True, low_ref, high_ref, take_low_ref, take_high_ref, share_ref, part_ref,
         None, None, None, ends, None, a, b, None, None,
     )
-    owned, cells = part_ref.shape
+    owned, cells = out_ref.shape
     back = one_hot(place_ref[...], (owned, owned), 1)
-    out_ref[:, FACE : cells - FACE] = picked(back, part_ref[:, FACE : cells - FACE])
+    out_ref[:, FACE : cells - FACE] = middle_ref[...]
     out_ref[:, :FACE] = picked(back, ends[:, :FACE])
     out_ref[:, cells - FACE :] = picked(back, ends[:, FACE:])
 
@@ -522,7 +527,7 @@
     order_is = position[None, :] == slot_ids[:, None]
     order = jnp.sum(jnp.where(order_is, slot_ids[None, :], 0), axis=1)
     seat = rank_within(anchor, jnp.arange(incoming, dtype=i32), anchor >= 0)
-    inbox = jnp.concatenate([jnp.full((kept,), -1, i32), anchor * CAP + seat])
+    inbox = jnp.concatenate([members * CAP + jnp.arange(kept, dtype=i32), anchor * CAP + seat])
     class_ids = jnp.arange(admittance.shape[0], dtype=i32)
     send_at = []
     take_at = []
@@ -536,7 +541,7 @@
     )
     near = [present[d].astype(f32) for d in range(6)]
     table = jnp.stack(
-        [number.astype(f32) for number in send_at + take_at + [inbox, slot_ids]]
+        [number.astype(f32) for number in send_at + take_at + [inbox]]
         + [rates, 2.0 * courant_sq / (courant * rates), near[4] + near[5]]
         + near
     )
@@ -612,19 +617,19 @@
                 compiler_params=VMEM,
             )(from_low, from_high, take_low, take_high, share, part, faces, send_x, send_y)
         else:
-            part = pl.pallas_call(
+            middle, part = pl.pallas_call(
                 last_inner_kernel,
-                out_shape=grid_shape,
-                scratch_shapes=[faces_scratch],
+                out_shape=[jax.ShapeDtypeStruct((owned, cells - 2 * FACE), f32), ends_shape],
+                scratch_shapes=[pltpu.VMEM((owned, cells), f32), faces_scratch],
                 compiler_params=VMEM,
                 cost_estimate=cost,
-            )(*fields)
+            )(*fields, place)
             return pl.pallas_call(
                 last_outer_kernel,
                 out_shape=grid_shape,
                 scratch_shapes=[ghost_scratch, ghost_scratch, pltpu.VMEM((owned, 2 * FACE), f32)],
                 compiler_params=VMEM,
-            )(from_low, from_high, take_low, take_high, share, part, place)
+            )(from_low, from_high, take_low, take_high, share, part, middle, place)
         lagging, state = state, (part, edges)
 
 

time: 193 us -> 193 us (level)
  no operation moved by 1% of the time
where the time goes in v6:
time: 193 us; the launch traced here: 192 us
  blocking collectives  77.8 us (40%)
  waiting for transfers between devices  46.6 us (24%)
  starting transfers between devices  37.7 us (20%)
  Pallas kernels  24.9 us (13%)
  other arithmetic  2.61 us (1%)
    all_to_all x4, blocking collectives, on_device(): lax.all_to_all(outbox, 'dom', split_axis=0, concat_axis=0, tiled=True)  77.8 us
    all_to_all x1, waiting for transfers between devices, on_device(): lax.all_to_all(outgoing, 'dom', split_axis=0, concat_axis=0, tiled=True)  45.2 us
    all_to_all x1, starting transfers between devices, on_device(): lax.all_to_all(outgoing, 'dom', split_axis=0, concat_axis=0, tiled=True)  19 us
    ppermute x4, starting transfers between devices, on_device(): lax.ppermute(up, 'slab', [(i, (i + 1) % slabs) for i in range(slabs)])  18.7 us
    pallas_call x2, Pallas kernels, on_device(): pl.pallas_call(functools.partial(inner_kernel, sweep, False), out_shape=[...  6.18 us
    pallas_call x1, Pallas kernels, on_device(): pl.pallas_call(first_inner_kernel, out_shape=[grid_shape, jax.ShapeDtypeS...  4.25 us
  transfers between devices with their start and end apart: 9, of which 4 were waited for; matrix products, arithmetic and copies ran while one was open for 2% of the time, Pallas kernels for 8%

profile of v6, /device:TPU:1, one launch (start us, length us, event | category | flops | bytes accessed | tf_op | source)
XLA Modules:
  0.0 192.2 jit_solution(3769673306488290750)
XLA Ops:
  0.0 2.9 %shard_map.109 = bf16[48,2,8192]{2,1,0:T(2,128)(2,1)} custom-call(s32[1,96]{1,0:T(1,128)} %bitcast.122, bf16[96,4096]{1,0:T(8,128)(2,1)} %now_hbm.1, bf16[96,4096]{1,0:T(8,128)(2,1)} %old_hbm.1), custom_call_target="tpu_custom_call" | custom-call | tf_op jit(solution)/shard_map/pallas_call | solution.py:495
  2.9 19.0 %all-to-all-start = ((bf16[48,2,8192]{2,1,0:T(2,128)(2,1)}), bf16[48,2,8192]{2,1,0:T(2,128)(2,1)S(1)}, u32[]{:S(2)}, u32[]{:S(2)}) async-start(bf16[48,2,8192]{2,1,0:T(2,128)(2,1)} %shard_map.109), calls=%async_computation | async-start | bytes 3145728 | tf_op jit(solution)/shard_map/all_to_all | solution.py:509
  22.0 0.6 convert_reduce_fusion.12
  25.3 0.6 gather_fusion
  26.8 2.6 %shard_map.110.share_ref.refs_7_ = f32[56,4096]{1,0:T(8,128)S(1)} custom-call(f32[56,256]{1,0:T(8,128)S(1)} %convert_element_type.132.height_ref, f32[56,14]{1,0:T(8,128)S(1)} %bitcast.114), custom_call_target="tpu_custom_call" | custom-call | tf_op jit(solution)/shard_map/pallas_call | solution.py:556
  29.4 45.2 %all-to-all-done.got_ref = bf16[48,2,8192]{2,1,0:T(2,128)(2,1)S(1)} async-done(((bf16[48,2,8192]{2,1,0:T(2,128)(2,1)}), bf16[48,2,8192]{2,1,0:T(2,128)(2,1)S(1)}, u32[]{:S(2)}, u32[]{:S(2)}) %all-to-all-start) | async-done | bytes 1572896 | tf_op jit(solution)/shard_map/all_to_all | solution.py:509
  74.6 1.3 shard_map.111
  75.9 25.4 %all_to_all.25.here_ref = bf16[48,16,128]{2,1,0:T(8,128)(2,1)S(1)} all-to-all(bf16[48,16,128]{2,1,0:T(8,128)(2,1)S(1)} %get-tuple-element.36), channel_id=1, replica_groups=mesh['slab'=16,'dom'=48] {'dom'}, dimensions={0} | all-to-all | bytes 393216 | tf_op jit(solution)/shard_map/all_to_all | solution.py:581
  101.3 4.3 %collective-permute-start = (bf16[48,4,128]{2,1,0:T(4,128)(2,1)S(1)}, bf16[48,4,128]{2,1,0:T(4,128)(2,1)S(1)}, u32[]{:S(2)}, u32[]{:S(2)}) collective-permute-start(bf16[48,4,128]{2,1,0:T(4,128)(2,1)S(1)} %get-tuple-element.76), channel_id=1, source_target_pairs={{0,48},{48,96},{96,144},{144,192},{192,240},{240,288},{288,336},{3... | collective-permute-start | bytes 147464 | tf_op jit(solution)/shard_map/ppermute | solution.py:584
  105.6 4.3 %shard_map.112 = (f32[56,4096]{1,0:T(8,128)S(1)}, f32[224,128]{1,0:T(8,128)S(1)}, f32[56,4096]{1,0:T(8,128)}, f32[56,512]{1,0:T(8,128)}, bf16[224,384]{1,0:T(8,1...) custom-call(bf16[48,16,128]{2,1,0:T(8,128)(2,1)S(1)} %all_to_all.25., ...), custom_call_target="tpu_custom_call" | custom-call | flops 13762560 | bytes 11010048 | tf_op jit(solution)/shard_map/pallas_call | solution.py:588
  109.8 1.1 shard_map.113
  110.9 17.4 %all_to_all.26.here_ref = s16[48,16,128]{2,1,0:T(8,128)(2,1)S(1)} all-to-all(s16[48,16,128]{2,1,0:T(8,128)(2,1)S(1)} %get-tuple-element.45), channel_id=1, replica_groups=mesh['slab'=16,'dom'=48] {'dom'}, dimensions={0} | all-to-all | bytes 393216 | tf_op jit(solution)/shard_map/all_to_all | solution.py:581
  128.4 4.9 %collective-permute-start.2 = (s16[48,4,128]{2,1,0:T(4,128)(2,1)S(1)}, s16[48,4,128]{2,1,0:T(4,128)(2,1)S(1)}, u32[]{:S(2)}, u32[]{:S(2)}) collective-permute-start(s16[48,4,128]{2,1,0:T(4,128)(2,1)S(1)} %get-tuple-element.74), channel_id=1, source_target_pairs={{0,48},{48,96},{96,144},{144,192},{192,240},{240,288},{288,336},{3... | collective-permute-start | bytes 147464 | tf_op jit(solution)/shard_map/ppermute | solution.py:584
  133.3 3.1 %shard_map.114 = (f32[56,4096]{1,0:T(8,128)S(1)}, f32[224,128]{1,0:T(8,128)S(1)}) custom-call(s16[48,16,128]{2,1,0:T(8,128)(2,1)S(1)} %all_to_all.26.here_ref, bf16[224,384]{1,0:T(8,128)(2,1)S(1)} %get-tuple-element.46.take_ref.refs_1_, f32[56,14]{1,0:T(8,128)S(1)} %bitcast.117, f32[56,4096]{1,0:T(8,128)S(1)} %get-tuple-element.41.part_ref.p_ref.q_ref, ...), custom_call_target="tpu_custom_call" | custom-call | flops 13762560 | bytes 11010048 | tf_op jit(solution)/shard_map/pallas_call | solution.py:605
  136.4 0.5 collective-permute-done.3.high_ref
  137.0 1.1 shard_map.115
  138.1 18.1 %all_to_all.27.here_ref = s16[48,16,128]{2,1,0:T(8,128)(2,1)S(1)} all-to-all(s16[48,16,128]{2,1,0:T(8,128)(2,1)S(1)} %get-tuple-element.50), channel_id=1, replica_groups=mesh['slab'=16,'dom'=48] {'dom'}, dimensions={0} | all-to-all | bytes 393216 | tf_op jit(solution)/shard_map/all_to_all | solution.py:581
  156.2 4.3 %collective-permute-start.4 = (s16[48,4,128]{2,1,0:T(4,128)(2,1)S(1)}, s16[48,4,128]{2,1,0:T(4,128)(2,1)S(1)}, u32[]{:S(2)}, u32[]{:S(2)}) collective-permute-start(s16[48,4,128]{2,1,0:T(4,128)(2,1)S(1)} %get-tuple-element.72), channel_id=1, source_target_pairs={{0,48},{48,96},{96,144},{144,192},{192,240},{240,288},{288,336},{3... | collective-permute-start | bytes 147464 | tf_op jit(solution)/shard_map/ppermute | solution.py:584
  160.4 3.1 %shard_map.116 = (f32[56,4096]{1,0:T(8,128)S(1)}, f32[224,128]{1,0:T(8,128)S(1)}) custom-call(s16[48,16,128]{2,1,0:T(8,128)(2,1)S(1)} %all_to_all.27.here_ref, bf16[224,384]{1,0:T(8,128)(2,1)S(1)} %get-tuple-element.46.take_ref.refs_1_, f32[56,14]{1,0:T(8,128)S(1)} %bitcast.118, f32[56,4096]{1,0:T(8,128)S(1)} %get-tuple-element.48.part_ref.p_ref.refs_5_, ...), custom_call_target="tpu_custom_call" | custom-call | flops 13762560 | bytes 11010048 | tf_op jit(solution)/shard_map/pallas_call | solution.py:605
  164.0 1.1 shard_map.117
  165.1 16.9 %all_to_all.28.refs_0_ = s16[48,16,128]{2,1,0:T(8,128)(2,1)S(1)} all-to-all(s16[48,16,128]{2,1,0:T(8,128)(2,1)S(1)} %get-tuple-element.54), channel_id=1, replica_groups=mesh['slab'=16,'dom'=48] {'dom'}, dimensions={0} | all-to-all | bytes 393216 | tf_op jit(solution)/shard_map/all_to_all | solution.py:581
  182.1 5.2 %collective-permute-start.6 = (s16[48,4,128]{2,1,0:T(4,128)(2,1)S(1)}, s16[48,4,128]{2,1,0:T(4,128)(2,1)S(1)}, u32[]{:S(2)}, u32[]{:S(2)}) collective-permute-start(s16[48,4,128]{2,1,0:T(4,128)(2,1)S(1)} %get-tuple-element.70), channel_id=1, source_target_pairs={{0,48},{48,96},{96,144},{144,192},{192,240},{240,288},{288,336},{3... | collective-permute-start | bytes 147464 | tf_op jit(solution)/shard_map/ppermute | solution.py:584
  187.3 3.0 %shard_map.118 = (f32[56,3584]{1,0:T(8,128)S(1)}, f32[56,512]{1,0:T(8,128)S(1)}) custom-call(s16[48,16,128]{2,1,0:T(8,128)(2,1)S(1)} %all_to_all.28.refs_0_, bf16[224,384]{1,0:T(8,128)(2,1)S(1)} %get-tuple-element.46.take_ref.refs_1_, f32[56,14]{1,0:T(8,128)S(1)} %bitcast.119, f32[56,4096]{1,0:T(8,128)S(1)} %get-tuple-element.52.part_ref.refs_3_, ...), custom_call_target="tpu_custom_call" | custom-call | flops 13762560 | bytes 11010048 | tf_op jit(solution)/shard_map/pallas_call | solution.py:620
  190.8 1.4 shard_map.119
  (73 shorter events, 3.9 us)
Async XLA Ops:
  0.0 25.3 %copy-start = (s32[56,256]{1,0:T(8,128)S(1)}, s32[56,256]{1,0:T(8,128)}, u32[]{:S(2)}) copy-start(s32[56,256]{1,0:T(8,128)} %param.17) | copy-start | bytes 172036
  2.9 19.1 %copy-start.3 = (s32[6,56]{1,0:T(8,128)S(1)}, s32[6,56]{1,0:T(8,128)}, u32[]{:S(2)}) copy-start(s32[6,56]{1,0:T(8,128)} %param.20) | copy-start | bytes 4036
  2.9 19.7 %copy-start.4 = (s32[48]{0:T(128)S(1)}, s32[48]{0:T(128)}, u32[]{:S(2)}) copy-start(s32[48]{0:T(128)} %param.16) | copy-start | bytes 580
  2.9 21.0 %copy-start.6 = (f32[8]{0:T(128)S(1)}, f32[8]{0:T(128)}, u32[]{:S(2)}) copy-start(f32[8]{0:T(128)} %param.19) | copy-start | bytes 100
  2.9 21.0 %copy-start.7 = (s32[56]{0:T(128)S(1)}, s32[56]{0:T(128)}, u32[]{:S(2)}) copy-start(s32[56]{0:T(128)} %param.18) | copy-start | bytes 676
  2.9 23.1 %copy-start.5 = (f32[2]{0:T(128)S(1)}, f32[2]{0:T(128)}, u32[]{:S(2)}) copy-start(f32[2]{0:T(128)} %constant.54.clone) | copy-start | bytes 28
  2.9 71.6 %all-to-all-start = ((bf16[48,2,8192]{2,1,0:T(2,128)(2,1)}), bf16[48,2,8192]{2,1,0:T(2,128)(2,1)S(1)}, u32[]{:S(2)}, u32[]{:S(2)}) async-start(bf16[48,2,8192]{2,1,0:T(2,128)(2,1)} %shard_map.109), calls=%async_computation | async-start | bytes 3145728 | tf_op jit(solution)/shard_map/all_to_all | solution.py:509
  21.9 52.6 %copy-start.2 = (bf16[8,4096]{1,0:T(8,128)(2,1)S(1)}, bf16[8,4096]{1,0:T(8,128)(2,1)}, u32[]{:S(2)}) copy-start(bf16[8,4096]{1,0:T(8,128)(2,1)} %own_ref.2) | copy-start | bytes 196612
  29.4 76.2 %copy-start.1 = (bf16[8,4096]{1,0:T(8,128)(2,1)S(1)}, bf16[8,4096]{1,0:T(8,128)(2,1)}, u32[]{:S(2)}) copy-start(bf16[8,4096]{1,0:T(8,128)(2,1)} %own_ref.3) | copy-start | bytes 196612
  101.3 8.6 %collective-permute-start = (bf16[48,4,128]{2,1,0:T(4,128)(2,1)S(1)}, bf16[48,4,128]{2,1,0:T(4,128)(2,1)S(1)}, u32[]{:S(2)}, u32[]{:S(2)}) collective-permute-start(bf16[48,4,128]{2,1,0:T(4,128)(2,1)S(1)} %get-tuple-element.76), channel_id=1, source_target_pairs={{0,48},{48,96},{96,144},{144,192},{192,240},{240,288},{288,336},{3... | collective-permute-start | bytes 147464 | tf_op jit(solution)/shard_map/ppermute | solution.py:584
  105.6 4.3 %collective-permute-start.1 = (bf16[48,4,128]{2,1,0:T(4,128)(2,1)S(1)}, bf16[48,4,128]{2,1,0:T(4,128)(2,1)S(1)}, u32[]{:S(2)}, u32[]{:S(2)}) collective-permute-start(bf16[48,4,128]{2,1,0:T(4,128)(2,1)S(1)} %get-tuple-element.75), channel_id=1, source_target_pairs={{48,0},{96,48},{144,96},{192,144},{240,192},{288,240},{336,288},{3... | collective-permute-start | bytes 147464 | tf_op jit(solution)/shard_map/ppermute | solution.py:585
  128.4 8.0 %collective-permute-start.2 = (s16[48,4,128]{2,1,0:T(4,128)(2,1)S(1)}, s16[48,4,128]{2,1,0:T(4,128)(2,1)S(1)}, u32[]{:S(2)}, u32[]{:S(2)}) collective-permute-start(s16[48,4,128]{2,1,0:T(4,128)(2,1)S(1)} %get-tuple-element.74), channel_id=1, source_target_pairs={{0,48},{48,96},{96,144},{144,192},{192,240},{240,288},{288,336},{3... | collective-permute-start | bytes 147464 | tf_op jit(solution)/shard_map/ppermute | solution.py:584
  133.3 3.7 %collective-permute-start.3 = (s16[48,4,128]{2,1,0:T(4,128)(2,1)S(1)}, s16[48,4,128]{2,1,0:T(4,128)(2,1)S(1)}, u32[]{:S(2)}, u32[]{:S(2)}) collective-permute-start(s16[48,4,128]{2,1,0:T(4,128)(2,1)S(1)} %get-tuple-element.73), channel_id=1, source_target_pairs={{48,0},{96,48},{144,96},{192,144},{240,192},{288,240},{336,288},{3... | collective-permute-start | bytes 147464 | tf_op jit(solution)/shard_map/ppermute | solution.py:585
  156.2 7.4 %collective-permute-start.4 = (s16[48,4,128]{2,1,0:T(4,128)(2,1)S(1)}, s16[48,4,128]{2,1,0:T(4,128)(2,1)S(1)}, u32[]{:S(2)}, u32[]{:S(2)}) collective-permute-start(s16[48,4,128]{2,1,0:T(4,128)(2,1)S(1)} %get-tuple-element.72), channel_id=1, source_target_pairs={{0,48},{48,96},{96,144},{144,192},{192,240},{240,288},{288,336},{3... | collective-permute-start | bytes 147464 | tf_op jit(solution)/shard_map/ppermute | solution.py:584
  160.4 3.5 %collective-permute-start.5 = (s16[48,4,128]{2,1,0:T(4,128)(2,1)S(1)}, s16[48,4,128]{2,1,0:T(4,128)(2,1)S(1)}, u32[]{:S(2)}, u32[]{:S(2)}) collective-permute-start(s16[48,4,128]{2,1,0:T(4,128)(2,1)S(1)} %get-tuple-element.71), channel_id=1, source_target_pairs={{48,0},{96,48},{144,96},{192,144},{240,192},{288,240},{336,288},{3... | collective-permute-start | bytes 147464 | tf_op jit(solution)/shard_map/ppermute | solution.py:585
  182.1 8.2 %collective-permute-start.6 = (s16[48,4,128]{2,1,0:T(4,128)(2,1)S(1)}, s16[48,4,128]{2,1,0:T(4,128)(2,1)S(1)}, u32[]{:S(2)}, u32[]{:S(2)}) collective-permute-start(s16[48,4,128]{2,1,0:T(4,128)(2,1)S(1)} %get-tuple-element.70), channel_id=1, source_target_pairs={{0,48},{48,96},{96,144},{144,192},{192,240},{240,288},{288,336},{3... | collective-permute-start | bytes 147464 | tf_op jit(solution)/shard_map/ppermute | solution.py:584
  187.3 3.5 %collective-permute-start.7 = (s16[48,4,128]{2,1,0:T(4,128)(2,1)S(1)}, s16[48,4,128]{2,1,0:T(4,128)(2,1)S(1)}, u32[]{:S(2)}, u32[]{:S(2)}) collective-permute-start(s16[48,4,128]{2,1,0:T(4,128)(2,1)S(1)} %get-tuple-element.69), channel_id=1, source_target_pairs={{48,0},{96,48},{144,96},{192,144},{240,192},{288,240},{336,288},{3... | collective-permute-start | bytes 147464 | tf_op jit(solution)/shard_map/ppermute | solution.py:585
